TPU v7x, 32 devices: a whole 2x2x4 slice. The times are simulated.
32 devices in a mesh: grp: 2 (over y), qp: 4 (over z), mode: 2 (over x), fc: 2 (over core).
Axes of the slice: x: 2, y: 2, z: 4, core: 2. Of those that a mesh axis runs over, the one named last changes fastest.
Arguments:
- home_vectors: bfloat16 [576, 288], P('grp'), parts along dimension 0, may hold values from -0.375 to 0.375
- home_freqs: bfloat16 [576], P('grp'), parts along dimension 0, may hold values from 0.5 to 4
- grid_vectors: bfloat16 [12, 288, 288], P('qp'), may hold values from -0.375 to 0.375
- partner_frequencies: bfloat16 [12, 288], P('qp'), may hold values from 0.5 to 4
- force_table: bfloat16 [288, 82944], P(None, ('mode', 'fc')), may hold values from -6 to 6
- partner: int32 [24], P(('grp', 'qp')), parts along dimension 0, may hold values from 0 to 11, as said below
- weights: int32 [24], P(('grp', 'qp')), parts along dimension 0, may hold values from 1 to 6
Outputs:
- widths: float32 [576], P(('grp', 'mode', 'fc')), parts along dimension 0
- collision: float32 [288, 24, 288], P(('mode', 'fc'), ('grp', 'qp')), parts along dimension 1
There are 2 independent parts, one for each index of `grp`. A program takes and returns all parts, laid end to end along the dimension named above; an argument that names none is the same for every part. Nothing has to cross between parts.
Inputs may be any that keep to these rules, and one draw needn't show every extreme that they name: partner is a permutation of 0 to 11; the owner of point y is y // 3. The 3 entries on one device of qp have 3 different owners; for one position on the device, the owners over all devices of qp are all different.
All inputs are finite; a program needn't handle non-finite values.
Results may differ from a plain program's by a relative error of at most 0.0012.
Values may be sent and summed in bfloat16 or wider, within the bound.
No kernel may reach another device: no remote copies, remote signals or barrier semaphores. Data moves between devices by JAX's collectives and lax.ppermute only.
A program may use at most 128 MiB of HBM per device.

v0:
```python
import math

import jax
import jax.numpy as jnp
from jax import lax
from jax.sharding import PartitionSpec as P

thermal_reservoir_kelvin = 1.0
smearing = 0.25


def lorentz(delta):
    return smearing / math.pi / (delta * delta + smearing * smearing)


def occupy(phonon_branch_energy):
    return 1.0 / (jnp.exp(phonon_branch_energy / thermal_reservoir_kelvin) - 1.0)


def coupled_contributions(collision_kernel_entries, home, first, second, weight, modes):
    home_b = home[:, None, None]
    first_b = first[None, :, None]
    second_b = second[None, None, :]
    power = collision_kernel_entries * collision_kernel_entries / (home_b * first_b * second_b)
    occ_one = occupy(first_b)
    occ_two = occupy(second_b)
    decay = (1.0 + occ_one + occ_two) * lorentz(home_b - first_b - second_b)
    merge_term = (occ_one - occ_two) * (
        lorentz(home_b + first_b - second_b) - lorentz(home_b - first_b + second_b)
    )
    scale = weight.astype(jnp.float32) / modes
    return (scale * jnp.sum(power * decay, axis=2), scale * jnp.sum(power * merge_term, axis=1))


def local(
    home_vectors, home_freqs, grid_vectors, partner_frequencies, force_table, partner, weights
):
    rows_per_chip_share = partner.shape[0]
    modes = home_vectors.shape[0]
    n_mode = lax.axis_size("mode")
    n_fc = lax.axis_size("fc")
    n_qp = lax.axis_size("qp")
    group = modes // (n_mode * n_fc)
    local_cols = force_table.shape[1]
    total_q = rows_per_chip_share * n_qp
    incomplete_contraction = jnp.dot(
        home_vectors.T, force_table, preferred_element_type=jnp.float32
    ).astype(jnp.bfloat16)
    moved = lax.all_to_all(
        lax.all_to_all(incomplete_contraction, "mode", split_axis=0, concat_axis=1, tiled=True),
        "fc",
        split_axis=0,
        concat_axis=1,
        tiled=True,
    )
    moved = moved.reshape(group, n_fc, n_mode, local_cols)
    projected = jnp.transpose(moved, (0, 2, 1, 3)).reshape(group, modes, modes)
    vec_piece = lax.all_gather(grid_vectors, "qp", axis=0, tiled=True)
    angular_energy_slice = lax.all_gather(partner_frequencies, "qp", axis=0, tiled=True)
    piece_rows = vec_piece.shape[0]
    targets = jnp.arange(piece_rows, dtype=jnp.int32)
    hits = (partner[:, None] == targets[None, :]).astype(jnp.bfloat16)
    vec_sum = jnp.einsum("pr,rjm->pjm", hits, vec_piece, preferred_element_type=jnp.float32)
    freq_sum = jnp.dot(hits, angular_energy_slice, preferred_element_type=jnp.float32)
    partner_eigenvectors = vec_sum.astype(jnp.bfloat16)
    group_index = lax.axis_index(("mode", "fc"))
    resident_rows = lax.dynamic_slice_in_dim(
        home_freqs.astype(jnp.float32), group_index * group, group
    )
    col_ones = []
    col_twos = []
    for which in range(rows_per_chip_share):
        inner = lax.dot_general(
            projected,
            grid_vectors[which],
            (((1,), (0,)), ((), ())),
            preferred_element_type=jnp.float32,
        )
        inner = inner.astype(jnp.bfloat16)
        collision_kernel_entries = lax.dot_general(
            inner,
            partner_eigenvectors[which],
            (((1,), (0,)), ((), ())),
            preferred_element_type=jnp.float32,
        )
        first_column, col_two = coupled_contributions(
            collision_kernel_entries,
            resident_rows,
            partner_frequencies[which].astype(jnp.float32),
            freq_sum[which],
            weights[which],
            modes,
        )
        col_ones.append(first_column)
        col_twos.append(col_two)
    own_cols = jnp.stack(col_ones, axis=1)
    seconds = jnp.stack(col_twos, axis=0)
    placing = (partner[:, None] == jnp.arange(total_q, dtype=jnp.int32)[None, :]).astype(
        jnp.float32
    )
    spread_term = jnp.einsum("pn,plm->lnm", placing, seconds, precision=lax.Precision.HIGHEST)
    landed = lax.psum_scatter(spread_term, "qp", scatter_dimension=1, tiled=True)
    collision = own_cols + landed
    local_total = jnp.sum(own_cols, axis=(1, 2)) + jnp.sum(seconds, axis=(0, 2))
    widths = lax.psum(local_total, "qp") / (total_q * modes)
    return (widths, collision)


def solution(mesh):
    placed = (
        P("grp", None),
        P("grp"),
        P("qp", None, None),
        P("qp", None),
        P(None, ("mode", "fc")),
        P(("grp", "qp")),
        P(("grp", "qp")),
    )
    return jax.shard_map(
        local,
        mesh=mesh,
        in_specs=placed,
        out_specs=(P(("grp", "mode", "fc")), P(("mode", "fc"), ("grp", "qp"), None)),
        check_vma=False,
    )
```

profile of v0, /device:TPU:0, one launch (start us, length us, event | category | flops | bytes accessed | tf_op | source)
XLA Modules:
  0.0 533.3 jit_solution(2063386374988955999)
XLA Ops:
  8.1 12.0 %convolution_convert_fusion = bf16[288,20736]{1,0:T(8,128)(2,1)} fusion(bf16[288,288]{1,0:T(8,128)(2,1)S(1)} %copy-done, bf16[288,20736]{1,0:T(8,128)(2,1)} %param.11), kind=kOutput, calls=%fused_computation.9 | convolution fusion | flops 3445825536 | bytes 24053760 | tf_op jit(solution)/shard_map/dot_general | solution.py:46
  20.1 8.3 %all-to-all-start = ((bf16[2,144,20736]{2,1,0:T(8,128)(2,1)}), bf16[2,144,20736]{2,1,0:T(8,128)(2,1)}, u32[]{:S(2)}, u32[]{:S(2)}) async-start(bf16[2,144,20736]{2,1,0:T(8,128)(2,1)} %bitcast.95), calls=%async_computation | async-start | bytes 23887872 | tf_op jit(solution)/shard_map/all_to_all | solution.py:50
  29.2 14.7 %all-gather = bf16[4,3,288]{2,1,0:T(4,128)(2,1)S(1)} all-gather(bf16[1,3,288]{2,1,0:T(4,128)(2,1)S(1)} %bitcast.98), channel_id=1, replica_groups=mesh['grp'=2,'qp'=4,'mode'=2,'fc'=2] {'qp'}, dimensions={0}, use_global_device_ids=true | all-gather | bytes 8640 | tf_op jit(solution)/shard_map/all_gather | solution.py:59
  50.8 38.6 %all-gather.3.cloned.1.call-done = bf16[12,288,288]{2,1,0:T(8,128)(2,1)} async-done(((bf16[3,288,288]{2,1,0:T(8,128)(2,1)}), bf16[12,288,288]{2,1,0:T(8,128)(2,1)}) %all-gather.3.cloned.1.call-update) | async-done | bytes 1990672 | tf_op jit(solution)/shard_map/all_gather | solution.py:58
  89.4 2.8 fusion.11
  92.1 1.8 fusion.46
  94.0 66.3 %all-to-all-done = bf16[2,144,20736]{2,1,0:T(8,128)(2,1)} async-done(((bf16[2,144,20736]{2,1,0:T(8,128)(2,1)}), bf16[2,144,20736]{2,1,0:T(8,128)(2,1)}, u32[]{:S(2)}, u32[]{:S(2)}) %all-to-all-start) | async-done | bytes 11943968 | tf_op jit(solution)/shard_map/all_to_all | solution.py:50
  160.3 42.9 %copy.19 = bf16[144,2,20736]{2,1,0:T(2,128)(2,1)} copy(bf16[144,2,20736]{2,0,1:T(8,128)(2,1)} %bitcast.2) | data formatting | bytes 23887872 | tf_op jit(solution)/shard_map/all_to_all | solution.py:50
  203.2 17.4 %all_to_all.27 = bf16[2,72,41472]{2,1,0:T(8,128)(2,1)} reshape(bf16[144,2,20736]{2,1,0:T(2,128)(2,1)} %copy.19) | data formatting | bytes 23887872 | tf_op jit(solution)/shard_map/all_to_all | solution.py:49
  220.6 24.3 %all_to_all.32 = bf16[2,72,41472]{2,1,0:T(8,128)(2,1)} all-to-all(bf16[2,72,41472]{2,1,0:T(8,128)(2,1)} %all_to_all.27), channel_id=1, replica_groups=mesh['grp'=2,'qp'=4,'mode'=2,'fc'=2] {'fc'}, dimensions={0} | all-to-all | bytes 23887872 | tf_op jit(solution)/shard_map/all_to_all | solution.py:49
  244.9 15.4 %reshape.620 = bf16[72,2,2,20736]{3,2,0,1:T(2,128)(2,1)} reshape(bf16[72,2,41472]{2,0,1:T(8,128)(2,1)} %bitcast.96) | data formatting | bytes 23887872 | tf_op jit(solution)/shard_map/reshape | solution.py:56
  260.2 18.0 %copy.66 = bf16[72,2,2,20736]{3,1,2,0:T(2,128)(2,1)} copy(bf16[72,2,2,20736]{3,2,0,1:T(2,128)(2,1)} %reshape.620) | data formatting | bytes 23887872 | tf_op jit(solution)/shard_map/reshape | solution.py:56
  278.2 35.6 %reshape.621 = bf16[72,288,288]{2,1,0:T(8,128)(2,1)} reshape(bf16[72,2,2,20736]{3,2,1,0:T(2,128)(2,1)} %bitcast.97) | data formatting | bytes 23887872 | tf_op jit(solution)/shard_map/reshape | solution.py:57
  313.8 17.5 %fusion.clone.4 = bf16[72,288,288]{2,1,0:T(8,128)(2,1)} fusion(bf16[72,288,288]{2,1,0:T(8,128)(2,1)} %reshape.621, bf16[3,288,288]{2,1,0:T(8,128)(2,1)S(1)} %copy-done.2), kind=kOutput, calls=%fused_computation.10.clone.clone.clone.1 | convolution fusion | flops 3445825536 | bytes 24109056 | tf_op jit(solution)/shard_map/dot_general | solution.py:73
  331.4 18.0 %fusion.2.clone.4 = bf16[72,288,288]{2,1,0:T(8,128)(2,1)} fusion(bf16[72,288,288]{2,1,0:T(8,128)(2,1)} %reshape.621, bf16[3,288,288]{2,1,0:T(8,128)(2,1)S(1)} %copy-done.2), kind=kOutput, calls=%fused_computation.12.clone.clone.clone.1 | convolution fusion | flops 3445825536 | bytes 24109056 | tf_op jit(solution)/shard_map/dot_general | solution.py:73
  349.4 17.7 %fusion.1.clone.4 = bf16[72,288,288]{2,1,0:T(8,128)(2,1)} fusion(bf16[72,288,288]{2,1,0:T(8,128)(2,1)} %reshape.621, bf16[3,288,288]{2,1,0:T(8,128)(2,1)S(1)} %copy-done.2), kind=kOutput, calls=%fused_computation.11.clone.clone.clone.1 | convolution fusion | flops 3445825536 | bytes 24109056 | tf_op jit(solution)/shard_map/dot_general | solution.py:73
  367.1 40.0 %multiply_reduce_fusion.3 = (f32[72,288]{1,0:T(8,128)}, f32[72,288]{1,0:T(8,128)S(1)}) fusion(f32[72,288]{1,0:T(8,128)S(1)} %get-tuple-element.57, f32[288,288]{1,0:T(8,128)S(1)} %get-tuple-element.49, f32[288]{0:T(512)S(1)} %get-tuple-element.9, f32[72,288]{1,0:T(8,128)S(1)} %get-tuple-element.58, f32[288,288]{1,0:T(8,128)S(1)} %get-tuple-element.48, ...), kind=kOutput, calls=%fused_computation.3 | convolution fusion | flops 3571195392 | bytes 13189248 | tf_op jit(solution)/shard_map/dot_general | solution.py:80
  408.6 39.7 %multiply_reduce_fusion.4 = (f32[72,288]{1,0:T(8,128)}, f32[72,288]{1,0:T(8,128)S(1)}) fusion(f32[72,288]{1,0:T(8,128)S(1)} %copy-done.15, f32[288,288]{1,0:T(8,128)S(1)} %copy-done.6, f32[288]{0:T(512)S(1)} %copy-done.23, f32[72,288]{1,0:T(8,128)S(1)} %copy-done.14, f32[288,288]{1,0:T(8,128)S(1)} %copy-done.5, f32[72,288]{1,0:T(8,128)S(1)} %copy-done.16, ...), kind=kOutput, calls=%fused_computation.5 | convolution fusion | flops 3571195392 | bytes 13189248 | tf_op jit(solution)/shard_map/dot_general | solution.py:80
  449.9 39.2 %multiply_reduce_fusion.5 = (f32[72,288]{1,0:T(8,128)S(1)}, f32[72,288]{1,0:T(8,128)S(1)}) fusion(f32[72,288]{1,0:T(8,128)S(1)} %copy-done.12, f32[288,288]{1,0:T(8,128)S(1)} %copy-done.4, f32[288]{0:T(512)S(1)} %copy-done.21, f32[72,288]{1,0:T(8,128)S(1)} %copy-done.13, f32[288,288]{1,0:T(8,128)S(1)} %copy-done.3, f32[72,288]{1,0:T(8,128)S(1)} %copy-done.11, ...), kind=kOutput, calls=%fused_computation.7 | convolution fusion | flops 3571195392 | bytes 13189248 | tf_op jit(solution)/shard_map/dot_general | solution.py:80
  489.4 1.1 convolution_bitcast_fusion
  490.6 1.5 copy.30
  492.5 12.3 %psum.7 = f32[72]{0:T(128)S(1)} all-reduce(f32[72]{0:T(128)S(1)} %add_add_fusion), channel_id=1, replica_groups=mesh['grp'=2,'qp'=4,'mode'=2,'fc'=2] {'qp'}, use_global_device_ids=true, to_apply=%region_12.13 | all-reduce | flops 72 | bytes 576 | tf_op jit(solution)/shard_map/psum | solution.py:105
  505.3 19.1 %reduce-scatter.4.cloned.1.call-done = f32[72,3,288]{2,0,1:T(8,128)} async-done(((f32[72,12,288]{2,0,1:T(8,128)}), f32[72,3,288]{2,0,1:T(8,128)}) %reduce-scatter.4.cloned.1.call-update) | async-done | bytes 248848
  524.5 1.7 maximum_add_fusion
  (92 shorter events, 10.5 us)
Async XLA Ops:
  20.1 140.2 %all-to-all-start = ((bf16[2,144,20736]{2,1,0:T(8,128)(2,1)}), bf16[2,144,20736]{2,1,0:T(8,128)(2,1)}, u32[]{:S(2)}, u32[]{:S(2)}) async-start(bf16[2,144,20736]{2,1,0:T(8,128)(2,1)} %bitcast.95), calls=%async_computation | async-start | bytes 23887872 | tf_op jit(solution)/shard_map/all_to_all | solution.py:50
  28.4 61.0 %all-gather.3.cloned.1.call-start = ((), (), s32[]{:S(2)}) async-start(), calls=%async_computation.3 | async-start | bytes 3317760 | tf_op jit(solution)/shard_map/all_gather | solution.py:58
  29.1 495.3 %reduce-scatter.4.cloned.1.call-start = ((), (), s32[]{:S(2)}) async-start(), calls=%async_computation.4 | async-start | bytes 1658880
  367.0 41.4 %copy-start.5 = (f32[288,288]{1,0:T(8,128)S(1)}, f32[288,288]{1,0:T(8,128)}, u32[]{:S(2)}) copy-start(f32[288,288]{1,0:T(8,128)} %get-tuple-element.44) | copy-start | bytes 995332
  367.0 41.4 %copy-start.6 = (f32[288,288]{1,0:T(8,128)S(1)}, f32[288,288]{1,0:T(8,128)}, u32[]{:S(2)}) copy-start(f32[288,288]{1,0:T(8,128)} %get-tuple-element.45) | copy-start | bytes 995332
  367.0 41.4 %copy-start.10 = (bf16[1,288,288]{2,0,1:T(2,128)(2,1)S(1)}, bf16[1,288,288]{2,0,1:T(2,128)(2,1)}, u32[]{:S(2)}) copy-start(bf16[1,288,288]{2,0,1:T(2,128)(2,1)} %get-tuple-element.22) | copy-start | bytes 497668
  367.0 41.4 %copy-start.14 = (f32[72,288]{1,0:T(8,128)S(1)}, f32[72,288]{1,0:T(8,128)}, u32[]{:S(2)}) copy-start(f32[72,288]{1,0:T(8,128)} %get-tuple-element.35) | copy-start | bytes 248836
  367.0 41.4 %copy-start.15 = (f32[72,288]{1,0:T(8,128)S(1)}, f32[72,288]{1,0:T(8,128)}, u32[]{:S(2)}) copy-start(f32[72,288]{1,0:T(8,128)} %get-tuple-element.36) | copy-start | bytes 248836
  367.1 41.4 %copy-start.16 = (f32[72,288]{1,0:T(8,128)S(1)}, f32[72,288]{1,0:T(8,128)}, u32[]{:S(2)}) copy-start(f32[72,288]{1,0:T(8,128)} %get-tuple-element.37) | copy-start | bytes 248836
  367.1 41.4 %copy-start.23 = (f32[288]{0:T(512)S(1)}, f32[288]{0:T(512)}, u32[]{:S(2)}) copy-start(f32[288]{0:T(512)} %copy-done.22) | copy-start | bytes 3460
  367.1 41.4 %copy-start.31 = (bf16[72,288,288]{2,1,0:T(8,128)(2,1)S(1)}, bf16[72,288,288]{2,1,0:T(8,128)(2,1)}, u32[]{:S(2)}) copy-start(bf16[72,288,288]{2,1,0:T(8,128)(2,1)} %fusion.1.clone.4) | copy-start | bytes 35831812
  408.5 41.3 %copy-start.3 = (f32[288,288]{1,0:T(8,128)S(1)}, f32[288,288]{1,0:T(8,128)}, u32[]{:S(2)}) copy-start(f32[288,288]{1,0:T(8,128)} %get-tuple-element.46) | copy-start | bytes 995332
  408.5 41.3 %copy-start.4 = (f32[288,288]{1,0:T(8,128)S(1)}, f32[288,288]{1,0:T(8,128)}, u32[]{:S(2)}) copy-start(f32[288,288]{1,0:T(8,128)} %get-tuple-element.47) | copy-start | bytes 995332
  408.5 41.3 %copy-start.9 = (bf16[1,288,288]{2,0,1:T(2,128)(2,1)S(1)}, bf16[1,288,288]{2,0,1:T(2,128)(2,1)}, u32[]{:S(2)}) copy-start(bf16[1,288,288]{2,0,1:T(2,128)(2,1)} %get-tuple-element.24) | copy-start | bytes 497668
  408.5 41.2 %copy-start.11 = (f32[72,288]{1,0:T(8,128)S(1)}, f32[72,288]{1,0:T(8,128)}, u32[]{:S(2)}) copy-start(f32[72,288]{1,0:T(8,128)} %get-tuple-element.53) | copy-start | bytes 248836
  408.5 41.2 %copy-start.12 = (f32[72,288]{1,0:T(8,128)S(1)}, f32[72,288]{1,0:T(8,128)}, u32[]{:S(2)}) copy-start(f32[72,288]{1,0:T(8,128)} %get-tuple-element.54) | copy-start | bytes 248836
  408.6 41.2 %copy-start.13 = (f32[72,288]{1,0:T(8,128)S(1)}, f32[72,288]{1,0:T(8,128)}, u32[]{:S(2)}) copy-start(f32[72,288]{1,0:T(8,128)} %get-tuple-element.55) | copy-start | bytes 248836
  408.6 41.2 %copy-start.21 = (f32[288]{0:T(512)S(1)}, f32[288]{0:T(512)}, u32[]{:S(2)}) copy-start(f32[288]{0:T(512)} %copy-done.20) | copy-start | bytes 3460
  408.6 41.2 %copy-start.30 = (bf16[72,288,288]{2,1,0:T(8,128)(2,1)S(1)}, bf16[72,288,288]{2,1,0:T(8,128)(2,1)}, u32[]{:S(2)}) copy-start(bf16[72,288,288]{2,1,0:T(8,128)(2,1)} %fusion.2.clone.4) | copy-start | bytes 35831812
  449.9 42.2 %copy-start.17 = (f32[72,288]{1,0:T(8,128)S(1)}, f32[72,288]{1,0:T(8,128)}, u32[]{:S(2)}) copy-start(f32[72,288]{1,0:T(8,128)} %get-tuple-element.6) | copy-start | bytes 248836
  449.9 42.5 %copy-start.18 = (f32[72,288]{1,0:T(8,128)S(1)}, f32[72,288]{1,0:T(8,128)}, u32[]{:S(2)}) copy-start(f32[72,288]{1,0:T(8,128)} %get-tuple-element.2) | copy-start | bytes 248836
  449.9 42.6 %copy-start.27 = (f32[72]{0:T(128)S(1)}, f32[72]{0:T(128)}, u32[]{:S(2)}) copy-start(f32[72]{0:T(128)} %get-tuple-element.18) | copy-start | bytes 868
  449.9 42.6 %copy-start.28 = (f32[72]{0:T(128)S(1)}, f32[72]{0:T(128)}, u32[]{:S(2)}) copy-start(f32[72]{0:T(128)} %get-tuple-element.34) | copy-start | bytes 868
  449.9 76.3 %copy-start.1 = (bf16[288,288]{1,0:T(8,128)(2,1)S(1)}, bf16[288,288]{1,0:T(8,128)(2,1)}, u32[]{:S(2)}) copy-start(bf16[288,288]{1,0:T(8,128)(2,1)} %param.7) | copy-start | bytes 497668
  (11 other events, 242.7 us)
Sparse Core Ops, SparseCore 0:
  30.8 58.5 all-gather.2
  492.2 32.1 reduce-scatter.3
where the time goes:
time: 542 us; the launch traced here: 533 us
  matrix products  188 us (35%)
  local copies, waits for them, and re-layouts  137 us (25%)
  waiting for transfers between devices  125 us (23%)
  blocking collectives  51.3 us (9%)
  between operations  16.7 us (3%)
  starting transfers between devices  8.39 us (2%)
  other arithmetic  7.31 us (1%)
    dot_general x3, matrix products, local(): lax.dot_general(inner, partner_eigenvectors[which], (((1,), (0,)), ((), (...  119 us
    all_to_all x1, waiting for transfers between devices, local(): lax.all_to_all(incomplete_contraction, 'mode', split_axis=0, concat_axis=...  66.3 us
    dot_general x3, matrix products, local(): lax.dot_general(projected, grid_vectors[which], (((1,), (0,)), ((), ())),...  53.2 us
    all_to_all x1, local copies, waits for them, and re-layouts, local(): lax.all_to_all(incomplete_contraction, 'mode', split_axis=0, concat_axis=...  42.9 us
    all_gather x1, waiting for transfers between devices, local(): vec_piece = lax.all_gather(grid_vectors, 'qp', axis=0, tiled=True)  38.6 us
    reshape x1, local copies, waits for them, and re-layouts, local(): projected = jnp.transpose(moved, (0, 2, 1, 3)).reshape(group, modes, modes)  35.6 us
    reshape x2, local copies, waits for them, and re-layouts, local(): moved = moved.reshape(group, n_fc, n_mode, local_cols)  33.3 us
    all_to_all x1, blocking collectives, local(): lax.all_to_all(lax.all_to_all(incomplete_contraction, 'mode', split_axis=...  24.3 us
  transfers between devices with their start and end apart: 3, of which 3 were waited for; matrix products, arithmetic and copies ran while one was open for 2% of the time, Pallas kernels for 0%

commit v1 on v0

v1 whole, which is shorter than its diff:
```python
import functools
import math

import jax
import jax.numpy as jnp
from jax import lax
from jax.experimental import pallas as pl
from jax.experimental.pallas import tpu as pltpu
from jax.sharding import PartitionSpec as P

thermal_reservoir_kelvin = 1.0
smearing = 0.25

MAIN = 256
TILE = 128
F32 = jnp.float32
BF16 = jnp.bfloat16


def ceil_div(a, b):
    return -(-a // b)


def occupy(energy):
    return 1.0 / (jnp.exp(energy / thermal_reservoir_kelvin) - 1.0)


def dot_nn(a, b):
    return lax.dot_general(a, b, (((1,), (0,)), ((), ())), preferred_element_type=F32)


def dot_nt(a, b):
    return lax.dot_general(a, b, (((1,), (1,)), ((), ())), preferred_element_type=F32)


def project_kernel(groups, share, home_ref, force_ref, out_ref, main_ref, rest_ref):
    modes = home_ref.shape[1]
    lines = home_ref.shape[0]
    rest = modes - MAIN
    per_slot = MAIN // rest
    depth = out_ref.shape[2]
    step = pl.program_id(0)
    here = force_ref.shape[1] // modes
    result = dot_nn(home_ref[...], force_ref[...])
    for c in range(here):
        row = pl.multiple_of((step * here + c) * lines, 8)
        piece = result[:, c * modes : (c + 1) * modes]
        main_ref[0, pl.ds(row, lines), :] = piece[:, :TILE]
        main_ref[1, pl.ds(row, lines), :] = piece[:, TILE:MAIN]
        rest_ref[pl.ds(row, lines), :] = jnp.concatenate(
            [piece[:, MAIN:], jnp.zeros((lines, TILE - rest), F32)], axis=1
        )

    @pl.when(step == pl.num_programs(0) - 1)
    def _():
        lane = lax.broadcasted_iota(jnp.int32, (depth, TILE), 1)
        for t in range(groups):
            for r in range(share):
                line = t * share + r
                for h in range(2):
                    out_ref[t, r, :, h * TILE : (h + 1) * TILE] = main_ref[
                        h, pl.ds(line, depth, stride=lines), :
                    ].astype(BF16)
            for g in range(ceil_div(share, per_slot)):
                for h in range(2):
                    packed = jnp.zeros((depth, TILE), F32)
                    for b in range(per_slot // 2):
                        r = g * per_slot + h * (per_slot // 2) + b
                        if r < share:
                            piece = rest_ref[pl.ds(t * share + r, depth, stride=lines), :]
                            if b > 0:
                                piece = pltpu.roll(piece, b * rest, 1)
                            packed = jnp.where(lane // rest == b, piece, packed)
                    out_ref[t, share + g, :, h * TILE : (h + 1) * TILE] = packed.astype(BF16)


def project(home_rows, force_table, groups, share, modes):
    lines = home_rows.shape[0]
    depth = force_table.shape[1] // modes
    rest = modes - MAIN
    slots = share + ceil_div(share, MAIN // rest)
    here = 8 if depth % 8 == 0 else 4
    steps = depth // here
    return pl.pallas_call(
        functools.partial(project_kernel, groups, share),
        grid=(steps,),
        in_specs=[
            pl.BlockSpec((lines, modes), lambda i: (0, 0)),
            pl.BlockSpec((modes, here * modes), lambda i: (0, i)),
        ],
        out_specs=pl.BlockSpec((groups, slots, depth, MAIN), lambda i: (0, 0, 0, 0)),
        out_shape=jax.ShapeDtypeStruct((groups, slots, depth, MAIN), BF16),
        scratch_shapes=[
            pltpu.VMEM((2, depth * lines, TILE), F32),
            pltpu.VMEM((depth * lines, TILE), F32),
        ],
        compiler_params=pltpu.CompilerParams(vmem_limit_bytes=56 << 20),
        name="project",
    )(home_rows, force_table)


def coupling_kernel(
    share,
    partner_ref,
    weight_ref,
    home_ref,
    grid_ref,
    freq_row_ref,
    freq_col_ref,
    home_row_ref,
    moved_ref,
    out_ref,
    turned_ref,
    grid_t_ref,
    grid_rest_ref,
    inner_rest_ref,
    gather_ref,
    table_ref,
    sums_ref,
    pick_ref,
    inner0,
    inner1,
    inner2,
    value0,
    value1,
    value2,
):
    pairs = grid_ref.shape[0]
    modes = grid_ref.shape[2]
    rest = modes - MAIN
    sources, depth = moved_ref.shape[0], moved_ref.shape[2]
    per_slot = MAIN // rest
    rest_lanes = home_row_ref.shape[1]
    inners = (inner0, inner1, inner2)
    values = (value0, value1, value2)
    s2 = smearing * smearing

    eye = (
        lax.broadcasted_iota(jnp.int32, (modes, modes), 0)
        == lax.broadcasted_iota(jnp.int32, (modes, modes), 1)
    ).astype(BF16)

    def turn_grid(x, carry):
        turned = dot_nt(eye, grid_ref[x, :modes, :]).astype(BF16)
        grid_t_ref[x] = turned
        grid_rest_ref[pl.ds(pl.multiple_of(x * rest, rest), rest), :] = turned[MAIN:, :]
        return carry

    lax.fori_loop(0, pairs, turn_grid, 0)
    lane = lax.broadcasted_iota(jnp.int32, (depth, TILE), 1)
    inner_rest_ref[...] = jnp.zeros_like(inner_rest_ref)
    for r in range(share):
        slot, spot = share + r // per_slot, r % per_slot
        half, spot = spot // (per_slot // 2), spot % (per_slot // 2)
        for s in range(sources):
            gather_ref[s * depth : (s + 1) * depth, :MAIN] = moved_ref[s, r].astype(F32)
            tail = moved_ref[s, slot, :, half * TILE : (half + 1) * TILE].astype(F32)
            if spot > 0:
                tail = pltpu.roll(tail, TILE - spot * rest, 1)
            gather_ref[s * depth : (s + 1) * depth, MAIN:] = tail[:, :rest]
        block = gather_ref[...].astype(BF16)
        turned_ref[r] = dot_nt(eye, block).astype(BF16)
        found = dot_nn(grid_rest_ref[...], block).astype(BF16)
        for x in range(pairs):
            inner_rest_ref[x, r * rest : (r + 1) * rest, :] = found[x * rest : (x + 1) * rest, :]

    row_id = lax.broadcasted_iota(jnp.int32, pick_ref.shape, 0)
    col_id = lax.broadcasted_iota(jnp.int32, pick_ref.shape, 1)
    branch = jnp.where(
        row_id < share * TILE, row_id // TILE, (row_id - share * TILE) // rest
    )
    pick_ref[...] = (branch == col_id).astype(BF16)
    out_ref[...] = jnp.zeros_like(out_ref)

    def contract_first(x, r, into):
        into[...] = dot_nn(turned_ref[r], grid_ref[x, :modes, :MAIN]).astype(BF16)

    def contract_second(x, source, into):
        into[...] = dot_nn(grid_t_ref[partner_ref[x]], source[...])

    def weigh(x, r, source):
        w = home_ref[r]
        c1 = w * w - s2
        c2 = (4.0 * s2) * (w * w)
        total = jnp.zeros((8, MAIN), F32)
        rows = 16
        for n in range(0, modes, rows):
            v = source[n : n + rows, :]
            p = v * v
            d = table_ref[0, n : n + rows, :MAIN] - w
            t = (p * table_ref[2, n : n + rows, :MAIN]) * pl.reciprocal(d * d + s2, approx=True)
            total = total + t[:8] + t[8:]
            e = table_ref[1, n : n + rows, :MAIN] - c1
            u = (p * table_ref[3, n : n + rows, :MAIN]) * pl.reciprocal(e * e + c2, approx=True)
            sums_ref[r, n : n + rows, :] = (u[:, :TILE] + u[:, TILE:]).astype(BF16)
        line = jnp.sum(total, axis=0, keepdims=True) * (1.0 / w)
        out_ref[x, pl.ds(r, 1), :MAIN] += line

    def tables(x):
        w1 = freq_row_ref[x]
        spots = lax.broadcasted_iota(jnp.int32, freq_col_ref.shape, 1)
        w2 = jnp.sum(
            jnp.where(spots == partner_ref[x], freq_col_ref[...], 0.0), axis=1, keepdims=True
        )
        o1, o2 = occupy(w1), occupy(w2)
        scale = weight_ref[x] * (smearing / math.pi / modes)
        i1, i2 = scale / w1, 1.0 / w2
        for n in range(0, modes, 48):
            w2n, o2n, i2n = w2[n : n + 48], o2[n : n + 48], i2[n : n + 48]
            a = w1 - w2n
            both = i1 * i2n
            table_ref[0, n : n + 48, :] = w1 + w2n
            table_ref[1, n : n + 48, :] = a * a
            table_ref[2, n : n + 48, :] = (1.0 + o1 + o2n) * both
            table_ref[3, n : n + 48, :] = (4.0 * a) * (o2n - o1) * both

    def finish(x):
        target = partner_ref[x]
        left = grid_t_ref[target]
        for start in range(0, rest_lanes, TILE):
            found = dot_nt(left, inner_rest_ref[x, start : start + TILE, :])
            w = home_row_ref[:, start : start + TILE]
            c1 = w * w - s2
            c2 = (4.0 * s2) * (w * w)
            total = jnp.zeros((8, TILE), F32)
            for n in range(0, modes, 16):
                v = found[n : n + 16]
                p = v * v
                d = table_ref[0, n : n + 16, MAIN:] - w
                t = (p * table_ref[2, n : n + 16, MAIN:]) * pl.reciprocal(
                    d * d + s2, approx=True
                )
                total = total + t[:8] + t[8:]
                e = table_ref[1, n : n + 16, MAIN:] - c1
                u = (p * table_ref[3, n : n + 16, MAIN:]) * pl.reciprocal(
                    e * e + c2, approx=True
                )
                sums_ref[share + start // TILE, n : n + 16, :] = u.astype(BF16)
            line = jnp.sum(total, axis=0, keepdims=True) / w
            for b in range(TILE // rest):
                r = start // rest + b
                if r < share:
                    out_ref[x, r : r + 1, MAIN:] += line[:, b * rest : (b + 1) * rest]
        second = jnp.zeros((modes, TILE), F32)
        for c in range(share + rest_lanes // TILE):
            second += dot_nn(sums_ref[c], pick_ref[c * TILE : (c + 1) * TILE, :])
        out_ref[target, :share, :] += second.T[:share, :]

    unroll = 3
    assert share % unroll == 0
    contract_first(0, 0, inners[0])
    contract_first(0, 1, inners[1])
    contract_second(0, inners[0], values[0])

    def one_pair(x, carry):
        tables(x)

        def some(i, inner_carry):
            for u in range(unroll):
                r = i * unroll + u

                def ahead(by):
                    wraps = (r + by >= share).astype(jnp.int32)
                    return jnp.minimum(x + wraps, pairs - 1), r + by - wraps * share

                x2, r2 = ahead(2)
                contract_first(x2, r2, inners[(u + 2) % 3])
                x1, _ = ahead(1)
                contract_second(x1, inners[(u + 1) % 3], values[(u + 1) % 3])
                weigh(x, r, values[u])
            return inner_carry

        lax.fori_loop(0, share // unroll, some, 0)
        finish(x)
        return carry

    lax.fori_loop(0, pairs, one_pair, 0)

    totals = jnp.zeros(out_ref.shape[1:], F32)
    for y in range(pairs):
        totals = totals + out_ref[y]
    widths = jnp.sum(totals, axis=1, keepdims=True) * (1.0 / (pairs * modes))
    spread = jnp.where(
        lax.broadcasted_iota(jnp.int32, totals.shape, 0)
        == lax.broadcasted_iota(jnp.int32, totals.shape, 1),
        widths,
        0.0,
    )
    out_ref[:, share, :] = jnp.broadcast_to(
        jnp.sum(spread, axis=0, keepdims=True), (pairs, modes)
    )


def coupling(partner, weights, home, grid, freq_rows, freq_cols, home_row, moved, share, modes):
    pairs = grid.shape[0]
    rest = modes - MAIN
    rest_lanes = home_row.shape[1]
    padded = (share // 8 + 1) * 8
    smem = pl.BlockSpec(memory_space=pltpu.SMEM)
    vmem = pl.BlockSpec(memory_space=pltpu.VMEM)
    chunks = share + rest_lanes // TILE
    return pl.pallas_call(
        functools.partial(coupling_kernel, share),
        in_specs=[smem, smem, smem, vmem, vmem, vmem, vmem, vmem],
        out_specs=vmem,
        out_shape=jax.ShapeDtypeStruct((pairs, padded, modes), F32),
        scratch_shapes=[
            pltpu.VMEM((share, modes, modes), BF16),
            pltpu.VMEM((pairs, modes, modes), BF16),
            pltpu.VMEM((pairs * rest, modes), BF16),
            pltpu.VMEM((pairs, rest_lanes, modes), BF16),
            pltpu.VMEM((modes, modes), F32),
            pltpu.VMEM((4, modes, MAIN + TILE), F32),
            pltpu.VMEM((chunks, modes, TILE), BF16),
            pltpu.VMEM((chunks * TILE, TILE), BF16),
            pltpu.VMEM((modes, MAIN), BF16),
            pltpu.VMEM((modes, MAIN), BF16),
            pltpu.VMEM((modes, MAIN), BF16),
            pltpu.VMEM((modes, MAIN), F32),
            pltpu.VMEM((modes, MAIN), F32),
            pltpu.VMEM((modes, MAIN), F32),
        ],
        compiler_params=pltpu.CompilerParams(vmem_limit_bytes=56 << 20),
        name="coupling",
    )(partner, weights, home, grid, freq_rows, freq_cols, home_row, moved)


def local(
    home_vectors, home_freqs, grid_vectors, partner_frequencies, force_table, partner, weights
):
    own_pairs = partner.shape[0]
    modes = home_vectors.shape[0]
    n_mode = lax.axis_size("mode")
    n_fc = lax.axis_size("fc")
    n_qp = lax.axis_size("qp")
    groups = n_mode * n_fc
    group = modes // groups
    pairs = own_pairs * n_qp
    share = ceil_div(group, n_qp)
    rest = modes - MAIN
    here = lax.axis_index("qp")

    extra = jnp.zeros((own_pairs, 16, modes), BF16)
    extra = extra.at[:, 0, :].set(partner_frequencies)
    extra = extra.at[:, 1, 0].set(partner.astype(BF16))
    extra = extra.at[:, 1, 1].set(weights.astype(BF16))
    gathered = lax.all_gather(
        jnp.concatenate([grid_vectors, extra], axis=1), "qp", axis=0, tiled=True
    )

    rows = home_vectors.T.reshape(groups, group, modes)
    rows = jnp.pad(rows, ((0, 0), (0, share * n_qp - group), (0, 0)))
    rows = lax.dynamic_slice_in_dim(rows, here * share, share, axis=1)
    rows = rows.reshape(groups * share, modes)
    sent = project(rows, force_table, groups, share, modes)
    moved = lax.all_to_all(sent, ("mode", "fc"), split_axis=0, concat_axis=0, tiled=True)

    own = lax.axis_index(("mode", "fc"))
    home = home_freqs.astype(F32).reshape(groups, group)
    home = jnp.pad(home, ((0, 0), (0, share * n_qp - group)), constant_values=1.0)
    home = lax.dynamic_slice(home, (own, here * share), (1, share)).reshape(share)
    rest_lanes = ceil_div(share * rest, TILE) * TILE
    home_row = jnp.repeat(home, rest)
    home_row = jnp.pad(home_row, (0, rest_lanes - share * rest), constant_values=1.0)[None]

    freqs = gathered[:, modes, :].astype(F32)
    freq_rows = jnp.concatenate(
        [freqs[:, :MAIN]] + [freqs[:, MAIN:]] * (TILE // rest), axis=1
    )[:, None, :]
    all_partner = gathered[:, modes + 1, 0].astype(jnp.int32)
    all_weights = gathered[:, modes + 1, 1].astype(F32)
    found = coupling(
        all_partner, all_weights, home, gathered, freq_rows, freqs.T, home_row, moved, share, modes
    )

    padded = found.shape[1]
    back = lax.all_to_all(
        found.reshape(n_qp, own_pairs, padded, modes), "qp", split_axis=0, concat_axis=0, tiled=True
    )
    widths = back[:, 0, share, :share].reshape(n_qp * share)[:group]
    collision = jnp.transpose(back[:, :, :share, :], (0, 2, 1, 3))
    collision = collision.reshape(n_qp * share, own_pairs, modes)[:group]
    return (widths, collision)


def solution(mesh):
    placed = (
        P("grp", None),
        P("grp"),
        P("qp", None, None),
        P("qp", None),
        P(None, ("mode", "fc")),
        P(("grp", "qp")),
        P(("grp", "qp")),
    )
    return jax.shard_map(
        local,
        mesh=mesh,
        in_specs=placed,
        out_specs=(P(("grp", "mode", "fc")), P(("mode", "fc"), ("grp", "qp"), None)),
        check_vma=False,
    )
```

time: 542 us -> 205 us (0.38); the launches traced: 533 us -> 204 us
  matrix products: 188 us -> 0 us
  local copies, waits for them, and re-layouts: 137 us -> 18.3 us
  Pallas kernels: 0 us -> 105 us
  waiting for transfers between devices: 125 us -> 39.6 us
  blocking collectives: 51.3 us -> 16.4 us
    dot_general x10 -> x0, matrix products: 188 us -> none  [the longest x3 119 us: local(): lax.dot_general(inner, partner_eigenvectors[which], (((1,), (0,)), ((), (...]
    pallas_call x0 -> x2, Pallas kernels: none -> 105 us  [the longest x1 92.4 us: coupling(): pl.pallas_call(functools.partial(coupling_kernel, share), in_specs=[smem,...]
    reshape x3 -> x5, local copies, waits for them, and re-layouts: 68.9 us -> 1.66 us  [the longest x1 0.77 us: local(): collision = collision.reshape(n_qp * share, own_pairs, modes)[:group]]
    all_to_all x1, waiting for transfers between devices: 66.3 us -> 0.01 us  [local(): lax.all_to_all(sent, ('mode', 'fc'), split_axis=0, concat_axis=0, tiled=T...]
    all_to_all x2 -> x0, local copies, waits for them, and re-layouts: 60.3 us -> none  [the longest x1 42.9 us: local(): lax.all_to_all(incomplete_contraction, 'mode', split_axis=0, concat_axis=...]
    unnamed x3 -> x1, waiting for transfers between devices: 19.8 us -> 0.02 us
    all_gather x1 -> x0, blocking collectives: 14.7 us -> none  [local(): lax.all_gather(partner_frequencies, 'qp', axis=0, tiled=True)]
    psum x1 -> x0, blocking collectives: 12.3 us -> none  [local(): widths = lax.psum(local_total, 'qp') / (total_q * modes)]
  transfers between devices with their start and end apart: 3 -> 2, of which waited for: 3 -> 1; matrix products, arithmetic and copies ran while one was open for 2% -> 8% of each run, Pallas kernels for 0% -> 6%
where the time goes in v1:
time: 205 us; the launch traced here: 204 us
  Pallas kernels  105 us (51%)
  waiting for transfers between devices  39.6 us (19%)
  local copies, waits for them, and re-layouts  18.3 us (9%)
  blocking collectives  16.4 us (8%)
  between operations  14.1 us (7%)
  other arithmetic  6.25 us (3%)
  starting transfers between devices  4.42 us (2%)
    pallas_call x1, Pallas kernels, coupling(): pl.pallas_call(functools.partial(coupling_kernel, share), in_specs=[smem,...  92.4 us
    all_gather x1, waiting for transfers between devices, local(): lax.all_gather(jnp.concatenate([grid_vectors, extra], axis=1), 'qp', axis...  39.6 us
    all_to_all x1, blocking collectives, local(): lax.all_to_all(found.reshape(n_qp, own_pairs, padded, modes), 'qp', split...  16.4 us
    pallas_call x1, Pallas kernels, project(): pl.pallas_call(functools.partial(project_kernel, groups, share), grid=(st...  12.5 us
    unnamed x11, local copies, waits for them, and re-layouts  6.3 us
    all_gather x1, local copies, waits for them, and re-layouts, local(): lax.all_gather(jnp.concatenate([grid_vectors, extra], axis=1), 'qp', axis...  4.54 us
    all_to_all x1, starting transfers between devices, local(): lax.all_to_all(sent, ('mode', 'fc'), split_axis=0, concat_axis=0, tiled=T...  4.38 us
  transfers between devices with their start and end apart: 2, of which 1 were waited for; matrix products, arithmetic and copies ran while one was open for 8% of the time, Pallas kernels for 6%

profile of v1, /device:TPU:0, one launch (start us, length us, event | category | flops | bytes accessed | tf_op | source)
XLA Modules:
  0.0 204.0 jit_solution(2458500817436354409)
XLA Ops:
  7.2 1.5 copy.35
  8.7 0.7 convert_bitcast_fusion.1
  9.5 0.7 convert_bitcast_fusion
  10.2 0.7 scatter.10
  11.1 0.2 copy.36
  11.3 1.0 pad_maximum_fusion
  12.3 0.2 copy.42
  12.6 0.7 reshape.139.home_ref
  13.2 12.5 %project.1 = bf16[4,21,72,256]{3,2,1,0:T(8,128)(2,1)} custom-call(bf16[72,288]{1,0:T(8,128)(2,1)} %reshape.139.home_ref, bf16[288,20736]{1,0:T(8,128)(2,1)} %force_ref.1), custom_call_target="tpu_custom_call" | custom-call | tf_op jit(solution)/shard_map/project/pallas_call | solution.py:84
  25.7 4.4 %all-to-all-start = ((bf16[4,21,72,256]{3,2,1,0:T(8,128)(2,1)}), bf16[4,21,72,256]{3,2,1,0:T(8,128)(2,1)S(1)}, u32[]{:S(2)}, u32[]{:S(2)}) async-start(bf16[4,21,72,256]{3,2,1,0:T(8,128)(2,1)} %project.1), calls=%async_computation | async-start | bytes 6193152 | tf_op jit(solution)/shard_map/all_to_all | solution.py:356
  30.4 0.6 broadcast_in_dim.12.home_row_ref
  31.0 39.6 %all-gather.2.cloned.1.call-done = bf16[12,304,288]{1,2,0:T(8,128)(2,1)} async-done(((bf16[3,304,288]{1,2,0:T(8,128)(2,1)}), bf16[12,304,288]{1,2,0:T(8,128)(2,1)}) %all-gather.2.cloned.1.call-update) | async-done | bytes 2101264 | tf_op jit(solution)/shard_map/all_gather | solution.py:347
  70.5 2.4 %slice.89 = bf16[12,1,288]{1,2,0:T(8,128)(2,1)} slice(bf16[12,304,288]{1,2,0:T(8,128)(2,1)} %all-gather.2.cloned.1.call-done), slice={[0:12], [288:289], [0:288]} | slice | bytes 13824 | tf_op jit(solution)/shard_map/slice | solution.py:366
  72.9 3.0 %copy.45 = bf16[12,1,288]{0,2,1:T(8,128)(2,1)S(1)} copy(bf16[12,1,288]{1,2,0:T(8,128)(2,1)} %slice.89) | data formatting | bytes 13824
  75.9 0.7 fusion
  76.8 0.6 broadcast_in_dim.10.freq_row_ref
  77.5 4.5 %copy.43.grid_ref = bf16[12,304,288]{2,1,0:T(8,128)(2,1)} copy(bf16[12,304,288]{1,2,0:T(8,128)(2,1)} %all-gather.2.cloned.1.call-done) | data formatting | bytes 4202496 | tf_op jit(solution)/shard_map/all_gather | solution.py:347
  82.0 1.6 fusion.2.partner_ref
  83.6 1.5 fusion.1.weight_ref
  85.2 1.7 copy-done
  86.8 92.4 %coupling.1 = f32[12,24,288]{2,1,0:T(8,128)} custom-call(s32[12]{0:T(128)} %fusion.2.partner_ref, f32[12]{0:T(128)} %fusion.1.weight_ref, f32[18]{0:T(128)} %copy-done.2, bf16[12,304,288]{2,1,0:T(8,128)(2,1)} %copy.43.grid_ref, f32[12,1,384]{2,1,0:T(1,128)} %broadcast_in_dim.10.freq_row_ref, f32[288,12]{1,0:T(8,128)} %get-tuple-element.38.freq_col_ref, ...), custom_call_target="tpu_custom_call" | custom-call | tf_op jit(solution)/shard_map/coupling/pallas_call | solution.py:302
  179.3 16.4 %all_to_all.10 = f32[4,3,24,288]{3,2,1,0:T(8,128)S(1)} all-to-all(f32[4,3,24,288]{3,2,1,0:T(8,128)} %bitcast.22), channel_id=1, replica_groups=mesh['grp'=2,'qp'=4,'mode'=2,'fc'=2] {'qp'}, dimensions={0} | all-to-all | bytes 663552 | tf_op jit(solution)/shard_map/all_to_all | solution.py:377
  195.7 0.8 reshape.141
  196.5 0.6 reshape_squeeze.3
  (27 shorter events, 1.1 us)
Async XLA Ops:
  7.2 5.2 %copy-start.1 = (bf16[288,288]{1,0:T(8,128)(2,1)S(1)}, bf16[288,288]{1,0:T(8,128)(2,1)}, u32[]{:S(2)}) copy-start(bf16[288,288]{1,0:T(8,128)(2,1)} %param.13) | copy-start | bytes 497668
  7.2 63.4 %all-gather.2.cloned.1.call-start = ((), (), s32[]{:S(2)}) async-start(), calls=%async_computation.2 | async-start | bytes 3317760 | tf_op jit(solution)/shard_map/all_gather | solution.py:347
  25.7 4.4 %copy-start.3 = (bf16[288]{0:T(512)(128)(2,1)S(1)}, bf16[288]{0:T(512)(128)(2,1)}, u32[]{:S(2)}) copy-start(bf16[288]{0:T(512)(128)(2,1)} %param.14) | copy-start | bytes 1732
  25.7 59.5 %all-to-all-start = ((bf16[4,21,72,256]{3,2,1,0:T(8,128)(2,1)}), bf16[4,21,72,256]{3,2,1,0:T(8,128)(2,1)S(1)}, u32[]{:S(2)}, u32[]{:S(2)}) async-start(bf16[4,21,72,256]{3,2,1,0:T(8,128)(2,1)} %project.1), calls=%async_computation | async-start | bytes 6193152 | tf_op jit(solution)/shard_map/all_to_all | solution.py:356
  30.2 51.8 %copy-start.2 = (f32[18]{0:T(128)}, f32[18]{0:T(128)S(1)}, u32[]{:S(2)}) copy-start(f32[18]{0:T(128)S(1)} %dynamic-slice_bitcast_fusion.home_ref) | copy-start | bytes 220
  85.2 1.7 copy-start
Sparse Core Ops, SparseCore 0:
  12.4 58.0 all-gather.1

commit v2 on v1

v2 whole, which is shorter than its diff:
```python
import functools
import math

import jax
import jax.numpy as jnp
from jax import lax
from jax.experimental import pallas as pl
from jax.experimental.pallas import tpu as pltpu
from jax.sharding import PartitionSpec as P

thermal_reservoir_kelvin = 1.0
smearing = 0.25

MAIN = 256
TILE = 128
F32 = jnp.float32
BF16 = jnp.bfloat16


def ceil_div(a, b):
    return -(-a // b)


def occupy(energy):
    return 1.0 / (jnp.exp(energy / thermal_reservoir_kelvin) - 1.0)


def dot_nn(a, b):
    return lax.dot_general(a, b, (((1,), (0,)), ((), ())), preferred_element_type=F32)


def dot_nt(a, b):
    return lax.dot_general(a, b, (((1,), (1,)), ((), ())), preferred_element_type=F32)


def slots_of(count, modes):
    return count + ceil_div(count, MAIN // (modes - MAIN))


def project_kernel(groups, n_qp, group, chunks, here_ref, home_ref, force_ref, *refs):
    outs = refs[: len(chunks)]
    rows_ref, main_ref, rest_ref = refs[len(chunks) :]
    modes = home_ref.shape[0]
    lines = rows_ref.shape[0]
    share = lines // groups
    rest = modes - MAIN
    per_slot = MAIN // rest
    depth = outs[0].shape[2]
    step = pl.program_id(0)
    here = force_ref.shape[1] // modes

    @pl.when(step == 0)
    def _():
        line = lax.broadcasted_iota(jnp.int32, (lines, modes), 0)
        column = lax.broadcasted_iota(jnp.int32, (lines, modes), 1)
        own = here_ref[0] * share + line % share
        wanted = (line // share) * group + own
        select = jnp.logical_and(column == wanted, own < group).astype(BF16)
        rows_ref[...] = dot_nt(select, home_ref[...]).astype(BF16)

    result = dot_nn(rows_ref[...], force_ref[...])
    for c in range(here):
        row = pl.multiple_of((step * here + c) * lines, 8)
        piece = result[:, c * modes : (c + 1) * modes]
        main_ref[0, pl.ds(row, lines), :] = piece[:, :TILE]
        main_ref[1, pl.ds(row, lines), :] = piece[:, TILE:MAIN]
        rest_ref[pl.ds(row, lines), :] = jnp.concatenate(
            [piece[:, MAIN:], jnp.zeros((lines, TILE - rest), F32)], axis=1
        )

    @pl.when(step == pl.num_programs(0) - 1)
    def _():
        lane = lax.broadcasted_iota(jnp.int32, (depth, TILE), 1)
        for (first, count), out_ref in zip(chunks, outs):
            for t in range(groups):
                base = t * share + first
                for r in range(count):
                    for h in range(2):
                        out_ref[t, r, :, h * TILE : (h + 1) * TILE] = main_ref[
                            h, pl.ds(base + r, depth, stride=lines), :
                        ].astype(BF16)
                for g in range(ceil_div(count, per_slot)):
                    for h in range(2):
                        packed = jnp.zeros((depth, TILE), F32)
                        for b in range(per_slot // 2):
                            r = g * per_slot + h * (per_slot // 2) + b
                            if r < count:
                                piece = rest_ref[pl.ds(base + r, depth, stride=lines), :]
                                if b > 0:
                                    piece = pltpu.roll(piece, b * rest, 1)
                                packed = jnp.where(lane // rest == b, piece, packed)
                        out_ref[t, count + g, :, h * TILE : (h + 1) * TILE] = packed.astype(BF16)


def project(here, home_vectors, force_table, groups, n_qp, group, share, chunks):
    modes = home_vectors.shape[0]
    lines = groups * share
    depth = force_table.shape[1] // modes
    per_step = 8 if depth % 8 == 0 else 4
    steps = depth // per_step
    shapes = [(groups, slots_of(count, modes), depth, MAIN) for _, count in chunks]
    return pl.pallas_call(
        functools.partial(project_kernel, groups, n_qp, group, chunks),
        grid=(steps,),
        in_specs=[
            pl.BlockSpec(memory_space=pltpu.SMEM),
            pl.BlockSpec((modes, modes), lambda i: (0, 0)),
            pl.BlockSpec((modes, per_step * modes), lambda i: (0, i)),
        ],
        out_specs=[pl.BlockSpec(shape, lambda i: (0, 0, 0, 0)) for shape in shapes],
        out_shape=[jax.ShapeDtypeStruct(shape, BF16) for shape in shapes],
        scratch_shapes=[
            pltpu.VMEM((lines, modes), BF16),
            pltpu.VMEM((2, depth * lines, TILE), F32),
            pltpu.VMEM((depth * lines, TILE), F32),
        ],
        compiler_params=pltpu.CompilerParams(vmem_limit_bytes=56 << 20),
        name="project",
    )(here, home_vectors, force_table)


def identity(size):
    return (
        lax.broadcasted_iota(jnp.int32, (size, size), 0)
        == lax.broadcasted_iota(jnp.int32, (size, size), 1)
    ).astype(BF16)


def arrange_kernel(
    pack_ref, partner_ref, weight_ref, grid_ref, grid_t_ref, freq_row_ref, freq_col_ref
):
    owners, parts, each, rows, modes = pack_ref.shape
    half = modes // parts
    rest = modes - MAIN
    eye = identity(modes)
    source = lax.broadcasted_iota(jnp.int32, (modes, MAIN + TILE), 0)
    place = lax.broadcasted_iota(jnp.int32, (modes, MAIN + TILE), 1)
    wanted = jnp.where(place < MAIN, place, MAIN + (place - MAIN) % rest)
    spread = (source == wanted).astype(BF16)
    lane = lax.broadcasted_iota(jnp.int32, freq_col_ref.shape, 1)
    lane16 = lax.broadcasted_iota(jnp.int32, (16, modes), 1)
    line16 = lax.broadcasted_iota(jnp.int32, (16, modes), 0)
    freq_col_ref[...] = jnp.zeros_like(freq_col_ref)

    def one(q, carry):
        for s in range(each):
            x = q * each + s
            for part in range(parts):
                grid_ref[x, part * half : (part + 1) * half, :] = pack_ref[q, part, s, :half, :]
            grid_t_ref[x] = dot_nt(eye, grid_ref[x]).astype(BF16)
            side = pack_ref[q, 0, s, half : half + 16, :]
            freq_row_ref[x] = dot_nn(side, spread)[0:1, :]
            column = dot_nt(eye, side)[:, 0:1]
            freq_col_ref[...] = jnp.where(lane == x, column, freq_col_ref[...])
            wide = side.astype(F32)
            for spot, ref in ((0, partner_ref), (1, weight_ref)):
                found = jnp.sum(
                    jnp.where(jnp.logical_and(line16 == 1, lane16 == spot), wide, 0.0)
                )
                ref[x] = found.astype(ref.dtype)
        return carry

    lax.fori_loop(0, owners, one, 0)


def arrange(pack):
    owners, parts, each, _, modes = pack.shape
    pairs = owners * each
    smem = pl.BlockSpec(memory_space=pltpu.SMEM)
    vmem = pl.BlockSpec(memory_space=pltpu.VMEM)
    return pl.pallas_call(
        arrange_kernel,
        in_specs=[vmem],
        out_specs=[smem, smem, vmem, vmem, vmem, vmem],
        out_shape=[
            jax.ShapeDtypeStruct((pairs,), jnp.int32),
            jax.ShapeDtypeStruct((pairs,), F32),
            jax.ShapeDtypeStruct((pairs, modes, modes), BF16),
            jax.ShapeDtypeStruct((pairs, modes, modes), BF16),
            jax.ShapeDtypeStruct((pairs, 1, MAIN + TILE), F32),
            jax.ShapeDtypeStruct((modes, TILE), F32),
        ],
        compiler_params=pltpu.CompilerParams(vmem_limit_bytes=56 << 20),
        name="arrange",
    )(pack)


def coupling_kernel(
    share,
    block,
    buffers,
    partner_ref,
    weight_ref,
    home_ref,
    grid_ref,
    grid_t_ref,
    freq_row_ref,
    freq_col_ref,
    home_row_ref,
    moved_ref,
    out_ref,
    turned_ref,
    grid_rest_ref,
    inner_rest_ref,
    gather_ref,
    table_ref,
    sums_ref,
    pick_ref,
    *work,
):
    inners, values = work[:buffers], work[buffers:]
    pairs = grid_ref.shape[0]
    modes = grid_ref.shape[2]
    rest = modes - MAIN
    sources, depth = moved_ref.shape[0], moved_ref.shape[2]
    per_slot = MAIN // rest
    rest_lanes = home_row_ref.shape[1]
    s2 = smearing * smearing
    steps = share // block

    for x in range(pairs):
        grid_rest_ref[x * rest : (x + 1) * rest, :] = grid_t_ref[x, MAIN:, :]
    eye = identity(modes)
    inner_rest_ref[...] = jnp.zeros_like(inner_rest_ref)
    for r in range(share):
        slot, spot = share + r // per_slot, r % per_slot
        half, spot = spot // (per_slot // 2), spot % (per_slot // 2)
        for s in range(sources):
            gather_ref[s * depth : (s + 1) * depth, :MAIN] = moved_ref[s, r].astype(F32)
            tail = moved_ref[s, slot, :, half * TILE : (half + 1) * TILE].astype(F32)
            if spot > 0:
                tail = pltpu.roll(tail, TILE - spot * rest, 1)
            gather_ref[s * depth : (s + 1) * depth, MAIN:] = tail[:, :rest]
        whole = gather_ref[...].astype(BF16)
        turned_ref[r * modes : (r + 1) * modes, :] = dot_nt(eye, whole).astype(BF16)
        found = dot_nn(grid_rest_ref[...], whole).astype(BF16)
        for x in range(pairs):
            inner_rest_ref[x, r * rest : (r + 1) * rest, :] = found[x * rest : (x + 1) * rest, :]

    row_id = lax.broadcasted_iota(jnp.int32, pick_ref.shape, 0)
    col_id = lax.broadcasted_iota(jnp.int32, pick_ref.shape, 1)
    branch = jnp.where(
        row_id < share * TILE, row_id // TILE, (row_id - share * TILE) // rest
    )
    pick_ref[...] = (branch == col_id).astype(BF16)
    out_ref[...] = jnp.zeros_like(out_ref)

    def contract_first(x, step, into):
        start = pl.multiple_of(step * (block * modes), 16)
        found = dot_nn(turned_ref[pl.ds(start, block * modes), :], grid_ref[x, :, :MAIN])
        for b in range(block):
            into[:, b * MAIN : (b + 1) * MAIN] = found[b * modes : (b + 1) * modes].astype(BF16)

    def contract_second(x, source, into):
        into[...] = dot_nn(grid_t_ref[partner_ref[x]], source[...])

    def weigh(x, step, source):
        ws = [home_ref[step * block + b] for b in range(block)]
        c1s = [w * w - s2 for w in ws]
        c2s = [(4.0 * s2) * (w * w) for w in ws]
        totals = [jnp.zeros((8, MAIN), F32) for _ in ws]
        for n in range(0, modes, 16):
            t0 = table_ref[0, n : n + 16, :MAIN]
            t1 = table_ref[1, n : n + 16, :MAIN]
            t2 = table_ref[2, n : n + 16, :MAIN]
            t3 = table_ref[3, n : n + 16, :MAIN]
            for b in range(block):
                v = source[n : n + 16, b * MAIN : (b + 1) * MAIN]
                p = v * v
                d = t0 - ws[b]
                t = (p * t2) * pl.reciprocal(d * d + s2, approx=True)
                totals[b] = totals[b] + (t[:8] + t[8:])
                e = t1 - c1s[b]
                u = (p * t3) * pl.reciprocal(e * e + c2s[b], approx=True)
                sums_ref[step * block + b, n : n + 16, :] = (u[:, :TILE] + u[:, TILE:]).astype(BF16)
        for b in range(block):
            line = jnp.sum(totals[b], axis=0, keepdims=True) * (1.0 / ws[b])
            out_ref[x, pl.ds(step * block + b, 1), :MAIN] += line

    def tables(x):
        w1 = freq_row_ref[x]
        spots = lax.broadcasted_iota(jnp.int32, freq_col_ref.shape, 1)
        w2 = jnp.sum(
            jnp.where(spots == partner_ref[x], freq_col_ref[...], 0.0), axis=1, keepdims=True
        )
        o1, o2 = occupy(w1), occupy(w2)
        scale = weight_ref[x] * (smearing / math.pi / modes)
        i1, i2 = scale / w1, 1.0 / w2
        for n in range(0, modes, 48):
            w2n, o2n, i2n = w2[n : n + 48], o2[n : n + 48], i2[n : n + 48]
            a = w1 - w2n
            both = i1 * i2n
            table_ref[0, n : n + 48, :] = w1 + w2n
            table_ref[1, n : n + 48, :] = a * a
            table_ref[2, n : n + 48, :] = (1.0 + o1 + o2n) * both
            table_ref[3, n : n + 48, :] = (4.0 * a) * (o2n - o1) * both

    def finish(x):
        target = partner_ref[x]
        left = grid_t_ref[target]
        for start in range(0, rest_lanes, TILE):
            found = dot_nt(left, inner_rest_ref[x, start : start + TILE, :])
            w = home_row_ref[:, start : start + TILE]
            c1 = w * w - s2
            c2 = (4.0 * s2) * (w * w)
            total = jnp.zeros((8, TILE), F32)
            for n in range(0, modes, 16):
                v = found[n : n + 16]
                p = v * v
                d = table_ref[0, n : n + 16, MAIN:] - w
                t = (p * table_ref[2, n : n + 16, MAIN:]) * pl.reciprocal(
                    d * d + s2, approx=True
                )
                total = total + (t[:8] + t[8:])
                e = table_ref[1, n : n + 16, MAIN:] - c1
                u = (p * table_ref[3, n : n + 16, MAIN:]) * pl.reciprocal(
                    e * e + c2, approx=True
                )
                sums_ref[share + start // TILE, n : n + 16, :] = u.astype(BF16)
            line = jnp.sum(total, axis=0, keepdims=True) / w
            for b in range(TILE // rest):
                r = start // rest + b
                if r < share:
                    out_ref[x, r : r + 1, MAIN:] += line[:, b * rest : (b + 1) * rest]
        second = jnp.zeros((modes, TILE), F32)
        for c in range(share + rest_lanes // TILE):
            second += dot_nn(sums_ref[c], pick_ref[c * TILE : (c + 1) * TILE, :])
        out_ref[target, :share, :] += second.T[:share, :]

    if buffers > 1:
        contract_first(0, 0, inners[0])
        contract_first(0, 1, inners[1])
        contract_second(0, inners[0], values[0])

    def one_pair(x, carry):
        tables(x)

        def some(i, inner_carry):
            for u in range(buffers):
                step = i * buffers + u

                def ahead(by):
                    wraps = (step + by >= steps).astype(jnp.int32)
                    return jnp.minimum(x + wraps, pairs - 1), step + by - wraps * steps

                if buffers > 1:
                    x1, _ = ahead(1)
                    contract_second(x1, inners[(u + 1) % buffers], values[(u + 1) % buffers])
                    x2, step2 = ahead(2)
                    contract_first(x2, step2, inners[(u + 2) % buffers])
                else:
                    contract_first(x, step, inners[0])
                    contract_second(x, inners[0], values[0])
                weigh(x, step, values[u])
            return inner_carry

        lax.fori_loop(0, steps // buffers, some, 0)
        finish(x)
        return carry

    lax.fori_loop(0, pairs, one_pair, 0)

    totals = jnp.zeros(out_ref.shape[1:], F32)
    for y in range(pairs):
        totals = totals + out_ref[y]
    widths = jnp.sum(totals, axis=1, keepdims=True) * (1.0 / (pairs * modes))
    spread = jnp.where(
        lax.broadcasted_iota(jnp.int32, totals.shape, 0)
        == lax.broadcasted_iota(jnp.int32, totals.shape, 1),
        widths,
        0.0,
    )
    out_ref[:, share, :] = jnp.broadcast_to(
        jnp.sum(spread, axis=0, keepdims=True), (pairs, modes)
    )


def coupling(partner, weights, home, grid, grid_t, freq_rows, freq_cols, moved):
    pairs, modes = grid.shape[0], grid.shape[2]
    share = home.shape[0]
    rest = modes - MAIN
    rest_lanes = ceil_div(share * rest, TILE) * TILE
    home_row = jnp.repeat(home, rest)
    home_row = jnp.pad(home_row, (0, rest_lanes - share * rest), constant_values=1.0)[None]
    padded = (share // 8 + 1) * 8
    smem = pl.BlockSpec(memory_space=pltpu.SMEM)
    vmem = pl.BlockSpec(memory_space=pltpu.VMEM)
    tiles = share + rest_lanes // TILE
    block = 3 if share % 3 == 0 else 1
    steps = share // block
    buffers = 2 if steps % 2 == 0 else 3 if steps % 3 == 0 else 1
    return pl.pallas_call(
        functools.partial(coupling_kernel, share, block, buffers),
        in_specs=[smem, smem, smem, vmem, vmem, vmem, vmem, vmem, vmem],
        out_specs=vmem,
        out_shape=jax.ShapeDtypeStruct((pairs, padded, modes), F32),
        scratch_shapes=[
            pltpu.VMEM((share * modes, modes), BF16),
            pltpu.VMEM((pairs * rest, modes), BF16),
            pltpu.VMEM((pairs, rest_lanes, modes), BF16),
            pltpu.VMEM((modes, modes), F32),
            pltpu.VMEM((4, modes, MAIN + TILE), F32),
            pltpu.VMEM((tiles, modes, TILE), BF16),
            pltpu.VMEM((tiles * TILE, TILE), BF16),
        ]
        + [pltpu.VMEM((modes, block * MAIN), BF16)] * buffers
        + [pltpu.VMEM((modes, block * MAIN), F32)] * buffers,
        compiler_params=pltpu.CompilerParams(vmem_limit_bytes=56 << 20),
        cost_estimate=pl.CostEstimate(
            flops=4 * share * pairs * modes**3,
            bytes_accessed=8 * share * modes * modes,
            transcendentals=2 * share * pairs * modes**2,
        ),
        name="coupling",
    )(partner, weights, home, grid, grid_t, freq_rows, freq_cols, home_row, moved)


def local(
    home_vectors, home_freqs, grid_vectors, partner_frequencies, force_table, partner, weights
):
    own_pairs = partner.shape[0]
    modes = home_vectors.shape[0]
    n_mode = lax.axis_size("mode")
    n_fc = lax.axis_size("fc")
    n_qp = lax.axis_size("qp")
    groups = n_mode * n_fc
    group = modes // groups
    pairs = own_pairs * n_qp
    share = ceil_div(group, n_qp)
    here = lax.axis_index("qp")
    if share % 6 == 0 and share > 6:
        chunks = ((0, 6), (6, share - 6))
    else:
        chunks = ((0, share),)

    part_rows = modes // n_fc
    part = lax.dynamic_slice_in_dim(
        grid_vectors, lax.axis_index("fc") * part_rows, part_rows, axis=1
    )
    lane = jnp.arange(modes)[None]
    small = jnp.where(lane == 0, partner[:, None], jnp.where(lane == 1, weights[:, None], 0))
    side = jnp.stack([partner_frequencies, small.astype(BF16)], axis=1)
    side = jnp.pad(side, ((0, 0), (0, 14), (0, 0)))
    pack = lax.all_gather(jnp.concatenate([part, side], axis=1), ("qp", "fc"), axis=0)
    pack = pack.reshape(n_qp, n_fc, own_pairs, part_rows + 16, modes)

    sent = project(
        here.astype(jnp.int32)[None], home_vectors, force_table, groups, n_qp, group, share, chunks
    )
    moved = [
        lax.all_to_all(x, ("mode", "fc"), split_axis=0, concat_axis=0, tiled=True) for x in sent
    ]

    own = lax.axis_index(("mode", "fc"))
    home = home_freqs.astype(F32).reshape(groups, group)
    home = jnp.pad(home, ((0, 0), (0, share * n_qp - group)), constant_values=1.0)
    home = lax.dynamic_slice(home, (own, here * share), (1, share)).reshape(share)

    shared = arrange(pack)
    parts, widths = [], []
    for (first, count), block in zip(chunks, moved):
        found = coupling(
            shared[0], shared[1], home[first : first + count], *shared[2:], block
        )
        back = lax.all_to_all(
            found.reshape(n_qp, own_pairs, found.shape[1], modes),
            "qp",
            split_axis=0,
            concat_axis=0,
            tiled=True,
        )
        widths.append(back[:, 0, count, :count])
        parts.append(back[:, :, :count, :])
    widths = jnp.concatenate(widths, axis=1).reshape(n_qp * share)[:group]
    collision = jnp.transpose(jnp.concatenate(parts, axis=2), (0, 2, 1, 3))
    collision = collision.reshape(n_qp * share, own_pairs, modes)[:group]
    return (widths, collision)


def solution(mesh):
    placed = (
        P("grp", None),
        P("grp"),
        P("qp", None, None),
        P("qp", None),
        P(None, ("mode", "fc")),
        P(("grp", "qp")),
        P(("grp", "qp")),
    )
    return jax.shard_map(
        local,
        mesh=mesh,
        in_specs=placed,
        out_specs=(P(("grp", "mode", "fc")), P(("mode", "fc"), ("grp", "qp"), None)),
        check_vma=False,
    )
```

time: 205 us -> 182 us (0.89)
  waiting for transfers between devices: 39.6 us -> 11.8 us
  local copies, waits for them, and re-layouts: 18.3 us -> 3.18 us
  Pallas kernels: 105 us -> 118 us
  starting transfers between devices: 4.42 us -> 12.3 us
  other arithmetic: 6.25 us -> 2.41 us
  blocking collectives: 16.4 us -> 19.4 us
    all_gather x1, waiting for transfers between devices: 39.6 us -> 2.14 us  [local(): lax.all_gather(jnp.concatenate([part, side], axis=1), ('qp', 'fc'), axis=0)]
    pallas_call x2 -> x4, Pallas kernels: 105 us -> 118 us  [the longest x2 97.8 us: coupling(): pl.pallas_call(functools.partial(coupling_kernel, share, block, buffers),...]
    all_to_all x1 -> x3, waiting for transfers between devices: 0.01 us -> 9.69 us  [the longest x2 9.69 us: local(): lax.all_to_all(found.reshape(n_qp, own_pairs, found.shape[1], modes), 'qp...]
    all_to_all x1 -> x3, starting transfers between devices: 4.38 us -> 12.3 us  [the longest x2 8.68 us: local(): lax.all_to_all(found.reshape(n_qp, own_pairs, found.shape[1], modes), 'qp...]
    unnamed x11, local copies, waits for them, and re-layouts: 6.3 us -> 0.03 us
    all_gather x1 -> x0, local copies, waits for them, and re-layouts: 4.54 us -> none  [local(): lax.all_gather(jnp.concatenate([grid_vectors, extra], axis=1), 'qp', axis...]
    all_to_all x1, blocking collectives: 16.4 us -> 19.4 us  [local(): lax.all_to_all(x, ('mode', 'fc'), split_axis=0, concat_axis=0, tiled=True)]
    slice x4, local copies, waits for them, and re-layouts: 2.5 us -> 0.09 us  [the longest x2 0.08 us: local(): home[first:first + count]]
  transfers between devices with their start and end apart: 2 -> 4, of which waited for: 1 -> 2; matrix products, arithmetic and copies ran while one was open for 8% -> 1% of each run, Pallas kernels for 6% -> 65%
where the time goes in v2:
time: 182 us; the launch traced here: 181 us
  Pallas kernels  118 us (65%)
  blocking collectives  19.4 us (11%)
  between operations  14.2 us (8%)
  starting transfers between devices  12.3 us (7%)
  waiting for transfers between devices  11.8 us (6%)
  local copies, waits for them, and re-layouts  3.18 us (2%)
  other arithmetic  2.41 us (1%)
    pallas_call x2, Pallas kernels, coupling(): pl.pallas_call(functools.partial(coupling_kernel, share, block, buffers),...  97.8 us
    all_to_all x1, blocking collectives, local(): lax.all_to_all(x, ('mode', 'fc'), split_axis=0, concat_axis=0, tiled=True)  19.4 us
    pallas_call x1, Pallas kernels, project(): pl.pallas_call(functools.partial(project_kernel, groups, n_qp, group, chu...  12.7 us
    all_to_all x2, waiting for transfers between devices, local(): lax.all_to_all(found.reshape(n_qp, own_pairs, found.shape[1], modes), 'qp...  9.69 us
    all_to_all x2, starting transfers between devices, local(): lax.all_to_all(found.reshape(n_qp, own_pairs, found.shape[1], modes), 'qp...  8.68 us
    pallas_call x1, Pallas kernels, arrange(): pl.pallas_call(arrange_kernel, in_specs=[vmem], out_specs=[smem, smem, vm...  7.53 us
  transfers between devices with their start and end apart: 4, of which 2 were waited for; matrix products, arithmetic and copies ran while one was open for 1% of the time, Pallas kernels for 65%

profile of v2, /device:TPU:0, one launch (start us, length us, event | category | flops | bytes accessed | tf_op | source)
XLA Modules:
  0.0 181.3 jit_solution(14517422775856558846)
XLA Ops:
  7.2 0.8 select_convert_fusion
  8.0 0.7 pad_maximum_fusion
  8.8 0.8 fusion.1
  9.6 12.7 %project.1 = (bf16[4,7,72,256]{3,2,1,0:T(8,128)(2,1)}, bf16[4,14,72,256]{3,2,1,0:T(8,128)(2,1)}) custom-call(s32[1]{0:T(128)} %bitcast.4.here_ref, bf16[288,288]{1,0:T(8,128)(2,1)} %home_ref.1, bf16[288,20736]{1,0:T(8,128)(2,1)} %force_ref.1), custom_call_target="tpu_custom_call" | custom-call | tf_op jit(solution)/shard_map/project/pallas_call | solution.py:102
  22.3 19.4 %all_to_all.20.moved_ref = bf16[4,7,72,256]{3,2,1,0:T(8,128)(2,1)} all-to-all(bf16[4,7,72,256]{3,2,1,0:T(8,128)(2,1)} %get-tuple-element.16), channel_id=1, replica_groups=mesh['grp'=2,'qp'=4,'mode'=2,'fc'=2] {'mode','fc'}, dimensions={0} | all-to-all | bytes 2064384 | tf_op jit(solution)/shard_map/all_to_all | solution.py:451
  41.7 3.6 %all-to-all-start.2 = ((bf16[4,14,72,256]{3,2,1,0:T(8,128)(2,1)}), bf16[4,14,72,256]{3,2,1,0:T(8,128)(2,1)S(1)}, u32[]{:S(2)}, u32[]{:S(2)}) async-start(bf16[4,14,72,256]{3,2,1,0:T(8,128)(2,1)} %get-tuple-element.17), calls=%async_computation.2 | async-start | bytes 4128768 | tf_op jit(solution)/shard_map/all_to_all | solution.py:451
  45.3 0.1 reshape.133
  45.4 0.1 dynamic_slice.7
  45.5 0.1 broadcast_in_dim.59
  45.6 0.1 reshape.127
  45.6 0.1 slice_bitcast_fusion.home_ref
  45.7 0.1 broadcast_in_dim.62
  45.8 0.7 broadcast_in_dim.63.home_row_ref
  46.5 0.6 pad.9
  47.0 2.1 %all-gather.3.cloned.1.call-done = bf16[24,160,288]{2,1,0:T(8,128)(2,1)} async-done(((bf16[3,160,288]{2,1,0:T(8,128)(2,1)}), bf16[24,160,288]{2,1,0:T(8,128)(2,1)}) %all-gather.3.cloned.1.call-update) | async-done | bytes 2211856 | tf_op jit(solution)/shard_map/all_gather | solution.py:444
  49.2 7.5 %arrange.1 = (s32[12]{0:T(128)}, f32[12]{0:T(128)}, bf16[12,288,288]{2,1,0:T(8,128)(2,1)}, bf16[12,288,288]{2,1,0:T(8,128)(2,1)}, f32[12,1,384]{2,1,0:T(1,128)}, /*index=5*/f32[288,128]{1,0:T(8,128)}) custom-call(bf16[4,2,3,160,288]{4,3,2,1,0:T(8,128)(2,1)} %bitcast.18), custom_call_target="tpu_custom_call" | custom-call | tf_op jit(solution)/shard_map/arrange/pallas_call | solution.py:171
  56.7 36.3 %coupling.2 = f32[12,8,288]{2,1,0:T(8,128)} custom-call(s32[12]{0:T(128)} %get-tuple-element.10.partner_ref, f32[12]{0:T(128)} %get-tuple-element.11.weight_ref, f32[6]{0:T(128)} %copy-done.4, bf16[12,288,288]{2,1,0:T(8,128)(2,1)} %get-tuple-element.12.grid_ref, bf16[12,288,288]{2,1,0:T(8,128)(2,1)} %get-tuple-element.13.grid_t_ref, ...), custom_call_target="tpu_custom_call" | custom-call | flops 6879707136 | bytes 3981312 | tf_op jit(solution)/shard_map/coupling/pallas_call | solution.py:392
  93.0 3.6 %all-to-all-start.1 = ((f32[4,3,8,288]{3,2,1,0:T(8,128)}), f32[4,3,8,288]{3,2,1,0:T(8,128)S(1)}, u32[]{:S(2)}, u32[]{:S(2)}) async-start(f32[4,3,8,288]{3,2,1,0:T(8,128)} %bitcast.22), calls=%async_computation.1 | async-start | bytes 294912 | tf_op jit(solution)/shard_map/all_to_all | solution.py:465
  96.6 61.5 %coupling.3 = f32[12,16,288]{2,1,0:T(8,128)} custom-call(s32[12]{0:T(128)} %get-tuple-element.10.partner_ref, f32[12]{0:T(128)} %get-tuple-element.11.weight_ref, f32[12]{0:T(128)} %copy-done.3, bf16[12,288,288]{2,1,0:T(8,128)(2,1)} %get-tuple-element.12.grid_ref, bf16[12,288,288]{2,1,0:T(8,128)(2,1)} %get-tuple-element.13.grid_t_ref, ...), custom_call_target="tpu_custom_call" | custom-call | flops 13759414272 | bytes 7962624 | tf_op jit(solution)/shard_map/coupling/pallas_call | solution.py:392
  158.1 5.1 %all-to-all-start.3 = ((f32[4,3,16,288]{3,2,1,0:T(8,128)}), f32[4,3,16,288]{3,2,1,0:T(8,128)S(1)}, u32[]{:S(2)}, u32[]{:S(2)}) async-start(f32[4,3,16,288]{3,2,1,0:T(8,128)} %bitcast.21), calls=%async_computation.3 | async-start | bytes 589824 | tf_op jit(solution)/shard_map/all_to_all | solution.py:465
  163.2 9.7 %all-to-all-done.3 = f32[4,3,16,288]{3,2,1,0:T(8,128)S(1)} async-done(((f32[4,3,16,288]{3,2,1,0:T(8,128)}), f32[4,3,16,288]{3,2,1,0:T(8,128)S(1)}, u32[]{:S(2)}, u32[]{:S(2)}) %all-to-all-start.3) | async-done | bytes 221216 | tf_op jit(solution)/shard_map/all_to_all | solution.py:465
  173.0 0.8 reshape.131
  173.8 0.1 pad_maximum_fusion.1
  173.8 0.6 reshape.130
  (22 shorter events, 0.2 us)
Async XLA Ops:
  7.2 1.6 copy-start
  7.2 42.0 %all-gather.3.cloned.1.call-start = ((), (), s32[]{:S(2)}) async-start(), calls=%async_computation.4 | async-start | bytes 3317760 | tf_op jit(solution)/shard_map/all_gather | solution.py:444
  22.3 23.0 %copy-start.2 = (bf16[288]{0:T(512)(128)(2,1)S(1)}, bf16[288]{0:T(512)(128)(2,1)}, u32[]{:S(2)}) copy-start(bf16[288]{0:T(512)(128)(2,1)} %param.8) | copy-start | bytes 1732
  41.7 51.3 %all-to-all-start.2 = ((bf16[4,14,72,256]{3,2,1,0:T(8,128)(2,1)}), bf16[4,14,72,256]{3,2,1,0:T(8,128)(2,1)S(1)}, u32[]{:S(2)}, u32[]{:S(2)}) async-start(bf16[4,14,72,256]{3,2,1,0:T(8,128)(2,1)} %get-tuple-element.17), calls=%async_computation.2 | async-start | bytes 4128768 | tf_op jit(solution)/shard_map/all_to_all | solution.py:451
  45.5 11.2 %copy-start.4 = (f32[6]{0:T(128)}, f32[6]{0:T(128)S(1)}, u32[]{:S(2)}) copy-start(f32[6]{0:T(128)S(1)} %slice_bitcast_fusion.1.home_ref) | copy-start | bytes 76
  45.7 47.3 %copy-start.3 = (f32[12]{0:T(128)}, f32[12]{0:T(128)S(1)}, u32[]{:S(2)}) copy-start(f32[12]{0:T(128)S(1)} %slice_bitcast_fusion.home_ref) | copy-start | bytes 148
  93.0 3.6 %copy-start.1 = (bf16[4,14,72,256]{3,2,1,0:T(8,128)(2,1)}, bf16[4,14,72,256]{3,2,1,0:T(8,128)(2,1)S(1)}, u32[]{:S(2)}) copy-start(bf16[4,14,72,256]{3,2,1,0:T(8,128)(2,1)S(1)} %all-to-all-done.2.moved_ref) | copy-start | bytes 6193156
  93.0 65.1 %all-to-all-start.1 = ((f32[4,3,8,288]{3,2,1,0:T(8,128)}), f32[4,3,8,288]{3,2,1,0:T(8,128)S(1)}, u32[]{:S(2)}, u32[]{:S(2)}) async-start(f32[4,3,8,288]{3,2,1,0:T(8,128)} %bitcast.22), calls=%async_computation.1 | async-start | bytes 294912 | tf_op jit(solution)/shard_map/all_to_all | solution.py:465
  158.1 14.8 %all-to-all-start.3 = ((f32[4,3,16,288]{3,2,1,0:T(8,128)}), f32[4,3,16,288]{3,2,1,0:T(8,128)S(1)}, u32[]{:S(2)}, u32[]{:S(2)}) async-start(f32[4,3,16,288]{3,2,1,0:T(8,128)} %bitcast.21), calls=%async_computation.3 | async-start | bytes 589824 | tf_op jit(solution)/shard_map/all_to_all | solution.py:465
Sparse Core Ops, SparseCore 0:
  9.7 39.3 all-gather.2

commit v3 on v2

--- a/solution.py
+++ b/solution.py
@@ -185,10 +185,22 @@
     )(pack)
 
 
+def interleave(heavy, light):
+    done = 0
+    for i, task in enumerate(heavy):
+        task()
+        upto = (i + 1) * len(light) // len(heavy)
+        while done < upto:
+            light[done]()
+            done += 1
+    while done < len(light):
+        light[done]()
+        done += 1
+
+
 def coupling_kernel(
     share,
     block,
-    buffers,
     partner_ref,
     weight_ref,
     home_ref,
@@ -203,12 +215,11 @@
     grid_rest_ref,
     inner_rest_ref,
     gather_ref,
-    table_ref,
-    sums_ref,
     pick_ref,
+    rest_value_ref,
     *work,
 ):
-    inners, values = work[:buffers], work[buffers:]
+    inners, values, tabs, sums, firsts = (work[2 * i : 2 * i + 2] for i in range(5))
     pairs = grid_ref.shape[0]
     modes = grid_ref.shape[2]
     rest = modes - MAIN
@@ -221,7 +232,8 @@
     for x in range(pairs):
         grid_rest_ref[x * rest : (x + 1) * rest, :] = grid_t_ref[x, MAIN:, :]
     eye = identity(modes)
-    inner_rest_ref[...] = jnp.zeros_like(inner_rest_ref)
+    if share * rest < rest_lanes:
+        inner_rest_ref[...] = jnp.zeros_like(inner_rest_ref)
     for r in range(share):
         slot, spot = share + r // per_slot, r % per_slot
         half, spot = spot // (per_slot // 2), spot % (per_slot // 2)
@@ -243,122 +255,181 @@
         row_id < share * TILE, row_id // TILE, (row_id - share * TILE) // rest
     )
     pick_ref[...] = (branch == col_id).astype(BF16)
-    out_ref[...] = jnp.zeros_like(out_ref)
-
-    def contract_first(x, step, into):
-        start = pl.multiple_of(step * (block * modes), 16)
-        found = dot_nn(turned_ref[pl.ds(start, block * modes), :], grid_ref[x, :, :MAIN])
+    for ref in (out_ref, *sums, *firsts):
+        ref[...] = jnp.zeros_like(ref)
+
+    def contract_first(x, r, b, into):
+        def task():
+            found = dot_nn(turned_ref[r * modes : (r + 1) * modes, :], grid_ref[x, :, :MAIN])
+            into[:, b * MAIN : (b + 1) * MAIN] = found.astype(BF16)
+
+        return task
+
+    def contract_second(x, b, source, into):
+        lanes = slice(b * MAIN, (b + 1) * MAIN)
+
+        def task():
+            into[:, lanes] = dot_nn(grid_t_ref[partner_ref[x]], source[:, lanes])
+
+        return task
+
+    def line_shapes(v, t, w, c1, c2):
+        p = v * v
+        d = t[0] - w
+        e = t[1] - c1
+        return (
+            (p * t[2]) * pl.reciprocal(d * d + s2, approx=True),
+            (p * t[3]) * pl.reciprocal(e * e + c2, approx=True),
+        )
+
+    def weigh(step, source, tab, sum_ref, first_ref):
+        state = {}
+
+        def begin():
+            state["w"] = [home_ref[step * block + b] for b in range(block)]
+            state["c1"] = [w * w - s2 for w in state["w"]]
+            state["c2"] = [(4.0 * s2) * (w * w) for w in state["w"]]
+            state["total"] = [jnp.zeros((8, MAIN), F32) for _ in range(block)]
+
+        def rows(n):
+            def task():
+                if n == 0:
+                    begin()
+                t = [tab[k, n : n + 16, :MAIN] for k in range(4)]
+                for b in range(block):
+                    v = source[n : n + 16, b * MAIN : (b + 1) * MAIN]
+                    f, u = line_shapes(v, t, state["w"][b], state["c1"][b], state["c2"][b])
+                    state["total"][b] = state["total"][b] + (f[:8] + f[8:])
+                    r = step * block + b
+                    sum_ref[n : n + 16, r * TILE : (r + 1) * TILE] = (
+                        u[:, :TILE] + u[:, TILE:]
+                    ).astype(BF16)
+                if n + 16 == modes:
+                    for b in range(block):
+                        r = step * block + b
+                        line = jnp.sum(state["total"][b], axis=0, keepdims=True)
+                        first_ref[r : r + 1, :MAIN] = line * (1.0 / state["w"][b])
+
+            return task
+
+        return [rows(n) for n in range(0, modes, 16)]
+
+    def contract_rest(x):
+        def task():
+            rest_value_ref[...] = dot_nt(grid_t_ref[partner_ref[x]], inner_rest_ref[x])
+
+        return task
+
+    def weigh_rest(tab, sum_ref, first_ref):
+        def tile(start):
+            lanes = slice(start, start + TILE)
+            spot = share * TILE + start
+            state = {}
+
+            def rows(n):
+                def task():
+                    if n == 0:
+                        state["total"] = jnp.zeros((8, TILE), F32)
+                        state["w"] = home_row_ref[0:1, lanes]
+                        state["c1"] = home_row_ref[1:2, lanes]
+                        state["c2"] = home_row_ref[2:3, lanes]
+                    for k in range(n, n + 48, 16):
+                        t = [tab[i, k : k + 16, MAIN:] for i in range(4)]
+                        f, u = line_shapes(
+                            rest_value_ref[k : k + 16, lanes], t, state["w"], state["c1"], state["c2"]
+                        )
+                        state["total"] = state["total"] + (f[:8] + f[8:])
+                        sum_ref[k : k + 16, spot : spot + TILE] = u.astype(BF16)
+                    if n + 48 == modes:
+                        line = jnp.sum(state["total"], axis=0, keepdims=True)
+                        line = line * home_row_ref[3:4, lanes]
+                        for b in range(TILE // rest):
+                            r = start // rest + b
+                            if r < share:
+                                first_ref[r : r + 1, MAIN:] = line[:, b * rest : (b + 1) * rest]
+
+                return task
+
+            return [rows(n) for n in range(0, modes, 48)]
+
+        return [task for start in range(0, rest_lanes, TILE) for task in tile(start)]
+
+    def tables(x, tab):
+        state = {}
+
+        def begin():
+            w1 = freq_row_ref[x]
+            spots = lax.broadcasted_iota(jnp.int32, freq_col_ref.shape, 1)
+            w2 = jnp.sum(
+                jnp.where(spots == partner_ref[x], freq_col_ref[...], 0.0), axis=1, keepdims=True
+            )
+            state["w"] = (w1, w2)
+            state["o"] = (occupy(w1), occupy(w2))
+            scale = weight_ref[x] * (smearing / math.pi / modes)
+            state["i"] = (scale / w1, 1.0 / w2)
+
+        def rows(n):
+            def task():
+                if n == 0:
+                    begin()
+                part = slice(n, n + 48)
+                (w1, w2), (o1, o2), (i1, i2) = state["w"], state["o"], state["i"]
+                w2, o2, i2 = w2[part], o2[part], i2[part]
+                a = w1 - w2
+                both = i1 * i2
+                tab[0, part, :] = w1 + w2
+                tab[1, part, :] = a * a
+                tab[2, part, :] = (1.0 + o1 + o2) * both
+                tab[3, part, :] = (4.0 * a) * (o2 - o1) * both
+
+            return task
+
+        return [rows(n) for n in range(0, modes, 48)]
+
+    def finish(x, target, sum_ref, first_ref):
+        second = dot_nn(sum_ref[...], pick_ref[...])
+        out_ref[x, :share, :] += first_ref[:share, :]
+        out_ref[target, :share, :] += second.T[:share, :]
+
+    for task in tables(0, tabs[0]):
+        task()
+    for g in range(2):
         for b in range(block):
-            into[:, b * MAIN : (b + 1) * MAIN] = found[b * modes : (b + 1) * modes].astype(BF16)
-
-    def contract_second(x, source, into):
-        into[...] = dot_nn(grid_t_ref[partner_ref[x]], source[...])
-
-    def weigh(x, step, source):
-        ws = [home_ref[step * block + b] for b in range(block)]
-        c1s = [w * w - s2 for w in ws]
-        c2s = [(4.0 * s2) * (w * w) for w in ws]
-        totals = [jnp.zeros((8, MAIN), F32) for _ in ws]
-        for n in range(0, modes, 16):
-            t0 = table_ref[0, n : n + 16, :MAIN]
-            t1 = table_ref[1, n : n + 16, :MAIN]
-            t2 = table_ref[2, n : n + 16, :MAIN]
-            t3 = table_ref[3, n : n + 16, :MAIN]
-            for b in range(block):
-                v = source[n : n + 16, b * MAIN : (b + 1) * MAIN]
-                p = v * v
-                d = t0 - ws[b]
-                t = (p * t2) * pl.reciprocal(d * d + s2, approx=True)
-                totals[b] = totals[b] + (t[:8] + t[8:])
-                e = t1 - c1s[b]
-                u = (p * t3) * pl.reciprocal(e * e + c2s[b], approx=True)
-                sums_ref[step * block + b, n : n + 16, :] = (u[:, :TILE] + u[:, TILE:]).astype(BF16)
-        for b in range(block):
-            line = jnp.sum(totals[b], axis=0, keepdims=True) * (1.0 / ws[b])
-            out_ref[x, pl.ds(step * block + b, 1), :MAIN] += line
-
-    def tables(x):
-        w1 = freq_row_ref[x]
-        spots = lax.broadcasted_iota(jnp.int32, freq_col_ref.shape, 1)
-        w2 = jnp.sum(
-            jnp.where(spots == partner_ref[x], freq_col_ref[...], 0.0), axis=1, keepdims=True
-        )
-        o1, o2 = occupy(w1), occupy(w2)
-        scale = weight_ref[x] * (smearing / math.pi / modes)
-        i1, i2 = scale / w1, 1.0 / w2
-        for n in range(0, modes, 48):
-            w2n, o2n, i2n = w2[n : n + 48], o2[n : n + 48], i2[n : n + 48]
-            a = w1 - w2n
-            both = i1 * i2n
-            table_ref[0, n : n + 48, :] = w1 + w2n
-            table_ref[1, n : n + 48, :] = a * a
-            table_ref[2, n : n + 48, :] = (1.0 + o1 + o2n) * both
-            table_ref[3, n : n + 48, :] = (4.0 * a) * (o2n - o1) * both
-
-    def finish(x):
-        target = partner_ref[x]
-        left = grid_t_ref[target]
-        for start in range(0, rest_lanes, TILE):
-            found = dot_nt(left, inner_rest_ref[x, start : start + TILE, :])
-            w = home_row_ref[:, start : start + TILE]
-            c1 = w * w - s2
-            c2 = (4.0 * s2) * (w * w)
-            total = jnp.zeros((8, TILE), F32)
-            for n in range(0, modes, 16):
-                v = found[n : n + 16]
-                p = v * v
-                d = table_ref[0, n : n + 16, MAIN:] - w
-                t = (p * table_ref[2, n : n + 16, MAIN:]) * pl.reciprocal(
-                    d * d + s2, approx=True
-                )
-                total = total + (t[:8] + t[8:])
-                e = table_ref[1, n : n + 16, MAIN:] - c1
-                u = (p * table_ref[3, n : n + 16, MAIN:]) * pl.reciprocal(
-                    e * e + c2, approx=True
-                )
-                sums_ref[share + start // TILE, n : n + 16, :] = u.astype(BF16)
-            line = jnp.sum(total, axis=0, keepdims=True) / w
-            for b in range(TILE // rest):
-                r = start // rest + b
-                if r < share:
-                    out_ref[x, r : r + 1, MAIN:] += line[:, b * rest : (b + 1) * rest]
-        second = jnp.zeros((modes, TILE), F32)
-        for c in range(share + rest_lanes // TILE):
-            second += dot_nn(sums_ref[c], pick_ref[c * TILE : (c + 1) * TILE, :])
-        out_ref[target, :share, :] += second.T[:share, :]
-
-    if buffers > 1:
-        contract_first(0, 0, inners[0])
-        contract_first(0, 1, inners[1])
-        contract_second(0, inners[0], values[0])
-
-    def one_pair(x, carry):
-        tables(x)
-
-        def some(i, inner_carry):
-            for u in range(buffers):
-                step = i * buffers + u
-
-                def ahead(by):
-                    wraps = (step + by >= steps).astype(jnp.int32)
-                    return jnp.minimum(x + wraps, pairs - 1), step + by - wraps * steps
-
-                if buffers > 1:
-                    x1, _ = ahead(1)
-                    contract_second(x1, inners[(u + 1) % buffers], values[(u + 1) % buffers])
-                    x2, step2 = ahead(2)
-                    contract_first(x2, step2, inners[(u + 2) % buffers])
-                else:
-                    contract_first(x, step, inners[0])
-                    contract_second(x, inners[0], values[0])
-                weigh(x, step, values[u])
-            return inner_carry
-
-        lax.fori_loop(0, steps // buffers, some, 0)
-        finish(x)
+            x, step = jnp.int32(g // steps), g % steps
+            contract_first(x, step * block + b, b, inners[g])()
+    for b in range(block):
+        contract_second(jnp.int32(0), b, inners[0], values[0])()
+
+    def two_pairs(i, carry):
+        for e in range(2):
+            x = i * 2 + e
+
+            def later(g):
+                return jnp.minimum(i * 2 + g // steps, pairs - 1), g % steps
+
+            before = jnp.maximum(x - 1, 0)
+            target = partner_ref[before]
+            finish_sum, finish_first = sums[1 - e], firsts[1 - e]
+            extra = weigh_rest(tabs[e], sums[e], firsts[e])
+            extra = extra + tables(jnp.minimum(x + 1, pairs - 1), tabs[1 - e])
+            contract_rest(x)()
+            for s in range(steps):
+                g = e * steps + s
+                heavy = []
+                for b in range(block):
+                    x1, _ = later(g + 1)
+                    heavy.append(contract_second(x1, b, inners[(g + 1) % 2], values[(g + 1) % 2]))
+                for b in range(block):
+                    x2, step2 = later(g + 2)
+                    heavy.append(contract_first(x2, step2 * block + b, b, inners[g % 2]))
+                light = weigh(s, values[g % 2], tabs[e], sums[e], firsts[e])
+                light = light + extra[s * len(extra) // steps : (s + 1) * len(extra) // steps]
+                interleave(heavy, light)
+            finish(before, target, finish_sum, finish_first)
         return carry
 
-    lax.fori_loop(0, pairs, one_pair, 0)
+    lax.fori_loop(0, pairs // 2, two_pairs, 0)
+    finish(pairs - 1, partner_ref[pairs - 1], sums[1], firsts[1])
 
     totals = jnp.zeros(out_ref.shape[1:], F32)
     for y in range(pairs):
@@ -380,17 +451,18 @@
     share = home.shape[0]
     rest = modes - MAIN
     rest_lanes = ceil_div(share * rest, TILE) * TILE
-    home_row = jnp.repeat(home, rest)
-    home_row = jnp.pad(home_row, (0, rest_lanes - share * rest), constant_values=1.0)[None]
+    row = jnp.repeat(home, rest)
+    row = jnp.pad(row, (0, rest_lanes - share * rest), constant_values=1.0)
+    s2 = smearing * smearing
+    home_row = jnp.stack([row, row * row - s2, (4.0 * s2) * (row * row), 1.0 / row])
     padded = (share // 8 + 1) * 8
     smem = pl.BlockSpec(memory_space=pltpu.SMEM)
     vmem = pl.BlockSpec(memory_space=pltpu.VMEM)
     tiles = share + rest_lanes // TILE
     block = 3 if share % 3 == 0 else 1
-    steps = share // block
-    buffers = 2 if steps % 2 == 0 else 3 if steps % 3 == 0 else 1
+    assert pairs % 2 == 0
     return pl.pallas_call(
-        functools.partial(coupling_kernel, share, block, buffers),
+        functools.partial(coupling_kernel, share, block),
         in_specs=[smem, smem, smem, vmem, vmem, vmem, vmem, vmem, vmem],
         out_specs=vmem,
         out_shape=jax.ShapeDtypeStruct((pairs, padded, modes), F32),
@@ -399,12 +471,14 @@
             pltpu.VMEM((pairs * rest, modes), BF16),
             pltpu.VMEM((pairs, rest_lanes, modes), BF16),
             pltpu.VMEM((modes, modes), F32),
-            pltpu.VMEM((4, modes, MAIN + TILE), F32),
-            pltpu.VMEM((tiles, modes, TILE), BF16),
             pltpu.VMEM((tiles * TILE, TILE), BF16),
+            pltpu.VMEM((modes, rest_lanes), F32),
         ]
-        + [pltpu.VMEM((modes, block * MAIN), BF16)] * buffers
-        + [pltpu.VMEM((modes, block * MAIN), F32)] * buffers,
+        + [pltpu.VMEM((modes, block * MAIN), BF16)] * 2
+        + [pltpu.VMEM((modes, block * MAIN), F32)] * 2
+        + [pltpu.VMEM((4, modes, MAIN + TILE), F32)] * 2
+        + [pltpu.VMEM((modes, tiles * TILE), BF16)] * 2
+        + [pltpu.VMEM((padded, modes), F32)] * 2,
         compiler_params=pltpu.CompilerParams(vmem_limit_bytes=56 << 20),
         cost_estimate=pl.CostEstimate(
             flops=4 * share * pairs * modes**3,

time: 182 us -> 167 us (0.918)
  blocking collectives: 19.4 us -> 0 us
  Pallas kernels: 118 us -> 103 us
  waiting for transfers between devices: 11.8 us -> 25.8 us
  starting transfers between devices: 12.3 us -> 16.6 us
    all_to_all x1 -> x0, blocking collectives: 19.4 us -> none  [local(): lax.all_to_all(x, ('mode', 'fc'), split_axis=0, concat_axis=0, tiled=True)]
    pallas_call x2, Pallas kernels: 97.8 us -> 82.4 us  [coupling(): pl.pallas_call(functools.partial(coupling_kernel, share, block), in_specs...]
    all_to_all x1 -> x2, waiting for transfers between devices: 0.01 us -> 14.1 us  [local(): lax.all_to_all(x, ('mode', 'fc'), split_axis=0, concat_axis=0, tiled=True)]
    all_to_all x1 -> x2, starting transfers between devices: 3.6 us -> 7.86 us  [local(): lax.all_to_all(x, ('mode', 'fc'), split_axis=0, concat_axis=0, tiled=True)]
  transfers between devices with their start and end apart: 4 -> 5, of which waited for: 2 -> 3; matrix products, arithmetic and copies ran while one was open for 1% -> 1% of each run, Pallas kernels for 65% -> 62%
where the time goes in v3:
time: 167 us; the launch traced here: 166 us
  Pallas kernels  103 us (62%)
  waiting for transfers between devices  25.8 us (15%)
  starting transfers between devices  16.6 us (10%)
  between operations  14.2 us (9%)
  other arithmetic  3.64 us (2%)
  local copies, waits for them, and re-layouts  3 us (2%)
    pallas_call x2, Pallas kernels, coupling(): pl.pallas_call(functools.partial(coupling_kernel, share, block), in_specs...  82.4 us
    all_to_all x2, waiting for transfers between devices, local(): lax.all_to_all(x, ('mode', 'fc'), split_axis=0, concat_axis=0, tiled=True)  14.1 us
    pallas_call x1, Pallas kernels, project(): pl.pallas_call(functools.partial(project_kernel, groups, n_qp, group, chu...  12.7 us
    all_to_all x2, waiting for transfers between devices, local(): lax.all_to_all(found.reshape(n_qp, own_pairs, found.shape[1], modes), 'qp...  9.66 us
    all_to_all x2, starting transfers between devices, local(): lax.all_to_all(found.reshape(n_qp, own_pairs, found.shape[1], modes), 'qp...  8.69 us
    all_to_all x2, starting transfers between devices, local(): lax.all_to_all(x, ('mode', 'fc'), split_axis=0, concat_axis=0, tiled=True)  7.86 us
    pallas_call x1, Pallas kernels, arrange(): pl.pallas_call(arrange_kernel, in_specs=[vmem], out_specs=[smem, smem, vm...  7.52 us
  transfers between devices with their start and end apart: 5, of which 3 were waited for; matrix products, arithmetic and copies ran while one was open for 1% of the time, Pallas kernels for 62%

profile of v3, /device:TPU:0, one launch (start us, length us, event | category | flops | bytes accessed | tf_op | source)
XLA Modules:
  0.0 165.8 jit_solution(12516975798071210173)
XLA Ops:
  7.2 0.8 select_convert_fusion
  8.0 0.7 pad_maximum_fusion
  8.8 0.8 fusion.1
  9.6 12.7 %project.1 = (bf16[4,7,72,256]{3,2,1,0:T(8,128)(2,1)}, bf16[4,14,72,256]{3,2,1,0:T(8,128)(2,1)}) custom-call(s32[1]{0:T(128)} %bitcast.7.here_ref, bf16[288,288]{1,0:T(8,128)(2,1)} %home_ref.1, bf16[288,20736]{1,0:T(8,128)(2,1)} %force_ref.1), custom_call_target="tpu_custom_call" | custom-call | tf_op jit(solution)/shard_map/project/pallas_call | solution.py:102
  22.3 4.3 %all-to-all-start = ((bf16[4,7,72,256]{3,2,1,0:T(8,128)(2,1)}), bf16[4,7,72,256]{3,2,1,0:T(8,128)(2,1)S(1)}, u32[]{:S(2)}, u32[]{:S(2)}) async-start(bf16[4,7,72,256]{3,2,1,0:T(8,128)(2,1)} %get-tuple-element.16), calls=%async_computation | async-start | bytes 2064384 | tf_op jit(solution)/shard_map/all_to_all | solution.py:525
  26.6 0.1 reshape.163
  26.7 0.1 dynamic_slice.7
  26.8 14.1 %all-to-all-done.moved_ref = bf16[4,7,72,256]{3,2,1,0:T(8,128)(2,1)S(1)} async-done(((bf16[4,7,72,256]{3,2,1,0:T(8,128)(2,1)}), bf16[4,7,72,256]{3,2,1,0:T(8,128)(2,1)S(1)}, u32[]{:S(2)}, u32[]{:S(2)}) %all-to-all-start) | async-done | bytes 1032224 | tf_op jit(solution)/shard_map/all_to_all | solution.py:525
  40.9 1.0 copy-done.2
  41.9 3.6 %all-to-all-start.2 = ((bf16[4,14,72,256]{3,2,1,0:T(8,128)(2,1)}), bf16[4,14,72,256]{3,2,1,0:T(8,128)(2,1)S(1)}, u32[]{:S(2)}, u32[]{:S(2)}) async-start(bf16[4,14,72,256]{3,2,1,0:T(8,128)(2,1)} %get-tuple-element.17), calls=%async_computation.2 | async-start | bytes 4128768 | tf_op jit(solution)/shard_map/all_to_all | solution.py:525
  45.6 0.1 reshape.157
  45.8 0.1 stack.38
  45.9 0.6 pad_maximum_fusion.2.home_row_ref
  46.5 0.6 pad_maximum_fusion.1.home_row_ref
  47.1 2.0 %all-gather.3.cloned.1.call-done = bf16[24,160,288]{2,1,0:T(8,128)(2,1)} async-done(((bf16[3,160,288]{2,1,0:T(8,128)(2,1)}), bf16[24,160,288]{2,1,0:T(8,128)(2,1)}) %all-gather.3.cloned.1.call-update) | async-done | bytes 2211856 | tf_op jit(solution)/shard_map/all_gather | solution.py:518
  49.2 7.5 %arrange.1 = (s32[12]{0:T(128)}, f32[12]{0:T(128)}, bf16[12,288,288]{2,1,0:T(8,128)(2,1)}, bf16[12,288,288]{2,1,0:T(8,128)(2,1)}, f32[12,1,384]{2,1,0:T(1,128)}, /*index=5*/f32[288,128]{1,0:T(8,128)}) custom-call(bf16[4,2,3,160,288]{4,3,2,1,0:T(8,128)(2,1)} %bitcast.21), custom_call_target="tpu_custom_call" | custom-call | tf_op jit(solution)/shard_map/arrange/pallas_call | solution.py:171
  56.7 30.3 %coupling.2 = f32[12,8,288]{2,1,0:T(8,128)} custom-call(s32[12]{0:T(128)} %get-tuple-element.10.partner_ref, f32[12]{0:T(128)} %get-tuple-element.11.weight_ref, f32[6]{0:T(128)} %copy-done.5, bf16[12,288,288]{2,1,0:T(8,128)(2,1)} %get-tuple-element.12.grid_ref, bf16[12,288,288]{2,1,0:T(8,128)(2,1)} %get-tuple-element.13.grid_t_ref, ...), custom_call_target="tpu_custom_call" | custom-call | flops 6879707136 | bytes 3981312 | tf_op jit(solution)/shard_map/coupling/pallas_call | solution.py:464
  87.0 3.6 %all-to-all-start.1 = ((f32[4,3,8,288]{3,2,1,0:T(8,128)}), f32[4,3,8,288]{3,2,1,0:T(8,128)S(1)}, u32[]{:S(2)}, u32[]{:S(2)}) async-start(f32[4,3,8,288]{3,2,1,0:T(8,128)} %bitcast.25), calls=%async_computation.1 | async-start | bytes 294912 | tf_op jit(solution)/shard_map/all_to_all | solution.py:539
  90.6 52.1 %coupling.3 = f32[12,16,288]{2,1,0:T(8,128)} custom-call(s32[12]{0:T(128)} %get-tuple-element.10.partner_ref, f32[12]{0:T(128)} %get-tuple-element.11.weight_ref, f32[12]{0:T(128)} %copy-done.4, bf16[12,288,288]{2,1,0:T(8,128)(2,1)} %get-tuple-element.12.grid_ref, bf16[12,288,288]{2,1,0:T(8,128)(2,1)} %get-tuple-element.13.grid_t_ref, ...), custom_call_target="tpu_custom_call" | custom-call | flops 13759414272 | bytes 7962624 | tf_op jit(solution)/shard_map/coupling/pallas_call | solution.py:464
  142.7 5.1 %all-to-all-start.3 = ((f32[4,3,16,288]{3,2,1,0:T(8,128)}), f32[4,3,16,288]{3,2,1,0:T(8,128)S(1)}, u32[]{:S(2)}, u32[]{:S(2)}) async-start(f32[4,3,16,288]{3,2,1,0:T(8,128)} %bitcast.24), calls=%async_computation.3 | async-start | bytes 589824 | tf_op jit(solution)/shard_map/all_to_all | solution.py:539
  147.8 9.7 %all-to-all-done.3 = f32[4,3,16,288]{3,2,1,0:T(8,128)S(1)} async-done(((f32[4,3,16,288]{3,2,1,0:T(8,128)}), f32[4,3,16,288]{3,2,1,0:T(8,128)S(1)}, u32[]{:S(2)}, u32[]{:S(2)}) %all-to-all-start.3) | async-done | bytes 221216 | tf_op jit(solution)/shard_map/all_to_all | solution.py:539
  157.5 0.8 reshape.161
  158.3 0.1 pad_maximum_fusion.3
  158.4 0.6 reshape.160
  (28 shorter events, 0.5 us)
Async XLA Ops:
  7.2 1.6 copy-start
  7.2 42.0 %all-gather.3.cloned.1.call-start = ((), (), s32[]{:S(2)}) async-start(), calls=%async_computation.4 | async-start | bytes 3317760 | tf_op jit(solution)/shard_map/all_gather | solution.py:518
  9.6 17.0 %copy-start.3 = (bf16[288]{0:T(512)(128)(2,1)S(1)}, bf16[288]{0:T(512)(128)(2,1)}, u32[]{:S(2)}) copy-start(bf16[288]{0:T(512)(128)(2,1)} %param.8) | copy-start | bytes 1732
  22.3 18.5 %all-to-all-start = ((bf16[4,7,72,256]{3,2,1,0:T(8,128)(2,1)}), bf16[4,7,72,256]{3,2,1,0:T(8,128)(2,1)S(1)}, u32[]{:S(2)}, u32[]{:S(2)}) async-start(bf16[4,7,72,256]{3,2,1,0:T(8,128)(2,1)} %get-tuple-element.16), calls=%async_computation | async-start | bytes 2064384 | tf_op jit(solution)/shard_map/all_to_all | solution.py:525
  40.9 1.0 copy-start.2
  41.9 45.1 %all-to-all-start.2 = ((bf16[4,14,72,256]{3,2,1,0:T(8,128)(2,1)}), bf16[4,14,72,256]{3,2,1,0:T(8,128)(2,1)S(1)}, u32[]{:S(2)}, u32[]{:S(2)}) async-start(bf16[4,14,72,256]{3,2,1,0:T(8,128)(2,1)} %get-tuple-element.17), calls=%async_computation.2 | async-start | bytes 4128768 | tf_op jit(solution)/shard_map/all_to_all | solution.py:525
  45.5 11.2 %copy-start.5 = (f32[6]{0:T(128)}, f32[6]{0:T(128)S(1)}, u32[]{:S(2)}) copy-start(f32[6]{0:T(128)S(1)} %slice_bitcast_fusion.1.home_ref) | copy-start | bytes 76
  45.7 41.3 %copy-start.4 = (f32[12]{0:T(128)}, f32[12]{0:T(128)S(1)}, u32[]{:S(2)}) copy-start(f32[12]{0:T(128)S(1)} %slice_bitcast_fusion.home_ref) | copy-start | bytes 148
  87.0 3.6 %copy-start.1 = (bf16[4,14,72,256]{3,2,1,0:T(8,128)(2,1)}, bf16[4,14,72,256]{3,2,1,0:T(8,128)(2,1)S(1)}, u32[]{:S(2)}) copy-start(bf16[4,14,72,256]{3,2,1,0:T(8,128)(2,1)S(1)} %all-to-all-done.2.moved_ref) | copy-start | bytes 6193156
  87.0 55.7 %all-to-all-start.1 = ((f32[4,3,8,288]{3,2,1,0:T(8,128)}), f32[4,3,8,288]{3,2,1,0:T(8,128)S(1)}, u32[]{:S(2)}, u32[]{:S(2)}) async-start(f32[4,3,8,288]{3,2,1,0:T(8,128)} %bitcast.25), calls=%async_computation.1 | async-start | bytes 294912 | tf_op jit(solution)/shard_map/all_to_all | solution.py:539
  142.7 14.8 %all-to-all-start.3 = ((f32[4,3,16,288]{3,2,1,0:T(8,128)}), f32[4,3,16,288]{3,2,1,0:T(8,128)S(1)}, u32[]{:S(2)}, u32[]{:S(2)}) async-start(f32[4,3,16,288]{3,2,1,0:T(8,128)} %bitcast.24), calls=%async_computation.3 | async-start | bytes 589824 | tf_op jit(solution)/shard_map/all_to_all | solution.py:539
Sparse Core Ops, SparseCore 0:
  9.7 39.3 all-gather.2

commit v4 on v3

--- a/solution.py
+++ b/solution.py
@@ -19,6 +19,15 @@
 
 def ceil_div(a, b):
     return -(-a // b)
+
+
+def grant(shapes):
+    total = 0
+    for shape, dtype in shapes:
+        rows, lanes = shape[-2:]
+        size = ceil_div(rows, 16) * 16 * ceil_div(lanes, TILE) * TILE * jnp.dtype(dtype).itemsize
+        total += math.prod(shape[:-2]) * size
+    return total + total // 8 + (4 << 20)
 
 
 def occupy(energy):
@@ -114,7 +123,11 @@
             pltpu.VMEM((2, depth * lines, TILE), F32),
             pltpu.VMEM((depth * lines, TILE), F32),
         ],
-        compiler_params=pltpu.CompilerParams(vmem_limit_bytes=56 << 20),
+        compiler_params=pltpu.CompilerParams(vmem_limit_bytes=grant(
+                [((modes, per_step * modes), BF16)] * 2
+                + [(shape, BF16) for shape in shapes] * 2
+                + [((3 * depth * lines, TILE), F32), ((4 * lines, per_step * modes), F32)]
+            )),
         name="project",
     )(here, home_vectors, force_table)
 
@@ -180,7 +193,9 @@
             jax.ShapeDtypeStruct((pairs, 1, MAIN + TILE), F32),
             jax.ShapeDtypeStruct((modes, TILE), F32),
         ],
-        compiler_params=pltpu.CompilerParams(vmem_limit_bytes=56 << 20),
+        compiler_params=pltpu.CompilerParams(vmem_limit_bytes=grant(
+                [(pack.shape, BF16)] + [((pairs, modes, modes), BF16)] * 2 + [((pairs, 8, modes), F32)]
+            )),
         name="arrange",
     )(pack)
 
@@ -214,12 +229,13 @@
     turned_ref,
     grid_rest_ref,
     inner_rest_ref,
-    gather_ref,
     pick_ref,
     rest_value_ref,
     *work,
 ):
-    inners, values, tabs, sums, firsts = (work[2 * i : 2 * i + 2] for i in range(5))
+    gathers, inners, values, tabs, sums, rest_sums, firsts = (
+        work[2 * i : 2 * i + 2] for i in range(7)
+    )
     pairs = grid_ref.shape[0]
     modes = grid_ref.shape[2]
     rest = modes - MAIN
@@ -237,6 +253,7 @@
     for r in range(share):
         slot, spot = share + r // per_slot, r % per_slot
         half, spot = spot // (per_slot // 2), spot % (per_slot // 2)
+        gather_ref = gathers[r % 2]
         for s in range(sources):
             gather_ref[s * depth : (s + 1) * depth, :MAIN] = moved_ref[s, r].astype(F32)
             tail = moved_ref[s, slot, :, half * TILE : (half + 1) * TILE].astype(F32)
@@ -251,11 +268,8 @@
 
     row_id = lax.broadcasted_iota(jnp.int32, pick_ref.shape, 0)
     col_id = lax.broadcasted_iota(jnp.int32, pick_ref.shape, 1)
-    branch = jnp.where(
-        row_id < share * TILE, row_id // TILE, (row_id - share * TILE) // rest
-    )
-    pick_ref[...] = (branch == col_id).astype(BF16)
-    for ref in (out_ref, *sums, *firsts):
+    pick_ref[...] = (row_id // rest == col_id).astype(BF16)
+    for ref in (out_ref, *sums, *rest_sums, *firsts):
         ref[...] = jnp.zeros_like(ref)
 
     def contract_first(x, r, b, into):
@@ -301,9 +315,9 @@
                     f, u = line_shapes(v, t, state["w"][b], state["c1"][b], state["c2"][b])
                     state["total"][b] = state["total"][b] + (f[:8] + f[8:])
                     r = step * block + b
-                    sum_ref[n : n + 16, r * TILE : (r + 1) * TILE] = (
-                        u[:, :TILE] + u[:, TILE:]
-                    ).astype(BF16)
+                    sum_ref[n : n + 16, r : r + 1] = jnp.sum(
+                        u[:, :TILE] + u[:, TILE:], axis=1, keepdims=True
+                    )
                 if n + 16 == modes:
                     for b in range(block):
                         r = step * block + b
@@ -323,7 +337,6 @@
     def weigh_rest(tab, sum_ref, first_ref):
         def tile(start):
             lanes = slice(start, start + TILE)
-            spot = share * TILE + start
             state = {}
 
             def rows(n):
@@ -339,7 +352,7 @@
                             rest_value_ref[k : k + 16, lanes], t, state["w"], state["c1"], state["c2"]
                         )
                         state["total"] = state["total"] + (f[:8] + f[8:])
-                        sum_ref[k : k + 16, spot : spot + TILE] = u.astype(BF16)
+                        sum_ref[k : k + 16, lanes] = u.astype(BF16)
                     if n + 48 == modes:
                         line = jnp.sum(state["total"], axis=0, keepdims=True)
                         line = line * home_row_ref[3:4, lanes]
@@ -386,8 +399,8 @@
 
         return [rows(n) for n in range(0, modes, 48)]
 
-    def finish(x, target, sum_ref, first_ref):
-        second = dot_nn(sum_ref[...], pick_ref[...])
+    def finish(x, target, sum_ref, rest_sum_ref, first_ref):
+        second = sum_ref[...] + dot_nn(rest_sum_ref[...], pick_ref[...])
         out_ref[x, :share, :] += first_ref[:share, :]
         out_ref[target, :share, :] += second.T[:share, :]
 
@@ -409,8 +422,7 @@
 
             before = jnp.maximum(x - 1, 0)
             target = partner_ref[before]
-            finish_sum, finish_first = sums[1 - e], firsts[1 - e]
-            extra = weigh_rest(tabs[e], sums[e], firsts[e])
+            extra = weigh_rest(tabs[e], rest_sums[e], firsts[e])
             extra = extra + tables(jnp.minimum(x + 1, pairs - 1), tabs[1 - e])
             contract_rest(x)()
             for s in range(steps):
@@ -425,11 +437,11 @@
                 light = weigh(s, values[g % 2], tabs[e], sums[e], firsts[e])
                 light = light + extra[s * len(extra) // steps : (s + 1) * len(extra) // steps]
                 interleave(heavy, light)
-            finish(before, target, finish_sum, finish_first)
+            finish(before, target, sums[1 - e], rest_sums[1 - e], firsts[1 - e])
         return carry
 
     lax.fori_loop(0, pairs // 2, two_pairs, 0)
-    finish(pairs - 1, partner_ref[pairs - 1], sums[1], firsts[1])
+    finish(pairs - 1, partner_ref[pairs - 1], sums[1], rest_sums[1], firsts[1])
 
     totals = jnp.zeros(out_ref.shape[1:], F32)
     for y in range(pairs):
@@ -458,28 +470,33 @@
     padded = (share // 8 + 1) * 8
     smem = pl.BlockSpec(memory_space=pltpu.SMEM)
     vmem = pl.BlockSpec(memory_space=pltpu.VMEM)
-    tiles = share + rest_lanes // TILE
     block = 3 if share % 3 == 0 else 1
     assert pairs % 2 == 0
+    scratch = (
+        [
+            pltpu.VMEM((share * modes, modes), BF16),
+            pltpu.VMEM((pairs * rest, modes), BF16),
+            pltpu.VMEM((pairs, rest_lanes, modes), BF16),
+            pltpu.VMEM((rest_lanes, TILE), BF16),
+            pltpu.VMEM((modes, rest_lanes), F32),
+        ]
+        + [pltpu.VMEM((modes, modes), F32)] * 2
+        + [pltpu.VMEM((modes, block * MAIN), BF16)] * 2
+        + [pltpu.VMEM((modes, block * MAIN), F32)] * 2
+        + [pltpu.VMEM((4, modes, MAIN + TILE), F32)] * 2
+        + [pltpu.VMEM((modes, TILE), F32)] * 2
+        + [pltpu.VMEM((modes, rest_lanes), BF16)] * 2
+        + [pltpu.VMEM((padded, modes), F32)] * 2
+    )
+    held = [(x.shape, x.dtype) for x in (grid, grid_t, freq_rows, freq_cols, moved)]
+    held += [(x.shape, x.dtype) for x in scratch] + [((pairs, padded, modes), F32)] * 2
     return pl.pallas_call(
         functools.partial(coupling_kernel, share, block),
         in_specs=[smem, smem, smem, vmem, vmem, vmem, vmem, vmem, vmem],
         out_specs=vmem,
         out_shape=jax.ShapeDtypeStruct((pairs, padded, modes), F32),
-        scratch_shapes=[
-            pltpu.VMEM((share * modes, modes), BF16),
-            pltpu.VMEM((pairs * rest, modes), BF16),
-            pltpu.VMEM((pairs, rest_lanes, modes), BF16),
-            pltpu.VMEM((modes, modes), F32),
-            pltpu.VMEM((tiles * TILE, TILE), BF16),
-            pltpu.VMEM((modes, rest_lanes), F32),
-        ]
-        + [pltpu.VMEM((modes, block * MAIN), BF16)] * 2
-        + [pltpu.VMEM((modes, block * MAIN), F32)] * 2
-        + [pltpu.VMEM((4, modes, MAIN + TILE), F32)] * 2
-        + [pltpu.VMEM((modes, tiles * TILE), BF16)] * 2
-        + [pltpu.VMEM((padded, modes), F32)] * 2,
-        compiler_params=pltpu.CompilerParams(vmem_limit_bytes=56 << 20),
+        scratch_shapes=scratch,
+        compiler_params=pltpu.CompilerParams(vmem_limit_bytes=grant(held)),
         cost_estimate=pl.CostEstimate(
             flops=4 * share * pairs * modes**3,
             bytes_accessed=8 * share * modes * modes,
@@ -503,7 +520,7 @@
     share = ceil_div(group, n_qp)
     here = lax.axis_index("qp")
     if share % 6 == 0 and share > 6:
-        chunks = ((0, 6), (6, share - 6))
+        chunks = ((0, share - 6), (share - 6, 6))
     else:
         chunks = ((0, share),)
 

time: 167 us -> 161 us (0.964)
  Pallas kernels: 103 us -> 84.6 us
  local copies, waits for them, and re-layouts: 3 us -> 16.7 us
    unnamed x13 -> x23, local copies, waits for them, and re-layouts: 1.02 us -> 14.7 us
    pallas_call x2, Pallas kernels: 82.4 us -> 71.9 us  [coupling(): pl.pallas_call(functools.partial(coupling_kernel, share, block), in_specs...]
    pallas_call x1, Pallas kernels: 12.7 us -> 8.72 us  [project(): pl.pallas_call(functools.partial(project_kernel, groups, n_qp, group, chu...]
    pallas_call x1, Pallas kernels: 7.52 us -> 3.91 us  [arrange(): pl.pallas_call(arrange_kernel, in_specs=[vmem], out_specs=[smem, smem, vm...]
  transfers between devices with their start and end apart: 5 -> 5, of which waited for: 3 -> 3; matrix products, arithmetic and copies ran while one was open for 1% -> 0% of each run, Pallas kernels for 62% -> 53%
where the time goes in v4:
time: 161 us; the launch traced here: 160 us
  Pallas kernels  84.6 us (53%)
  waiting for transfers between devices  25.8 us (16%)
  local copies, waits for them, and re-layouts  16.7 us (10%)
  starting transfers between devices  16.7 us (10%)
  between operations  14.2 us (9%)
  other arithmetic  2.48 us (2%)
    pallas_call x2, Pallas kernels, coupling(): pl.pallas_call(functools.partial(coupling_kernel, share, block), in_specs...  71.9 us
    unnamed x23, local copies, waits for them, and re-layouts  14.7 us
    all_to_all x2, waiting for transfers between devices, local(): lax.all_to_all(x, ('mode', 'fc'), split_axis=0, concat_axis=0, tiled=True)  14.1 us
    all_to_all x2, waiting for transfers between devices, local(): lax.all_to_all(found.reshape(n_qp, own_pairs, found.shape[1], modes), 'qp...  9.7 us
    all_to_all x2, starting transfers between devices, local(): lax.all_to_all(found.reshape(n_qp, own_pairs, found.shape[1], modes), 'qp...  8.8 us
    pallas_call x1, Pallas kernels, project(): pl.pallas_call(functools.partial(project_kernel, groups, n_qp, group, chu...  8.72 us
    all_to_all x2, starting transfers between devices, local(): lax.all_to_all(x, ('mode', 'fc'), split_axis=0, concat_axis=0, tiled=True)  7.82 us
    pallas_call x1, Pallas kernels, arrange(): pl.pallas_call(arrange_kernel, in_specs=[vmem], out_specs=[smem, smem, vm...  3.91 us
  transfers between devices with their start and end apart: 5, of which 3 were waited for; matrix products, arithmetic and copies ran while one was open for 0% of the time, Pallas kernels for 53%

profile of v4, /device:TPU:0, one launch (start us, length us, event | category | flops | bytes accessed | tf_op | source)
XLA Modules:
  0.0 160.4 jit_solution(7395263897519067441)
XLA Ops:
  7.2 0.8 select_convert_fusion
  8.0 0.7 pad_maximum_fusion
  8.8 0.8 fusion.1
  9.7 4.4 %copy-done.1 = bf16[288,20736]{1,0:T(8,128)(2,1)S(1)} copy-done((bf16[288,20736]{1,0:T(8,128)(2,1)S(1)}, bf16[288,20736]{1,0:T(8,128)(2,1)}, u32[]{:S(2)}) %copy-start.1) | copy-done | bytes 11943960
  14.1 0.9 copy-done.5
  15.0 8.7 %project.1 = (bf16[4,14,72,256]{3,2,1,0:T(8,128)(2,1)}, bf16[4,7,72,256]{3,2,1,0:T(8,128)(2,1)}) custom-call(s32[1]{0:T(128)} %bitcast.3.here_ref, bf16[288,288]{1,0:T(8,128)(2,1)S(1)} %copy-done.5, bf16[288,20736]{1,0:T(8,128)(2,1)S(1)} %copy-done.1), custom_call_target="tpu_custom_call" | custom-call | tf_op jit(solution)/shard_map/project/pallas_call | solution.py:111
  23.7 4.2 %all-to-all-start.2 = ((bf16[4,7,72,256]{3,2,1,0:T(8,128)(2,1)}), bf16[4,7,72,256]{3,2,1,0:T(8,128)(2,1)S(1)}, u32[]{:S(2)}, u32[]{:S(2)}) async-start(bf16[4,7,72,256]{3,2,1,0:T(8,128)(2,1)} %get-tuple-element.17), calls=%async_computation.2 | async-start | bytes 2064384 | tf_op jit(solution)/shard_map/all_to_all | solution.py:542
  28.1 14.1 %all-to-all-done.2.moved_ref = bf16[4,7,72,256]{3,2,1,0:T(8,128)(2,1)S(1)} async-done(((bf16[4,7,72,256]{3,2,1,0:T(8,128)(2,1)}), bf16[4,7,72,256]{3,2,1,0:T(8,128)(2,1)S(1)}, u32[]{:S(2)}, u32[]{:S(2)}) %all-to-all-start.2) | async-done | bytes 1032224 | tf_op jit(solution)/shard_map/all_to_all | solution.py:542
  42.2 1.0 copy-done.3
  43.2 3.6 %all-to-all-start = ((bf16[4,14,72,256]{3,2,1,0:T(8,128)(2,1)}), bf16[4,14,72,256]{3,2,1,0:T(8,128)(2,1)S(1)}, u32[]{:S(2)}, u32[]{:S(2)}) async-start(bf16[4,14,72,256]{3,2,1,0:T(8,128)(2,1)} %get-tuple-element.16), calls=%async_computation | async-start | bytes 4128768 | tf_op jit(solution)/shard_map/all_to_all | solution.py:542
  47.3 1.9 %all-gather.3.cloned.1.call-done = bf16[24,160,288]{2,1,0:T(8,128)(2,1)} async-done(((bf16[3,160,288]{2,1,0:T(8,128)(2,1)}), bf16[24,160,288]{2,1,0:T(8,128)(2,1)}) %all-gather.3.cloned.1.call-update) | async-done | bytes 2211856 | tf_op jit(solution)/shard_map/all_gather | solution.py:535
  49.2 1.8 %copy-done.2 = bf16[24,160,288]{2,1,0:T(8,128)(2,1)S(1)} copy-done((bf16[24,160,288]{2,1,0:T(8,128)(2,1)S(1)}, bf16[24,160,288]{2,1,0:T(8,128)(2,1)}, u32[]{:S(2)}) %copy-start.2) | copy-done | bytes 2211864
  51.0 3.9 %arrange.1 = (s32[12]{0:T(128)S(1)}, f32[12]{0:T(128)S(1)}, bf16[12,288,288]{2,1,0:T(8,128)(2,1)S(1)}, bf16[12,288,288]{2,1,0:T(8,128)(2,1)S(1)}, f32[12,1,384]{2,1,0:T(1,128)S(1)}, /*index=5*/f32[288,128]{1,0:T(8,128)S(1)}) custom-call(bf16[4,2,3,160,288]{4,3,2,1,0:T(8,128)(2,1)S(1)} %bitcast.21), custom_call_target="tpu_custom_call" | custom-call | tf_op jit(solution)/shard_map/arrange/pallas_call | solution.py:184
  54.9 26.8 %coupling.3 = f32[12,8,288]{2,1,0:T(8,128)} custom-call(s32[12]{0:T(128)S(1)} %get-tuple-element.10.partner_ref, f32[12]{0:T(128)S(1)} %get-tuple-element.11.weight_ref, f32[6]{0:T(128)S(1)} %slice_bitcast_fusion.home_ref, bf16[12,288,288]{2,1,0:T(8,128)(2,1)S(1)} %get-tuple-element.12.grid_ref, bf16[12,288,288]{2,1,0:T(8,128)(2,1)S(1)} %get-tuple-element.13.grid_t_ref, ...), custom_call_target="tpu_custom_call" | custom-call | flops 6879707136 | bytes 3981312 | tf_op jit(solution)/shard_map/coupling/pallas_call | solution.py:493
  81.7 1.5 copy-done.6
  83.3 1.5 copy-done.8
  84.8 3.7 %all-to-all-start.3 = ((f32[4,3,8,288]{3,2,1,0:T(8,128)}), f32[4,3,8,288]{3,2,1,0:T(8,128)S(1)}, u32[]{:S(2)}, u32[]{:S(2)}) async-start(f32[4,3,8,288]{3,2,1,0:T(8,128)} %bitcast.11), calls=%async_computation.3 | async-start | bytes 294912 | tf_op jit(solution)/shard_map/all_to_all | solution.py:556
  88.5 1.7 %copy-done.7 = bf16[12,288,288]{2,1,0:T(8,128)(2,1)S(1)} copy-done((bf16[12,288,288]{2,1,0:T(8,128)(2,1)S(1)}, bf16[12,288,288]{2,1,0:T(8,128)(2,1)}, u32[]{:S(2)}) %copy-start.7) | copy-done | bytes 1990680
  90.3 1.7 %copy-done.9 = bf16[12,288,288]{2,1,0:T(8,128)(2,1)S(1)} copy-done((bf16[12,288,288]{2,1,0:T(8,128)(2,1)S(1)}, bf16[12,288,288]{2,1,0:T(8,128)(2,1)}, u32[]{:S(2)}) %copy-start.9) | copy-done | bytes 1990680
  92.0 45.2 %coupling.2 = f32[12,16,288]{2,1,0:T(8,128)} custom-call(s32[12]{0:T(128)S(1)} %get-tuple-element.10.partner_ref, f32[12]{0:T(128)S(1)} %get-tuple-element.11.weight_ref, f32[12]{0:T(128)S(1)} %slice_bitcast_fusion.1.home_ref, bf16[12,288,288]{2,1,0:T(8,128)(2,1)S(1)} %copy-done.7, bf16[12,288,288]{2,1,0:T(8,128)(2,1)S(1)} %copy-done.9, ...), custom_call_target="tpu_custom_call" | custom-call | flops 13759414272 | bytes 7962624 | tf_op jit(solution)/shard_map/coupling/pallas_call | solution.py:493
  137.2 5.1 %all-to-all-start.1 = ((f32[4,3,16,288]{3,2,1,0:T(8,128)}), f32[4,3,16,288]{3,2,1,0:T(8,128)S(1)}, u32[]{:S(2)}, u32[]{:S(2)}) async-start(f32[4,3,16,288]{3,2,1,0:T(8,128)} %bitcast.4), calls=%async_computation.1 | async-start | bytes 589824 | tf_op jit(solution)/shard_map/all_to_all | solution.py:556
  142.3 9.7 %all-to-all-done.1 = f32[4,3,16,288]{3,2,1,0:T(8,128)S(1)} async-done(((f32[4,3,16,288]{3,2,1,0:T(8,128)}), f32[4,3,16,288]{3,2,1,0:T(8,128)S(1)}, u32[]{:S(2)}, u32[]{:S(2)}) %all-to-all-start.1) | async-done | bytes 221216 | tf_op jit(solution)/shard_map/all_to_all | solution.py:556
  152.0 0.6 reshape.160
  152.7 0.8 reshape.161
  (38 shorter events, 0.9 us)
Async XLA Ops:
  7.2 1.6 copy-start
  7.2 42.0 %all-gather.3.cloned.1.call-start = ((), (), s32[]{:S(2)}) async-start(), calls=%async_computation.4 | async-start | bytes 3317760 | tf_op jit(solution)/shard_map/all_gather | solution.py:535
  9.7 4.4 %copy-start.1 = (bf16[288,20736]{1,0:T(8,128)(2,1)S(1)}, bf16[288,20736]{1,0:T(8,128)(2,1)}, u32[]{:S(2)}) copy-start(bf16[288,20736]{1,0:T(8,128)(2,1)} %force_ref.1) | copy-start | bytes 35831812
  14.1 0.9 copy-start.5
  15.0 12.9 %copy-start.10 = (bf16[288]{0:T(512)(128)(2,1)S(1)}, bf16[288]{0:T(512)(128)(2,1)}, u32[]{:S(2)}) copy-start(bf16[288]{0:T(512)(128)(2,1)} %param.8) | copy-start | bytes 1732
  23.7 18.5 %all-to-all-start.2 = ((bf16[4,7,72,256]{3,2,1,0:T(8,128)(2,1)}), bf16[4,7,72,256]{3,2,1,0:T(8,128)(2,1)S(1)}, u32[]{:S(2)}, u32[]{:S(2)}) async-start(bf16[4,7,72,256]{3,2,1,0:T(8,128)(2,1)} %get-tuple-element.17), calls=%async_computation.2 | async-start | bytes 2064384 | tf_op jit(solution)/shard_map/all_to_all | solution.py:542
  42.2 1.0 copy-start.3
  43.2 41.6 %all-to-all-start = ((bf16[4,14,72,256]{3,2,1,0:T(8,128)(2,1)}), bf16[4,14,72,256]{3,2,1,0:T(8,128)(2,1)S(1)}, u32[]{:S(2)}, u32[]{:S(2)}) async-start(bf16[4,14,72,256]{3,2,1,0:T(8,128)(2,1)} %get-tuple-element.16), calls=%async_computation | async-start | bytes 4128768 | tf_op jit(solution)/shard_map/all_to_all | solution.py:542
  49.2 1.8 %copy-start.2 = (bf16[24,160,288]{2,1,0:T(8,128)(2,1)S(1)}, bf16[24,160,288]{2,1,0:T(8,128)(2,1)}, u32[]{:S(2)}) copy-start(bf16[24,160,288]{2,1,0:T(8,128)(2,1)} %all-gather.3.cloned.1.call-done) | copy-start | bytes 6635524
  51.0 3.9 %copy-start.4 = (bf16[4,7,72,256]{3,2,1,0:T(8,128)(2,1)S(1)}, bf16[4,7,72,256]{3,2,1,0:T(8,128)(2,1)}, u32[]{:S(2)}) copy-start(bf16[4,7,72,256]{3,2,1,0:T(8,128)(2,1)} %copy-done.3) | copy-start | bytes 3096580
  81.7 1.5 copy-start.6
  83.3 1.5 copy-start.8
  84.8 52.4 %all-to-all-start.3 = ((f32[4,3,8,288]{3,2,1,0:T(8,128)}), f32[4,3,8,288]{3,2,1,0:T(8,128)S(1)}, u32[]{:S(2)}, u32[]{:S(2)}) async-start(f32[4,3,8,288]{3,2,1,0:T(8,128)} %bitcast.11), calls=%async_computation.3 | async-start | bytes 294912 | tf_op jit(solution)/shard_map/all_to_all | solution.py:556
  88.5 1.7 %copy-start.7 = (bf16[12,288,288]{2,1,0:T(8,128)(2,1)S(1)}, bf16[12,288,288]{2,1,0:T(8,128)(2,1)}, u32[]{:S(2)}) copy-start(bf16[12,288,288]{2,1,0:T(8,128)(2,1)} %copy-done.6) | copy-start | bytes 5971972
  90.3 1.7 %copy-start.9 = (bf16[12,288,288]{2,1,0:T(8,128)(2,1)S(1)}, bf16[12,288,288]{2,1,0:T(8,128)(2,1)}, u32[]{:S(2)}) copy-start(bf16[12,288,288]{2,1,0:T(8,128)(2,1)} %copy-done.8) | copy-start | bytes 5971972
  137.2 14.8 %all-to-all-start.1 = ((f32[4,3,16,288]{3,2,1,0:T(8,128)}), f32[4,3,16,288]{3,2,1,0:T(8,128)S(1)}, u32[]{:S(2)}, u32[]{:S(2)}) async-start(f32[4,3,16,288]{3,2,1,0:T(8,128)} %bitcast.4), calls=%async_computation.1 | async-start | bytes 589824 | tf_op jit(solution)/shard_map/all_to_all | solution.py:556
Sparse Core Ops, SparseCore 0:
  9.8 39.3 all-gather.2

commit v5 on v4

--- a/solution.py
+++ b/solution.py
@@ -21,13 +21,7 @@
     return -(-a // b)
 
 
-def grant(shapes):
-    total = 0
-    for shape, dtype in shapes:
-        rows, lanes = shape[-2:]
-        size = ceil_div(rows, 16) * 16 * ceil_div(lanes, TILE) * TILE * jnp.dtype(dtype).itemsize
-        total += math.prod(shape[:-2]) * size
-    return total + total // 8 + (4 << 20)
+VMEM_BYTES = 56 << 20
 
 
 def occupy(energy):
@@ -57,6 +51,7 @@
     depth = outs[0].shape[2]
     step = pl.program_id(0)
     here = force_ref.shape[1] // modes
+    pitch = lines + 1
 
     @pl.when(step == 0)
     def _():
@@ -69,7 +64,7 @@
 
     result = dot_nn(rows_ref[...], force_ref[...])
     for c in range(here):
-        row = pl.multiple_of((step * here + c) * lines, 8)
+        row = (step * here + c) * pitch
         piece = result[:, c * modes : (c + 1) * modes]
         main_ref[0, pl.ds(row, lines), :] = piece[:, :TILE]
         main_ref[1, pl.ds(row, lines), :] = piece[:, TILE:MAIN]
@@ -86,7 +81,7 @@
                 for r in range(count):
                     for h in range(2):
                         out_ref[t, r, :, h * TILE : (h + 1) * TILE] = main_ref[
-                            h, pl.ds(base + r, depth, stride=lines), :
+                            h, pl.ds(base + r, depth, stride=pitch), :
                         ].astype(BF16)
                 for g in range(ceil_div(count, per_slot)):
                     for h in range(2):
@@ -94,7 +89,7 @@
                         for b in range(per_slot // 2):
                             r = g * per_slot + h * (per_slot // 2) + b
                             if r < count:
-                                piece = rest_ref[pl.ds(base + r, depth, stride=lines), :]
+                                piece = rest_ref[pl.ds(base + r, depth, stride=pitch), :]
                                 if b > 0:
                                     piece = pltpu.roll(piece, b * rest, 1)
                                 packed = jnp.where(lane // rest == b, piece, packed)
@@ -120,14 +115,10 @@
         out_shape=[jax.ShapeDtypeStruct(shape, BF16) for shape in shapes],
         scratch_shapes=[
             pltpu.VMEM((lines, modes), BF16),
-            pltpu.VMEM((2, depth * lines, TILE), F32),
-            pltpu.VMEM((depth * lines, TILE), F32),
+            pltpu.VMEM((2, (depth + 1) * (lines + 1), TILE), F32),
+            pltpu.VMEM(((depth + 1) * (lines + 1), TILE), F32),
         ],
-        compiler_params=pltpu.CompilerParams(vmem_limit_bytes=grant(
-                [((modes, per_step * modes), BF16)] * 2
-                + [(shape, BF16) for shape in shapes] * 2
-                + [((3 * depth * lines, TILE), F32), ((4 * lines, per_step * modes), F32)]
-            )),
+        compiler_params=pltpu.CompilerParams(vmem_limit_bytes=VMEM_BYTES),
         name="project",
     )(here, home_vectors, force_table)
 
@@ -139,36 +130,108 @@
     ).astype(BF16)
 
 
+def pack_kernel(part_ref, partner_ref, weight_ref, grid_ref, freq_ref, out_ref):
+    own_pairs, modes, _ = grid_ref.shape
+    rest = modes - MAIN
+    lines = rest // 2
+    part = part_ref[0]
+    line = lax.broadcasted_iota(jnp.int32, (lines, modes), 0)
+    column = lax.broadcasted_iota(jnp.int32, (lines, modes), 1)
+    select = (column == MAIN + part * lines + line).astype(BF16)
+    freqs = freq_ref[...].astype(F32)
+    blank = jnp.zeros((own_pairs, TILE - rest), F32)
+    freq_tiles = (
+        freqs[:, :TILE],
+        freqs[:, TILE:MAIN],
+        jnp.concatenate([freqs[:, MAIN:], blank], axis=1),
+    )
+    line16 = lax.broadcasted_iota(jnp.int32, (16, TILE), 0)
+    lane16 = lax.broadcasted_iota(jnp.int32, (16, TILE), 1)
+    for s in range(own_pairs):
+        for p in range(2):
+
+            @pl.when(part == p)
+            def _():
+                out_ref[s, :modes, :] = grid_ref[s, :, p * TILE : (p + 1) * TILE]
+
+        turned = dot_nt(select, grid_ref[s])
+        turned = (
+            turned[:, :TILE],
+            turned[:, TILE:MAIN],
+            jnp.concatenate([turned[:, MAIN:], jnp.zeros((lines, TILE - rest), F32)], axis=1),
+        )
+        for h in range(3):
+            start = modes + h * lines
+            out_ref[s, start : start + lines, :] = turned[h].astype(BF16)
+        pair = partner_ref[s].astype(F32)
+        weight = weight_ref[s].astype(F32)
+        side = jnp.where(lane16 == 0, pair, jnp.where(lane16 == 1, weight, 0.0))
+        side = jnp.where(line16 == 3, side, 0.0)
+        for h in range(3):
+            side = jnp.where(line16 == h, freq_tiles[h][s : s + 1], side)
+        start = modes + 3 * lines
+        out_ref[s, start : start + 16, :] = side.astype(BF16)
+
+
+def pack_own(part, partner, weights, grid_vectors, partner_frequencies):
+    own_pairs, modes, _ = grid_vectors.shape
+    smem = pl.BlockSpec(memory_space=pltpu.SMEM)
+    vmem = pl.BlockSpec(memory_space=pltpu.VMEM)
+    rows = modes + 3 * (modes - MAIN) // 2 + 16
+    return pl.pallas_call(
+        pack_kernel,
+        in_specs=[smem, smem, smem, vmem, vmem],
+        out_specs=vmem,
+        out_shape=jax.ShapeDtypeStruct((own_pairs, rows, TILE), BF16),
+        compiler_params=pltpu.CompilerParams(vmem_limit_bytes=VMEM_BYTES),
+        name="pack_own",
+    )(part, partner, weights, grid_vectors, partner_frequencies)
+
+
 def arrange_kernel(
     pack_ref, partner_ref, weight_ref, grid_ref, grid_t_ref, freq_row_ref, freq_col_ref
 ):
-    owners, parts, each, rows, modes = pack_ref.shape
-    half = modes // parts
+    owners, parts, each, rows, _ = pack_ref.shape
+    modes = grid_ref.shape[1]
     rest = modes - MAIN
-    eye = identity(modes)
-    source = lax.broadcasted_iota(jnp.int32, (modes, MAIN + TILE), 0)
-    place = lax.broadcasted_iota(jnp.int32, (modes, MAIN + TILE), 1)
-    wanted = jnp.where(place < MAIN, place, MAIN + (place - MAIN) % rest)
-    spread = (source == wanted).astype(BF16)
-    lane = lax.broadcasted_iota(jnp.int32, freq_col_ref.shape, 1)
-    lane16 = lax.broadcasted_iota(jnp.int32, (16, modes), 1)
-    line16 = lax.broadcasted_iota(jnp.int32, (16, modes), 0)
+    lines = rest // parts
+    eye = identity(MAIN)
+    source = lax.broadcasted_iota(jnp.int32, (TILE, TILE), 0)
+    place = lax.broadcasted_iota(jnp.int32, (TILE, TILE), 1)
+    spread = (source == place % rest).astype(BF16)
+    eye_tile = (source == place).astype(BF16)
+    lane = lax.broadcasted_iota(jnp.int32, (TILE, freq_col_ref.shape[1]), 1)
+    line16 = lax.broadcasted_iota(jnp.int32, (16, TILE), 0)
+    lane16 = lax.broadcasted_iota(jnp.int32, (16, TILE), 1)
     freq_col_ref[...] = jnp.zeros_like(freq_col_ref)
 
     def one(q, carry):
         for s in range(each):
             x = q * each + s
             for part in range(parts):
-                grid_ref[x, part * half : (part + 1) * half, :] = pack_ref[q, part, s, :half, :]
-            grid_t_ref[x] = dot_nt(eye, grid_ref[x]).astype(BF16)
-            side = pack_ref[q, 0, s, half : half + 16, :]
-            freq_row_ref[x] = dot_nn(side, spread)[0:1, :]
-            column = dot_nt(eye, side)[:, 0:1]
-            freq_col_ref[...] = jnp.where(lane == x, column, freq_col_ref[...])
+                grid_ref[x, :, part * TILE : (part + 1) * TILE] = pack_ref[q, part, s, :modes, :]
+                for h in range(3):
+                    start, width = modes + h * lines, min(TILE, modes - h * TILE)
+                    piece = pack_ref[q, part, s, start : start + lines, :]
+                    grid_t_ref[
+                        x, MAIN + part * lines : MAIN + (part + 1) * lines, h * TILE : h * TILE + width
+                    ] = piece[:, :width]
+            grid_t_ref[x, :MAIN, :] = dot_nt(eye, grid_ref[x]).astype(BF16)
+            side = pack_ref[q, 0, s, modes + 3 * lines : modes + 3 * lines + 16, :]
             wide = side.astype(F32)
+            freq_row_ref[x, :, :TILE] = wide[0:1]
+            freq_row_ref[x, :, TILE:MAIN] = wide[1:2]
+            freq_row_ref[x, :, MAIN:] = dot_nn(side, spread)[2:3]
+            columns = dot_nt(eye_tile, side)
+            for h in range(3):
+                width = min(TILE, modes - h * TILE)
+                here = slice(h * TILE, h * TILE + width)
+                freq_col_ref[here, :] = jnp.where(
+                    lane[:width] == x, columns[:width, h : h + 1], freq_col_ref[here, :]
+                )
             for spot, ref in ((0, partner_ref), (1, weight_ref)):
                 found = jnp.sum(
-                    jnp.where(jnp.logical_and(line16 == 1, lane16 == spot), wide, 0.0)
+                    jnp.where(jnp.logical_and(line16 == 3, lane16 == spot), wide, 0.0)
                 )
                 ref[x] = found.astype(ref.dtype)
         return carry
@@ -176,8 +239,8 @@
     lax.fori_loop(0, owners, one, 0)
 
 
-def arrange(pack):
-    owners, parts, each, _, modes = pack.shape
+def arrange(pack, modes):
+    owners, parts, each, _, _ = pack.shape
     pairs = owners * each
     smem = pl.BlockSpec(memory_space=pltpu.SMEM)
     vmem = pl.BlockSpec(memory_space=pltpu.VMEM)
@@ -188,14 +251,12 @@
         out_shape=[
             jax.ShapeDtypeStruct((pairs,), jnp.int32),
             jax.ShapeDtypeStruct((pairs,), F32),
-            jax.ShapeDtypeStruct((pairs, modes, modes), BF16),
+            jax.ShapeDtypeStruct((pairs, modes, MAIN), BF16),
             jax.ShapeDtypeStruct((pairs, modes, modes), BF16),
             jax.ShapeDtypeStruct((pairs, 1, MAIN + TILE), F32),
             jax.ShapeDtypeStruct((modes, TILE), F32),
         ],
-        compiler_params=pltpu.CompilerParams(vmem_limit_bytes=grant(
-                [(pack.shape, BF16)] + [((pairs, modes, modes), BF16)] * 2 + [((pairs, 8, modes), F32)]
-            )),
+        compiler_params=pltpu.CompilerParams(vmem_limit_bytes=VMEM_BYTES),
         name="arrange",
     )(pack)
 
@@ -237,7 +298,7 @@
         work[2 * i : 2 * i + 2] for i in range(7)
     )
     pairs = grid_ref.shape[0]
-    modes = grid_ref.shape[2]
+    modes = grid_ref.shape[1]
     rest = modes - MAIN
     sources, depth = moved_ref.shape[0], moved_ref.shape[2]
     per_slot = MAIN // rest
@@ -274,7 +335,7 @@
 
     def contract_first(x, r, b, into):
         def task():
-            found = dot_nn(turned_ref[r * modes : (r + 1) * modes, :], grid_ref[x, :, :MAIN])
+            found = dot_nn(turned_ref[r * modes : (r + 1) * modes, :], grid_ref[x])
             into[:, b * MAIN : (b + 1) * MAIN] = found.astype(BF16)
 
         return task
@@ -399,10 +460,16 @@
 
         return [rows(n) for n in range(0, modes, 48)]
 
-    def finish(x, target, sum_ref, rest_sum_ref, first_ref):
-        second = sum_ref[...] + dot_nn(rest_sum_ref[...], pick_ref[...])
+    def collect(sum_ref, rest_sum_ref, state):
+        def task():
+            second = sum_ref[...] + dot_nn(rest_sum_ref[...], pick_ref[...])
+            state["second"] = second.T[:share, :]
+
+        return task
+
+    def deliver(x, target, state, first_ref):
         out_ref[x, :share, :] += first_ref[:share, :]
-        out_ref[target, :share, :] += second.T[:share, :]
+        out_ref[target, :share, :] += state["second"]
 
     for task in tables(0, tabs[0]):
         task()
@@ -425,6 +492,7 @@
             extra = weigh_rest(tabs[e], rest_sums[e], firsts[e])
             extra = extra + tables(jnp.minimum(x + 1, pairs - 1), tabs[1 - e])
             contract_rest(x)()
+            done = {}
             for s in range(steps):
                 g = e * steps + s
                 heavy = []
@@ -436,12 +504,16 @@
                     heavy.append(contract_first(x2, step2 * block + b, b, inners[g % 2]))
                 light = weigh(s, values[g % 2], tabs[e], sums[e], firsts[e])
                 light = light + extra[s * len(extra) // steps : (s + 1) * len(extra) // steps]
+                if s == 0:
+                    heavy.insert(1, collect(sums[1 - e], rest_sums[1 - e], done))
                 interleave(heavy, light)
-            finish(before, target, sums[1 - e], rest_sums[1 - e], firsts[1 - e])
+            deliver(before, target, done, firsts[1 - e])
         return carry
 
     lax.fori_loop(0, pairs // 2, two_pairs, 0)
-    finish(pairs - 1, partner_ref[pairs - 1], sums[1], rest_sums[1], firsts[1])
+    last = {}
+    collect(sums[1], rest_sums[1], last)()
+    deliver(pairs - 1, partner_ref[pairs - 1], last, firsts[1])
 
     totals = jnp.zeros(out_ref.shape[1:], F32)
     for y in range(pairs):
@@ -459,7 +531,7 @@
 
 
 def coupling(partner, weights, home, grid, grid_t, freq_rows, freq_cols, moved):
-    pairs, modes = grid.shape[0], grid.shape[2]
+    pairs, modes = grid.shape[0], grid.shape[1]
     share = home.shape[0]
     rest = modes - MAIN
     rest_lanes = ceil_div(share * rest, TILE) * TILE
@@ -488,15 +560,13 @@
         + [pltpu.VMEM((modes, rest_lanes), BF16)] * 2
         + [pltpu.VMEM((padded, modes), F32)] * 2
     )
-    held = [(x.shape, x.dtype) for x in (grid, grid_t, freq_rows, freq_cols, moved)]
-    held += [(x.shape, x.dtype) for x in scratch] + [((pairs, padded, modes), F32)] * 2
     return pl.pallas_call(
         functools.partial(coupling_kernel, share, block),
         in_specs=[smem, smem, smem, vmem, vmem, vmem, vmem, vmem, vmem],
         out_specs=vmem,
         out_shape=jax.ShapeDtypeStruct((pairs, padded, modes), F32),
         scratch_shapes=scratch,
-        compiler_params=pltpu.CompilerParams(vmem_limit_bytes=grant(held)),
+        compiler_params=pltpu.CompilerParams(vmem_limit_bytes=VMEM_BYTES),
         cost_estimate=pl.CostEstimate(
             flops=4 * share * pairs * modes**3,
             bytes_accessed=8 * share * modes * modes,
@@ -520,20 +590,15 @@
     share = ceil_div(group, n_qp)
     here = lax.axis_index("qp")
     if share % 6 == 0 and share > 6:
-        chunks = ((0, share - 6), (share - 6, 6))
+        chunks = ((0, 6), (6, share - 6))
     else:
         chunks = ((0, share),)
 
-    part_rows = modes // n_fc
-    part = lax.dynamic_slice_in_dim(
-        grid_vectors, lax.axis_index("fc") * part_rows, part_rows, axis=1
-    )
-    lane = jnp.arange(modes)[None]
-    small = jnp.where(lane == 0, partner[:, None], jnp.where(lane == 1, weights[:, None], 0))
-    side = jnp.stack([partner_frequencies, small.astype(BF16)], axis=1)
-    side = jnp.pad(side, ((0, 0), (0, 14), (0, 0)))
-    pack = lax.all_gather(jnp.concatenate([part, side], axis=1), ("qp", "fc"), axis=0)
-    pack = pack.reshape(n_qp, n_fc, own_pairs, part_rows + 16, modes)
+    assert n_fc * TILE == MAIN
+    own_part = lax.axis_index("fc").astype(jnp.int32)[None]
+    pack = pack_own(own_part, partner, weights, grid_vectors, partner_frequencies)
+    pack = lax.all_gather(pack, ("qp", "fc"), axis=0)
+    pack = pack.reshape(n_qp, n_fc, own_pairs, pack.shape[2], TILE)
 
     sent = project(
         here.astype(jnp.int32)[None], home_vectors, force_table, groups, n_qp, group, share, chunks
@@ -547,7 +612,7 @@
     home = jnp.pad(home, ((0, 0), (0, share * n_qp - group)), constant_values=1.0)
     home = lax.dynamic_slice(home, (own, here * share), (1, share)).reshape(share)
 
-    shared = arrange(pack)
+    shared = arrange(pack, modes)
     parts, widths = [], []
     for (first, count), block in zip(chunks, moved):
         found = coupling(

time: 161 us -> 154 us (0.957)
  local copies, waits for them, and re-layouts: 16.7 us -> 1.96 us
  Pallas kernels: 84.6 us -> 93.8 us
  waiting for transfers between devices: 25.8 us -> 23.8 us
  starting transfers between devices: 16.7 us -> 18.6 us
    unnamed x23 -> x10, local copies, waits for them, and re-layouts: 14.7 us -> 0.02 us
    pallas_call x1, Pallas kernels: 8.72 us -> 11.9 us  [project(): pl.pallas_call(functools.partial(project_kernel, groups, n_qp, group, chu...]
    pallas_call x0 -> x1, Pallas kernels: none -> 2.46 us  [pack_own(): pl.pallas_call(pack_kernel, in_specs=[smem, smem, smem, vmem, vmem], out_...]
    pallas_call x1, Pallas kernels: 3.91 us -> 5.87 us  [arrange(): pl.pallas_call(arrange_kernel, in_specs=[vmem], out_specs=[smem, smem, vm...]
    all_gather x1, waiting for transfers between devices: 1.91 us -> 0.01 us  [local(): pack = lax.all_gather(pack, ('qp', 'fc'), axis=0)]
    all_to_all x2, starting transfers between devices: 8.8 us -> 10.7 us  [local(): lax.all_to_all(found.reshape(n_qp, own_pairs, found.shape[1], modes), 'qp...]
    pallas_call x2, Pallas kernels: 71.9 us -> 73.6 us  [coupling(): pl.pallas_call(functools.partial(coupling_kernel, share, block), in_specs...]
  transfers between devices with their start and end apart: 5 -> 5, of which waited for: 3 -> 2; matrix products, arithmetic and copies ran while one was open for 0% -> 1% of each run, Pallas kernels for 53% -> 59%
where the time goes in v5:
time: 154 us
  Pallas kernels  93.8 us (61%)
  waiting for transfers between devices  23.8 us (15%)
  starting transfers between devices  18.6 us (12%)
  between operations  14.1 us (9%)
  local copies, waits for them, and re-layouts  1.96 us (1%)
    pallas_call x2, Pallas kernels, coupling(): pl.pallas_call(functools.partial(coupling_kernel, share, block), in_specs...  73.6 us
    all_to_all x2, waiting for transfers between devices, local(): lax.all_to_all(x, ('mode', 'fc'), split_axis=0, concat_axis=0, tiled=True)  14.1 us
    pallas_call x1, Pallas kernels, project(): pl.pallas_call(functools.partial(project_kernel, groups, n_qp, group, chu...  11.9 us
    all_to_all x2, starting transfers between devices, local(): lax.all_to_all(found.reshape(n_qp, own_pairs, found.shape[1], modes), 'qp...  10.7 us
    all_to_all x2, waiting for transfers between devices, local(): lax.all_to_all(found.reshape(n_qp, own_pairs, found.shape[1], modes), 'qp...  9.67 us
    all_to_all x2, starting transfers between devices, local(): lax.all_to_all(x, ('mode', 'fc'), split_axis=0, concat_axis=0, tiled=True)  7.83 us
    pallas_call x1, Pallas kernels, arrange(): pl.pallas_call(arrange_kernel, in_specs=[vmem], out_specs=[smem, smem, vm...  5.87 us
  transfers between devices with their start and end apart: 5, of which 2 were waited for; matrix products, arithmetic and copies ran while one was open for 1% of the time, Pallas kernels for 59%

profile of v5, /device:TPU:0, one launch (start us, length us, event | category | flops | bytes accessed | tf_op | source)
XLA Modules:
  0.0 153.6 jit_solution(16214744731068267042)
XLA Ops:
  7.2 2.5 %pack_own.1 = bf16[3,352,128]{2,1,0:T(8,128)(2,1)} custom-call(s32[1]{0:T(128)} %bitcast.part_ref, s32[3]{0:T(128)} %partner_ref.1, s32[3]{0:T(128)} %weight_ref.1, bf16[3,288,288]{2,1,0:T(8,128)(2,1)} %grid_ref.1, bf16[3,288]{1,0:T(4,128)(2,1)} %freq_ref.1), custom_call_target="tpu_custom_call" | custom-call | tf_op jit(solution)/shard_map/pack_own/pallas_call | solution.py:181
  9.7 11.9 %project.1 = (bf16[4,7,72,256]{3,2,1,0:T(8,128)(2,1)}, bf16[4,14,72,256]{3,2,1,0:T(8,128)(2,1)}) custom-call(s32[1]{0:T(128)} %bitcast.7.here_ref, bf16[288,288]{1,0:T(8,128)(2,1)} %home_ref.1, bf16[288,20736]{1,0:T(8,128)(2,1)} %force_ref.1), custom_call_target="tpu_custom_call" | custom-call | tf_op jit(solution)/shard_map/project/pallas_call | solution.py:106
  21.6 4.2 %all-to-all-start = ((bf16[4,7,72,256]{3,2,1,0:T(8,128)(2,1)}), bf16[4,7,72,256]{3,2,1,0:T(8,128)(2,1)S(1)}, u32[]{:S(2)}, u32[]{:S(2)}) async-start(bf16[4,7,72,256]{3,2,1,0:T(8,128)(2,1)} %get-tuple-element.16), calls=%async_computation | async-start | bytes 2064384 | tf_op jit(solution)/shard_map/all_to_all | solution.py:607
  25.8 0.1 reshape.72
  25.9 0.1 dynamic_slice.3
  26.0 14.1 %all-to-all-done.moved_ref = bf16[4,7,72,256]{3,2,1,0:T(8,128)(2,1)S(1)} async-done(((bf16[4,7,72,256]{3,2,1,0:T(8,128)(2,1)}), bf16[4,7,72,256]{3,2,1,0:T(8,128)(2,1)S(1)}, u32[]{:S(2)}, u32[]{:S(2)}) %all-to-all-start) | async-done | bytes 1032224 | tf_op jit(solution)/shard_map/all_to_all | solution.py:607
  40.1 3.6 %all-to-all-start.2 = ((bf16[4,14,72,256]{3,2,1,0:T(8,128)(2,1)}), bf16[4,14,72,256]{3,2,1,0:T(8,128)(2,1)S(1)}, u32[]{:S(2)}, u32[]{:S(2)}) async-start(bf16[4,14,72,256]{3,2,1,0:T(8,128)(2,1)} %get-tuple-element.17), calls=%async_computation.2 | async-start | bytes 4128768 | tf_op jit(solution)/shard_map/all_to_all | solution.py:607
  43.8 0.1 broadcast_in_dim.13
  43.8 0.1 reshape.66
  43.9 0.1 slice_bitcast_fusion.home_ref
  44.0 0.1 broadcast_in_dim.15
  44.1 0.1 stack.29
  44.2 0.6 pad_maximum_fusion.1.home_row_ref
  44.8 0.6 pad_maximum_fusion.home_row_ref
  45.4 5.9 %arrange.1 = (s32[12]{0:T(128)}, f32[12]{0:T(128)}, bf16[12,288,256]{2,1,0:T(8,128)(2,1)}, bf16[12,288,288]{2,1,0:T(8,128)(2,1)}, f32[12,1,384]{2,1,0:T(1,128)}, /*index=5*/f32[288,128]{1,0:T(8,128)}) custom-call(bf16[4,2,3,352,128]{4,3,2,1,0:T(8,128)(2,1)} %bitcast.21), custom_call_target="tpu_custom_call" | custom-call | tf_op jit(solution)/shard_map/arrange/pallas_call | solution.py:247
  51.3 28.2 %coupling.2 = f32[12,8,288]{2,1,0:T(8,128)} custom-call(s32[12]{0:T(128)} %get-tuple-element.10.partner_ref, f32[12]{0:T(128)} %get-tuple-element.11.weight_ref, f32[6]{0:T(128)} %copy-done.4, bf16[12,288,256]{2,1,0:T(8,128)(2,1)} %get-tuple-element.12.grid_ref, bf16[12,288,288]{2,1,0:T(8,128)(2,1)} %get-tuple-element.13.grid_t_ref, ...), custom_call_target="tpu_custom_call" | custom-call | flops 6879707136 | bytes 3981312 | tf_op jit(solution)/shard_map/coupling/pallas_call | solution.py:563
  79.5 5.6 %all-to-all-start.1 = ((f32[4,3,8,288]{3,2,1,0:T(8,128)}), f32[4,3,8,288]{3,2,1,0:T(8,128)S(1)}, u32[]{:S(2)}, u32[]{:S(2)}) async-start(f32[4,3,8,288]{3,2,1,0:T(8,128)} %bitcast.25), calls=%async_computation.1 | async-start | bytes 294912 | tf_op jit(solution)/shard_map/all_to_all | solution.py:621
  85.1 45.4 %coupling.3 = f32[12,16,288]{2,1,0:T(8,128)} custom-call(s32[12]{0:T(128)} %get-tuple-element.10.partner_ref, f32[12]{0:T(128)} %get-tuple-element.11.weight_ref, f32[12]{0:T(128)} %copy-done.3, bf16[12,288,256]{2,1,0:T(8,128)(2,1)} %get-tuple-element.12.grid_ref, bf16[12,288,288]{2,1,0:T(8,128)(2,1)} %get-tuple-element.13.grid_t_ref, ...), custom_call_target="tpu_custom_call" | custom-call | flops 13759414272 | bytes 7962624 | tf_op jit(solution)/shard_map/coupling/pallas_call | solution.py:563
  130.5 5.1 %all-to-all-start.3 = ((f32[4,3,16,288]{3,2,1,0:T(8,128)}), f32[4,3,16,288]{3,2,1,0:T(8,128)S(1)}, u32[]{:S(2)}, u32[]{:S(2)}) async-start(f32[4,3,16,288]{3,2,1,0:T(8,128)} %bitcast.24), calls=%async_computation.3 | async-start | bytes 589824 | tf_op jit(solution)/shard_map/all_to_all | solution.py:621
  135.6 9.7 %all-to-all-done.3 = f32[4,3,16,288]{3,2,1,0:T(8,128)S(1)} async-done(((f32[4,3,16,288]{3,2,1,0:T(8,128)}), f32[4,3,16,288]{3,2,1,0:T(8,128)S(1)}, u32[]{:S(2)}, u32[]{:S(2)}) %all-to-all-start.3) | async-done | bytes 221216 | tf_op jit(solution)/shard_map/all_to_all | solution.py:621
  145.2 0.1 maximum_bitcast_fusion
  145.3 0.8 reshape.70
  146.1 0.1 pad_maximum_fusion.2
  146.2 0.6 reshape.69
  (21 shorter events, 0.1 us)
Async XLA Ops:
  7.2 38.2 %all-gather.3.cloned.1.call-start = ((), (), s32[]{:S(2)}) async-start(), calls=%async_computation.4 | async-start | bytes 2433024 | tf_op jit(solution)/shard_map/all_gather | solution.py:600
  9.7 16.1 %copy-start.2 = (bf16[288]{0:T(512)(128)(2,1)S(1)}, bf16[288]{0:T(512)(128)(2,1)}, u32[]{:S(2)}) copy-start(bf16[288]{0:T(512)(128)(2,1)} %param.8) | copy-start | bytes 1732
  21.6 18.5 %all-to-all-start = ((bf16[4,7,72,256]{3,2,1,0:T(8,128)(2,1)}), bf16[4,7,72,256]{3,2,1,0:T(8,128)(2,1)S(1)}, u32[]{:S(2)}, u32[]{:S(2)}) async-start(bf16[4,7,72,256]{3,2,1,0:T(8,128)(2,1)} %get-tuple-element.16), calls=%async_computation | async-start | bytes 2064384 | tf_op jit(solution)/shard_map/all_to_all | solution.py:607
  40.1 11.1 %copy-start.1 = (bf16[4,7,72,256]{3,2,1,0:T(8,128)(2,1)}, bf16[4,7,72,256]{3,2,1,0:T(8,128)(2,1)S(1)}, u32[]{:S(2)}) copy-start(bf16[4,7,72,256]{3,2,1,0:T(8,128)(2,1)S(1)} %all-to-all-done.moved_ref) | copy-start | bytes 3096580
  40.1 39.4 %all-to-all-start.2 = ((bf16[4,14,72,256]{3,2,1,0:T(8,128)(2,1)}), bf16[4,14,72,256]{3,2,1,0:T(8,128)(2,1)S(1)}, u32[]{:S(2)}, u32[]{:S(2)}) async-start(bf16[4,14,72,256]{3,2,1,0:T(8,128)(2,1)} %get-tuple-element.17), calls=%async_computation.2 | async-start | bytes 4128768 | tf_op jit(solution)/shard_map/all_to_all | solution.py:607
  43.8 7.5 %copy-start.4 = (f32[6]{0:T(128)}, f32[6]{0:T(128)S(1)}, u32[]{:S(2)}) copy-start(f32[6]{0:T(128)S(1)} %slice_bitcast_fusion.1.home_ref) | copy-start | bytes 76
  44.0 35.5 %copy-start.3 = (f32[12]{0:T(128)}, f32[12]{0:T(128)S(1)}, u32[]{:S(2)}) copy-start(f32[12]{0:T(128)S(1)} %slice_bitcast_fusion.home_ref) | copy-start | bytes 148
  79.5 5.6 %copy-start = (bf16[4,14,72,256]{3,2,1,0:T(8,128)(2,1)}, bf16[4,14,72,256]{3,2,1,0:T(8,128)(2,1)S(1)}, u32[]{:S(2)}) copy-start(bf16[4,14,72,256]{3,2,1,0:T(8,128)(2,1)S(1)} %all-to-all-done.2.moved_ref) | copy-start | bytes 6193156
  79.5 51.0 %all-to-all-start.1 = ((f32[4,3,8,288]{3,2,1,0:T(8,128)}), f32[4,3,8,288]{3,2,1,0:T(8,128)S(1)}, u32[]{:S(2)}, u32[]{:S(2)}) async-start(f32[4,3,8,288]{3,2,1,0:T(8,128)} %bitcast.25), calls=%async_computation.1 | async-start | bytes 294912 | tf_op jit(solution)/shard_map/all_to_all | solution.py:621
  130.5 14.8 %all-to-all-start.3 = ((f32[4,3,16,288]{3,2,1,0:T(8,128)}), f32[4,3,16,288]{3,2,1,0:T(8,128)S(1)}, u32[]{:S(2)}, u32[]{:S(2)}) async-start(f32[4,3,16,288]{3,2,1,0:T(8,128)} %bitcast.24), calls=%async_computation.3 | async-start | bytes 589824 | tf_op jit(solution)/shard_map/all_to_all | solution.py:621
Sparse Core Ops, SparseCore 0:
  10.2 32.3 all-gather.2

commit v6 on v5

--- a/solution.py
+++ b/solution.py
@@ -211,12 +211,14 @@
             for part in range(parts):
                 grid_ref[x, :, part * TILE : (part + 1) * TILE] = pack_ref[q, part, s, :modes, :]
                 for h in range(3):
-                    start, width = modes + h * lines, min(TILE, modes - h * TILE)
-                    piece = pack_ref[q, part, s, start : start + lines, :]
+                    start = modes + h * lines
                     grid_t_ref[
-                        x, MAIN + part * lines : MAIN + (part + 1) * lines, h * TILE : h * TILE + width
-                    ] = piece[:, :width]
-            grid_t_ref[x, :MAIN, :] = dot_nt(eye, grid_ref[x]).astype(BF16)
+                        x,
+                        MAIN + part * lines : MAIN + (part + 1) * lines,
+                        h * TILE : (h + 1) * TILE,
+                    ] = pack_ref[q, part, s, start : start + lines, :]
+            grid_t_ref[x, :MAIN, MAIN:] = jnp.zeros((MAIN, TILE), BF16)
+            grid_t_ref[x, :MAIN, :modes] = dot_nt(eye, grid_ref[x]).astype(BF16)
             side = pack_ref[q, 0, s, modes + 3 * lines : modes + 3 * lines + 16, :]
             wide = side.astype(F32)
             freq_row_ref[x, :, :TILE] = wide[0:1]
@@ -252,7 +254,7 @@
             jax.ShapeDtypeStruct((pairs,), jnp.int32),
             jax.ShapeDtypeStruct((pairs,), F32),
             jax.ShapeDtypeStruct((pairs, modes, MAIN), BF16),
-            jax.ShapeDtypeStruct((pairs, modes, modes), BF16),
+            jax.ShapeDtypeStruct((pairs, modes, MAIN + TILE), BF16),
             jax.ShapeDtypeStruct((pairs, 1, MAIN + TILE), F32),
             jax.ShapeDtypeStruct((modes, TILE), F32),
         ],
@@ -292,23 +294,26 @@
     inner_rest_ref,
     pick_ref,
     rest_value_ref,
+    force_rest_ref,
     *work,
 ):
-    gathers, inners, values, tabs, sums, rest_sums, firsts = (
-        work[2 * i : 2 * i + 2] for i in range(7)
+    gathers, inners, lefts, wides, values, tabs, sums, rest_sums, firsts = (
+        work[2 * i : 2 * i + 2] for i in range(9)
     )
     pairs = grid_ref.shape[0]
     modes = grid_ref.shape[1]
     rest = modes - MAIN
     sources, depth = moved_ref.shape[0], moved_ref.shape[2]
     per_slot = MAIN // rest
+    per_tile = TILE // rest
     rest_lanes = home_row_ref.shape[1]
     s2 = smearing * smearing
     steps = share // block
 
     for x in range(pairs):
-        grid_rest_ref[x * rest : (x + 1) * rest, :] = grid_t_ref[x, MAIN:, :]
+        grid_rest_ref[x * rest : (x + 1) * rest, :] = grid_t_ref[x, MAIN:, :modes]
     eye = identity(modes)
+    force_rest_ref[...] = jnp.zeros_like(force_rest_ref)
     if share * rest < rest_lanes:
         inner_rest_ref[...] = jnp.zeros_like(inner_rest_ref)
     for r in range(share):
@@ -322,7 +327,9 @@
                 tail = pltpu.roll(tail, TILE - spot * rest, 1)
             gather_ref[s * depth : (s + 1) * depth, MAIN:] = tail[:, :rest]
         whole = gather_ref[...].astype(BF16)
-        turned_ref[r * modes : (r + 1) * modes, :] = dot_nt(eye, whole).astype(BF16)
+        turned_ref[r * modes : (r + 1) * modes, :] = dot_nt(eye, whole[:MAIN]).astype(BF16)
+        line = (r // block * per_tile + r % block) * rest
+        force_rest_ref[line : line + rest, :] = whole[MAIN:]
         found = dot_nn(grid_rest_ref[...], whole).astype(BF16)
         for x in range(pairs):
             inner_rest_ref[x, r * rest : (r + 1) * rest, :] = found[x * rest : (x + 1) * rest, :]
@@ -330,21 +337,38 @@
     row_id = lax.broadcasted_iota(jnp.int32, pick_ref.shape, 0)
     col_id = lax.broadcasted_iota(jnp.int32, pick_ref.shape, 1)
     pick_ref[...] = (row_id // rest == col_id).astype(BF16)
-    for ref in (out_ref, *sums, *rest_sums, *firsts):
+    for ref in (out_ref, *inners, *sums, *rest_sums, *firsts):
         ref[...] = jnp.zeros_like(ref)
+
+    def contract_wide(x, into):
+        def task():
+            left = grid_t_ref[partner_ref[x], :, :modes]
+            into[...] = dot_nt(left, force_rest_ref[...]).astype(BF16)
+
+        return task
 
     def contract_first(x, r, b, into):
         def task():
-            found = dot_nn(turned_ref[r * modes : (r + 1) * modes, :], grid_ref[x])
-            into[:, b * MAIN : (b + 1) * MAIN] = found.astype(BF16)
+            lanes = slice(b * MAIN, (b + 1) * MAIN)
+            found = dot_nn(turned_ref[r * modes : (r + 1) * modes, :], grid_ref[x, :MAIN, :])
+            into[:modes, lanes] = found.astype(BF16)
+            start = MAIN + TILE + b * rest
+            into[start : start + rest, lanes] = grid_ref[x, MAIN:, :]
 
         return task
 
-    def contract_second(x, b, source, into):
+    def prepare_second(x, step, wide, left):
+        def task():
+            left[:, : MAIN + TILE] = grid_t_ref[partner_ref[x]]
+            left[:, MAIN + TILE :] = wide[:, step * TILE : (step + 1) * TILE]
+
+        return task
+
+    def contract_second(b, left, source, into):
         lanes = slice(b * MAIN, (b + 1) * MAIN)
 
         def task():
-            into[:, lanes] = dot_nn(grid_t_ref[partner_ref[x]], source[:, lanes])
+            into[:, lanes] = dot_nn(left[...], source[:, lanes])
 
         return task
 
@@ -391,7 +415,9 @@
 
     def contract_rest(x):
         def task():
-            rest_value_ref[...] = dot_nt(grid_t_ref[partner_ref[x]], inner_rest_ref[x])
+            rest_value_ref[...] = dot_nt(
+                grid_t_ref[partner_ref[x], :, :modes], inner_rest_ref[x]
+            )
 
         return task
 
@@ -477,8 +503,10 @@
         for b in range(block):
             x, step = jnp.int32(g // steps), g % steps
             contract_first(x, step * block + b, b, inners[g])()
+    contract_wide(jnp.int32(0), wides[0])()
+    prepare_second(jnp.int32(0), 0, wides[0], lefts[0])()
     for b in range(block):
-        contract_second(jnp.int32(0), b, inners[0], values[0])()
+        contract_second(b, lefts[0], inners[0], values[0])()
 
     def two_pairs(i, carry):
         for e in range(2):
@@ -496,9 +524,13 @@
             for s in range(steps):
                 g = e * steps + s
                 heavy = []
+                if s == 0:
+                    contract_wide(jnp.minimum(x + 1, pairs - 1), wides[1 - e])()
+                x1, step1 = later(g + 1)
+                odd = (g + 1) % 2
+                prepare_second(x1, step1, wides[(g + 1) // steps % 2], lefts[odd])()
                 for b in range(block):
-                    x1, _ = later(g + 1)
-                    heavy.append(contract_second(x1, b, inners[(g + 1) % 2], values[(g + 1) % 2]))
+                    heavy.append(contract_second(b, lefts[odd], inners[odd], values[odd]))
                 for b in range(block):
                     x2, step2 = later(g + 2)
                     heavy.append(contract_first(x2, step2 * block + b, b, inners[g % 2]))
@@ -546,14 +578,17 @@
     assert pairs % 2 == 0
     scratch = (
         [
-            pltpu.VMEM((share * modes, modes), BF16),
+            pltpu.VMEM((share * modes, MAIN), BF16),
             pltpu.VMEM((pairs * rest, modes), BF16),
             pltpu.VMEM((pairs, rest_lanes, modes), BF16),
             pltpu.VMEM((rest_lanes, TILE), BF16),
             pltpu.VMEM((modes, rest_lanes), F32),
+            pltpu.VMEM((share // block * TILE, modes), BF16),
         ]
         + [pltpu.VMEM((modes, modes), F32)] * 2
-        + [pltpu.VMEM((modes, block * MAIN), BF16)] * 2
+        + [pltpu.VMEM((2 * MAIN, block * MAIN), BF16)] * 2
+        + [pltpu.VMEM((modes, 2 * MAIN), BF16)] * 2
+        + [pltpu.VMEM((modes, share // block * TILE), BF16)] * 2
         + [pltpu.VMEM((modes, block * MAIN), F32)] * 2
         + [pltpu.VMEM((4, modes, MAIN + TILE), F32)] * 2
         + [pltpu.VMEM((modes, TILE), F32)] * 2

time: 154 us -> 154 us (level)
  no operation moved by 1% of the time
where the time goes in v6:
time: 154 us; the launch traced here: 153 us
  Pallas kernels  93.5 us (61%)
  waiting for transfers between devices  23.8 us (15%)
  starting transfers between devices  18.6 us (12%)
  between operations  14.1 us (9%)
  local copies, waits for them, and re-layouts  1.96 us (1%)
    pallas_call x2, Pallas kernels, coupling(): pl.pallas_call(functools.partial(coupling_kernel, share, block), in_specs...  73.3 us
    all_to_all x2, waiting for transfers between devices, local(): lax.all_to_all(x, ('mode', 'fc'), split_axis=0, concat_axis=0, tiled=True)  14.1 us
    pallas_call x1, Pallas kernels, project(): pl.pallas_call(functools.partial(project_kernel, groups, n_qp, group, chu...  11.9 us
    all_to_all x2, starting transfers between devices, local(): lax.all_to_all(found.reshape(n_qp, own_pairs, found.shape[1], modes), 'qp...  10.7 us
    all_to_all x2, waiting for transfers between devices, local(): lax.all_to_all(found.reshape(n_qp, own_pairs, found.shape[1], modes), 'qp...  9.7 us
    all_to_all x2, starting transfers between devices, local(): lax.all_to_all(x, ('mode', 'fc'), split_axis=0, concat_axis=0, tiled=True)  7.83 us
    pallas_call x1, Pallas kernels, arrange(): pl.pallas_call(arrange_kernel, in_specs=[vmem], out_specs=[smem, smem, vm...  5.88 us
  transfers between devices with their start and end apart: 5, of which 2 were waited for; matrix products, arithmetic and copies ran while one was open for 1% of the time, Pallas kernels for 59%

profile of v6, /device:TPU:0, one launch (start us, length us, event | category | flops | bytes accessed | tf_op | source)
XLA Modules:
  0.0 153.3 jit_solution(9063799976601403923)
XLA Ops:
  7.2 2.5 %pack_own.1 = bf16[3,352,128]{2,1,0:T(8,128)(2,1)} custom-call(s32[1]{0:T(128)} %bitcast.part_ref, s32[3]{0:T(128)} %partner_ref.1, s32[3]{0:T(128)} %weight_ref.1, bf16[3,288,288]{2,1,0:T(8,128)(2,1)} %grid_ref.1, bf16[3,288]{1,0:T(4,128)(2,1)} %freq_ref.1), custom_call_target="tpu_custom_call" | custom-call | tf_op jit(solution)/shard_map/pack_own/pallas_call | solution.py:181
  9.7 11.9 %project.1 = (bf16[4,7,72,256]{3,2,1,0:T(8,128)(2,1)}, bf16[4,14,72,256]{3,2,1,0:T(8,128)(2,1)}) custom-call(s32[1]{0:T(128)} %bitcast.7.here_ref, bf16[288,288]{1,0:T(8,128)(2,1)} %home_ref.1, bf16[288,20736]{1,0:T(8,128)(2,1)} %force_ref.1), custom_call_target="tpu_custom_call" | custom-call | tf_op jit(solution)/shard_map/project/pallas_call | solution.py:106
  21.6 4.2 %all-to-all-start = ((bf16[4,7,72,256]{3,2,1,0:T(8,128)(2,1)}), bf16[4,7,72,256]{3,2,1,0:T(8,128)(2,1)S(1)}, u32[]{:S(2)}, u32[]{:S(2)}) async-start(bf16[4,7,72,256]{3,2,1,0:T(8,128)(2,1)} %get-tuple-element.16), calls=%async_computation | async-start | bytes 2064384 | tf_op jit(solution)/shard_map/all_to_all | solution.py:642
  25.8 0.1 reshape.72
  25.9 0.1 dynamic_slice.3
  26.0 14.1 %all-to-all-done.moved_ref = bf16[4,7,72,256]{3,2,1,0:T(8,128)(2,1)S(1)} async-done(((bf16[4,7,72,256]{3,2,1,0:T(8,128)(2,1)}), bf16[4,7,72,256]{3,2,1,0:T(8,128)(2,1)S(1)}, u32[]{:S(2)}, u32[]{:S(2)}) %all-to-all-start) | async-done | bytes 1032224 | tf_op jit(solution)/shard_map/all_to_all | solution.py:642
  40.1 3.6 %all-to-all-start.2 = ((bf16[4,14,72,256]{3,2,1,0:T(8,128)(2,1)}), bf16[4,14,72,256]{3,2,1,0:T(8,128)(2,1)S(1)}, u32[]{:S(2)}, u32[]{:S(2)}) async-start(bf16[4,14,72,256]{3,2,1,0:T(8,128)(2,1)} %get-tuple-element.17), calls=%async_computation.2 | async-start | bytes 4128768 | tf_op jit(solution)/shard_map/all_to_all | solution.py:642
  43.8 0.1 broadcast_in_dim.13
  43.8 0.1 reshape.66
  43.9 0.1 slice_bitcast_fusion.home_ref
  44.0 0.1 broadcast_in_dim.15
  44.1 0.1 stack.29
  44.2 0.6 pad_maximum_fusion.1.home_row_ref
  44.8 0.6 pad_maximum_fusion.home_row_ref
  45.4 5.9 %arrange.1 = (s32[12]{0:T(128)}, f32[12]{0:T(128)}, bf16[12,288,256]{2,1,0:T(8,128)(2,1)}, bf16[12,288,384]{2,1,0:T(8,128)(2,1)}, f32[12,1,384]{2,1,0:T(1,128)}, /*index=5*/f32[288,128]{1,0:T(8,128)}) custom-call(bf16[4,2,3,352,128]{4,3,2,1,0:T(8,128)(2,1)} %bitcast.21), custom_call_target="tpu_custom_call" | custom-call | tf_op jit(solution)/shard_map/arrange/pallas_call | solution.py:249
  51.3 27.7 %coupling.2 = f32[12,8,288]{2,1,0:T(8,128)} custom-call(s32[12]{0:T(128)} %get-tuple-element.10.partner_ref, f32[12]{0:T(128)} %get-tuple-element.11.weight_ref, f32[6]{0:T(128)} %copy-done.4, bf16[12,288,256]{2,1,0:T(8,128)(2,1)} %get-tuple-element.12.grid_ref, bf16[12,288,384]{2,1,0:T(8,128)(2,1)} %get-tuple-element.13.grid_t_ref, ...), custom_call_target="tpu_custom_call" | custom-call | flops 6879707136 | bytes 3981312 | tf_op jit(solution)/shard_map/coupling/pallas_call | solution.py:598
  79.0 5.6 %all-to-all-start.1 = ((f32[4,3,8,288]{3,2,1,0:T(8,128)}), f32[4,3,8,288]{3,2,1,0:T(8,128)S(1)}, u32[]{:S(2)}, u32[]{:S(2)}) async-start(f32[4,3,8,288]{3,2,1,0:T(8,128)} %bitcast.25), calls=%async_computation.1 | async-start | bytes 294912 | tf_op jit(solution)/shard_map/all_to_all | solution.py:656
  84.6 45.5 %coupling.3 = f32[12,16,288]{2,1,0:T(8,128)} custom-call(s32[12]{0:T(128)} %get-tuple-element.10.partner_ref, f32[12]{0:T(128)} %get-tuple-element.11.weight_ref, f32[12]{0:T(128)} %copy-done.3, bf16[12,288,256]{2,1,0:T(8,128)(2,1)} %get-tuple-element.12.grid_ref, bf16[12,288,384]{2,1,0:T(8,128)(2,1)} %get-tuple-element.13.grid_t_ref, ...), custom_call_target="tpu_custom_call" | custom-call | flops 13759414272 | bytes 7962624 | tf_op jit(solution)/shard_map/coupling/pallas_call | solution.py:598
  130.2 5.1 %all-to-all-start.3 = ((f32[4,3,16,288]{3,2,1,0:T(8,128)}), f32[4,3,16,288]{3,2,1,0:T(8,128)S(1)}, u32[]{:S(2)}, u32[]{:S(2)}) async-start(f32[4,3,16,288]{3,2,1,0:T(8,128)} %bitcast.24), calls=%async_computation.3 | async-start | bytes 589824 | tf_op jit(solution)/shard_map/all_to_all | solution.py:656
  135.3 9.7 %all-to-all-done.3 = f32[4,3,16,288]{3,2,1,0:T(8,128)S(1)} async-done(((f32[4,3,16,288]{3,2,1,0:T(8,128)}), f32[4,3,16,288]{3,2,1,0:T(8,128)S(1)}, u32[]{:S(2)}, u32[]{:S(2)}) %all-to-all-start.3) | async-done | bytes 221216 | tf_op jit(solution)/shard_map/all_to_all | solution.py:656
  145.0 0.1 maximum_bitcast_fusion
  145.1 0.8 reshape.70
  145.8 0.1 pad_maximum_fusion.2
  145.9 0.6 reshape.69
  (21 shorter events, 0.1 us)
Async XLA Ops:
  7.2 38.2 %all-gather.3.cloned.1.call-start = ((), (), s32[]{:S(2)}) async-start(), calls=%async_computation.4 | async-start | bytes 2433024 | tf_op jit(solution)/shard_map/all_gather | solution.py:635
  9.7 16.1 %copy-start.2 = (bf16[288]{0:T(512)(128)(2,1)S(1)}, bf16[288]{0:T(512)(128)(2,1)}, u32[]{:S(2)}) copy-start(bf16[288]{0:T(512)(128)(2,1)} %param.8) | copy-start | bytes 1732
  21.6 18.5 %all-to-all-start = ((bf16[4,7,72,256]{3,2,1,0:T(8,128)(2,1)}), bf16[4,7,72,256]{3,2,1,0:T(8,128)(2,1)S(1)}, u32[]{:S(2)}, u32[]{:S(2)}) async-start(bf16[4,7,72,256]{3,2,1,0:T(8,128)(2,1)} %get-tuple-element.16), calls=%async_computation | async-start | bytes 2064384 | tf_op jit(solution)/shard_map/all_to_all | solution.py:642
  40.1 11.1 %copy-start.1 = (bf16[4,7,72,256]{3,2,1,0:T(8,128)(2,1)}, bf16[4,7,72,256]{3,2,1,0:T(8,128)(2,1)S(1)}, u32[]{:S(2)}) copy-start(bf16[4,7,72,256]{3,2,1,0:T(8,128)(2,1)S(1)} %all-to-all-done.moved_ref) | copy-start | bytes 3096580
  40.1 38.9 %all-to-all-start.2 = ((bf16[4,14,72,256]{3,2,1,0:T(8,128)(2,1)}), bf16[4,14,72,256]{3,2,1,0:T(8,128)(2,1)S(1)}, u32[]{:S(2)}, u32[]{:S(2)}) async-start(bf16[4,14,72,256]{3,2,1,0:T(8,128)(2,1)} %get-tuple-element.17), calls=%async_computation.2 | async-start | bytes 4128768 | tf_op jit(solution)/shard_map/all_to_all | solution.py:642
  43.8 7.5 %copy-start.4 = (f32[6]{0:T(128)}, f32[6]{0:T(128)S(1)}, u32[]{:S(2)}) copy-start(f32[6]{0:T(128)S(1)} %slice_bitcast_fusion.1.home_ref) | copy-start | bytes 76
  44.0 35.0 %copy-start.3 = (f32[12]{0:T(128)}, f32[12]{0:T(128)S(1)}, u32[]{:S(2)}) copy-start(f32[12]{0:T(128)S(1)} %slice_bitcast_fusion.home_ref) | copy-start | bytes 148
  79.0 5.6 %copy-start = (bf16[4,14,72,256]{3,2,1,0:T(8,128)(2,1)}, bf16[4,14,72,256]{3,2,1,0:T(8,128)(2,1)S(1)}, u32[]{:S(2)}) copy-start(bf16[4,14,72,256]{3,2,1,0:T(8,128)(2,1)S(1)} %all-to-all-done.2.moved_ref) | copy-start | bytes 6193156
  79.0 51.2 %all-to-all-start.1 = ((f32[4,3,8,288]{3,2,1,0:T(8,128)}), f32[4,3,8,288]{3,2,1,0:T(8,128)S(1)}, u32[]{:S(2)}, u32[]{:S(2)}) async-start(f32[4,3,8,288]{3,2,1,0:T(8,128)} %bitcast.25), calls=%async_computation.1 | async-start | bytes 294912 | tf_op jit(solution)/shard_map/all_to_all | solution.py:656
  130.2 14.8 %all-to-all-start.3 = ((f32[4,3,16,288]{3,2,1,0:T(8,128)}), f32[4,3,16,288]{3,2,1,0:T(8,128)S(1)}, u32[]{:S(2)}, u32[]{:S(2)}) async-start(f32[4,3,16,288]{3,2,1,0:T(8,128)} %bitcast.24), calls=%async_computation.3 | async-start | bytes 589824 | tf_op jit(solution)/shard_map/all_to_all | solution.py:656
Sparse Core Ops, SparseCore 0:
  10.2 32.3 all-gather.2

commit v7 on v5

--- a/solution.py
+++ b/solution.py
@@ -236,7 +236,7 @@
                 ref[x] = found.astype(ref.dtype)
         return carry
 
-    lax.fori_loop(0, owners, one, 0)
+    lax.fori_loop(0, owners, one, 0, unroll=owners <= 4)
 
 
 def arrange(pack, modes):
@@ -277,6 +277,7 @@
 def coupling_kernel(
     share,
     block,
+    behind,
     partner_ref,
     weight_ref,
     home_ref,
@@ -286,14 +287,18 @@
     freq_col_ref,
     home_row_ref,
     moved_ref,
-    out_ref,
-    turned_ref,
-    grid_rest_ref,
-    inner_rest_ref,
-    pick_ref,
-    rest_value_ref,
-    *work,
+    *refs,
 ):
+    earlier_ref = refs[0] if behind else None
+    (
+        out_ref,
+        turned_ref,
+        grid_rest_ref,
+        inner_rest_ref,
+        pick_ref,
+        rest_value_ref,
+        *work,
+    ) = refs[1:] if behind else refs
     gathers, inners, values, tabs, sums, rest_sums, firsts = (
         work[2 * i : 2 * i + 2] for i in range(7)
     )
@@ -349,13 +354,12 @@
         return task
 
     def line_shapes(v, t, w, c1, c2):
-        p = v * v
         d = t[0] - w
         e = t[1] - c1
-        return (
-            (p * t[2]) * pl.reciprocal(d * d + s2, approx=True),
-            (p * t[3]) * pl.reciprocal(e * e + c2, approx=True),
-        )
+        d = d * d + s2
+        e = e * e + c2
+        p = (v * v) * pl.reciprocal(d * e, approx=True)
+        return (t[2] * e) * p, (t[3] * d) * p
 
     def weigh(step, source, tab, sum_ref, first_ref):
         state = {}
@@ -515,6 +519,13 @@
     collect(sums[1], rest_sums[1], last)()
     deliver(pairs - 1, partner_ref[pairs - 1], last, firsts[1])
 
+    if behind is None:
+        return
+    row = share
+    if behind:
+        place = ceil_div(share, 8) * 8
+        out_ref[:, place:, :] = earlier_ref[...]
+        row = place + behind
     totals = jnp.zeros(out_ref.shape[1:], F32)
     for y in range(pairs):
         totals = totals + out_ref[y]
@@ -525,12 +536,10 @@
         widths,
         0.0,
     )
-    out_ref[:, share, :] = jnp.broadcast_to(
-        jnp.sum(spread, axis=0, keepdims=True), (pairs, modes)
-    )
-
-
-def coupling(partner, weights, home, grid, grid_t, freq_rows, freq_cols, moved):
+    out_ref[:, row, :] = jnp.broadcast_to(jnp.sum(spread, axis=0, keepdims=True), (pairs, modes))
+
+
+def coupling(behind, partner, weights, home, grid, grid_t, freq_rows, freq_cols, moved, *earlier):
     pairs, modes = grid.shape[0], grid.shape[1]
     share = home.shape[0]
     rest = modes - MAIN
@@ -540,6 +549,8 @@
     s2 = smearing * smearing
     home_row = jnp.stack([row, row * row - s2, (4.0 * s2) * (row * row), 1.0 / row])
     padded = (share // 8 + 1) * 8
+    if behind:
+        padded = ceil_div(share, 8) * 8 + earlier[0].shape[1]
     smem = pl.BlockSpec(memory_space=pltpu.SMEM)
     vmem = pl.BlockSpec(memory_space=pltpu.VMEM)
     block = 3 if share % 3 == 0 else 1
@@ -561,8 +572,8 @@
         + [pltpu.VMEM((padded, modes), F32)] * 2
     )
     return pl.pallas_call(
-        functools.partial(coupling_kernel, share, block),
-        in_specs=[smem, smem, smem, vmem, vmem, vmem, vmem, vmem, vmem],
+        functools.partial(coupling_kernel, share, block, behind),
+        in_specs=[smem] * 3 + [vmem] * (6 + len(earlier)),
         out_specs=vmem,
         out_shape=jax.ShapeDtypeStruct((pairs, padded, modes), F32),
         scratch_shapes=scratch,
@@ -573,7 +584,7 @@
             transcendentals=2 * share * pairs * modes**2,
         ),
         name="coupling",
-    )(partner, weights, home, grid, grid_t, freq_rows, freq_cols, home_row, moved)
+    )(partner, weights, home, grid, grid_t, freq_rows, freq_cols, home_row, moved, *earlier)
 
 
 def local(
@@ -613,21 +624,30 @@
     home = lax.dynamic_slice(home, (own, here * share), (1, share)).reshape(share)
 
     shared = arrange(pack, modes)
-    parts, widths = [], []
-    for (first, count), block in zip(chunks, moved):
-        found = coupling(
-            shared[0], shared[1], home[first : first + count], *shared[2:], block
+    found = ()
+    for at, ((first, count), block) in enumerate(zip(chunks, moved)):
+        behind = None if at + 1 < len(chunks) else 0 if at == 0 else chunks[0][1]
+        found = (
+            coupling(
+                behind, shared[0], shared[1], home[first : first + count], *shared[2:], block, *found
+            ),
         )
-        back = lax.all_to_all(
-            found.reshape(n_qp, own_pairs, found.shape[1], modes),
-            "qp",
-            split_axis=0,
-            concat_axis=0,
-            tiled=True,
-        )
-        widths.append(back[:, 0, count, :count])
-        parts.append(back[:, :, :count, :])
-    widths = jnp.concatenate(widths, axis=1).reshape(n_qp * share)[:group]
+    padded = found[0].shape[1]
+    back = lax.all_to_all(
+        found[0].reshape(n_qp, own_pairs, padded, modes),
+        "qp",
+        split_axis=0,
+        concat_axis=0,
+        tiled=True,
+    )
+    last = chunks[-1][1]
+    places = [(0, last)]
+    if len(chunks) > 1:
+        places.insert(0, (ceil_div(last, 8) * 8, chunks[0][1]))
+    row = places[0][0] + places[0][1]
+    widths = jnp.concatenate([back[:, 0, row, a : a + c] for a, c in places], axis=1)
+    widths = widths.reshape(n_qp * share)[:group]
+    parts = [back[:, :, a : a + c, :] for a, c in places]
     collision = jnp.transpose(jnp.concatenate(parts, axis=2), (0, 2, 1, 3))
     collision = collision.reshape(n_qp * share, own_pairs, modes)[:group]
     return (widths, collision)

time: 154 us -> 158 us (1.026)
  blocking collectives: 0 us -> 18.9 us
  starting transfers between devices: 18.6 us -> 7.87 us
  waiting for transfers between devices: 23.8 us -> 14.1 us
  Pallas kernels: 93.8 us -> 97.6 us
    all_to_all x0 -> x1, blocking collectives: none -> 18.9 us  [local(): lax.all_to_all(found[0].reshape(n_qp, own_pairs, padded, modes), 'qp', sp...]
    all_to_all x2 -> x0, starting transfers between devices: 10.7 us -> none  [local(): lax.all_to_all(found.reshape(n_qp, own_pairs, found.shape[1], modes), 'qp...]
    all_to_all x2 -> x0, waiting for transfers between devices: 9.67 us -> none  [local(): lax.all_to_all(found.reshape(n_qp, own_pairs, found.shape[1], modes), 'qp...]
    pallas_call x2, Pallas kernels: 73.6 us -> 78.2 us  [coupling(): pl.pallas_call(functools.partial(coupling_kernel, share, block, behind),...]
  transfers between devices with their start and end apart: 5 -> 3, of which waited for: 2 -> 1; matrix products, arithmetic and copies ran while one was open for 1% -> 1% of each run, Pallas kernels for 59% -> 30%
where the time goes in v7:
time: 158 us; the launch traced here: 157 us
  Pallas kernels  97.6 us (62%)
  blocking collectives  18.9 us (12%)
  waiting for transfers between devices  14.1 us (9%)
  between operations  14.1 us (9%)
  starting transfers between devices  7.87 us (5%)
  local copies, waits for them, and re-layouts  3.37 us (2%)
    pallas_call x2, Pallas kernels, coupling(): pl.pallas_call(functools.partial(coupling_kernel, share, block, behind),...  78.2 us
    all_to_all x1, blocking collectives, local(): lax.all_to_all(found[0].reshape(n_qp, own_pairs, padded, modes), 'qp', sp...  18.9 us
    all_to_all x2, waiting for transfers between devices, local(): lax.all_to_all(x, ('mode', 'fc'), split_axis=0, concat_axis=0, tiled=True)  14.1 us
    pallas_call x1, Pallas kernels, project(): pl.pallas_call(functools.partial(project_kernel, groups, n_qp, group, chu...  11.9 us
    all_to_all x2, starting transfers between devices, local(): lax.all_to_all(x, ('mode', 'fc'), split_axis=0, concat_axis=0, tiled=True)  7.83 us
    pallas_call x1, Pallas kernels, arrange(): pl.pallas_call(arrange_kernel, in_specs=[vmem], out_specs=[smem, smem, vm...  5.05 us
  transfers between devices with their start and end apart: 3, of which 1 were waited for; matrix products, arithmetic and copies ran while one was open for 1% of the time, Pallas kernels for 30%

profile of v7, /device:TPU:0, one launch (start us, length us, event | category | flops | bytes accessed | tf_op | source)
XLA Modules:
  0.0 157.4 jit_solution(15933254114567606107)
XLA Ops:
  7.2 2.5 %pack_own.1 = bf16[3,352,128]{2,1,0:T(8,128)(2,1)} custom-call(s32[1]{0:T(128)} %bitcast.part_ref, s32[3]{0:T(128)} %partner_ref.1, s32[3]{0:T(128)} %weight_ref.1, bf16[3,288,288]{2,1,0:T(8,128)(2,1)} %grid_ref.1, bf16[3,288]{1,0:T(4,128)(2,1)} %freq_ref.1), custom_call_target="tpu_custom_call" | custom-call | tf_op jit(solution)/shard_map/pack_own/pallas_call | solution.py:181
  9.7 11.9 %project.1 = (bf16[4,7,72,256]{3,2,1,0:T(8,128)(2,1)}, bf16[4,14,72,256]{3,2,1,0:T(8,128)(2,1)}) custom-call(s32[1]{0:T(128)} %bitcast.3.here_ref, bf16[288,288]{1,0:T(8,128)(2,1)} %home_ref.1, bf16[288,20736]{1,0:T(8,128)(2,1)} %force_ref.1), custom_call_target="tpu_custom_call" | custom-call | tf_op jit(solution)/shard_map/project/pallas_call | solution.py:106
  21.6 4.2 %all-to-all-start.1 = ((bf16[4,7,72,256]{3,2,1,0:T(8,128)(2,1)}), bf16[4,7,72,256]{3,2,1,0:T(8,128)(2,1)S(1)}, u32[]{:S(2)}, u32[]{:S(2)}) async-start(bf16[4,7,72,256]{3,2,1,0:T(8,128)(2,1)} %get-tuple-element.17), calls=%async_computation.1 | async-start | bytes 2064384 | tf_op jit(solution)/shard_map/all_to_all | solution.py:618
  25.8 0.1 reshape.68
  25.9 0.1 dynamic_slice.3
  26.0 14.1 %all-to-all-done.1.moved_ref = bf16[4,7,72,256]{3,2,1,0:T(8,128)(2,1)S(1)} async-done(((bf16[4,7,72,256]{3,2,1,0:T(8,128)(2,1)}), bf16[4,7,72,256]{3,2,1,0:T(8,128)(2,1)S(1)}, u32[]{:S(2)}, u32[]{:S(2)}) %all-to-all-start.1) | async-done | bytes 1032224 | tf_op jit(solution)/shard_map/all_to_all | solution.py:618
  40.1 3.6 %all-to-all-start = ((bf16[4,14,72,256]{3,2,1,0:T(8,128)(2,1)}), bf16[4,14,72,256]{3,2,1,0:T(8,128)(2,1)S(1)}, u32[]{:S(2)}, u32[]{:S(2)}) async-start(bf16[4,14,72,256]{3,2,1,0:T(8,128)(2,1)} %get-tuple-element.16), calls=%async_computation | async-start | bytes 4128768 | tf_op jit(solution)/shard_map/all_to_all | solution.py:618
  43.7 0.1 broadcast_in_dim.15
  43.8 0.1 reshape.63
  43.9 0.1 slice_bitcast_fusion.1.home_ref
  44.0 0.1 broadcast_in_dim.13
  44.0 0.1 stack.24
  44.1 0.6 pad_maximum_fusion.1.home_row_ref
  44.8 0.6 pad_maximum_fusion.home_row_ref
  45.4 5.1 %arrange.1 = (s32[12]{0:T(128)}, f32[12]{0:T(128)}, bf16[12,288,256]{2,1,0:T(8,128)(2,1)}, bf16[12,288,288]{2,1,0:T(8,128)(2,1)}, f32[12,1,384]{2,1,0:T(1,128)}, /*index=5*/f32[288,128]{1,0:T(8,128)}) custom-call(bf16[4,2,3,352,128]{4,3,2,1,0:T(8,128)(2,1)} %bitcast.18), custom_call_target="tpu_custom_call" | custom-call | tf_op jit(solution)/shard_map/arrange/pallas_call | solution.py:247
  50.4 29.7 %coupling.2.refs_0_ = f32[12,8,288]{2,1,0:T(8,128)} custom-call(s32[12]{0:T(128)} %get-tuple-element.10.partner_ref, f32[12]{0:T(128)} %get-tuple-element.11.weight_ref, f32[6]{0:T(128)} %copy-done.4, bf16[12,288,256]{2,1,0:T(8,128)(2,1)} %get-tuple-element.12.grid_ref, bf16[12,288,288]{2,1,0:T(8,128)(2,1)} %get-tuple-element.13.grid_t_ref, ...), custom_call_target="tpu_custom_call" | custom-call | flops 6879707136 | bytes 3981312 | tf_op jit(solution)/shard_map/coupling/pallas_call | solution.py:574
  80.2 1.3 copy-done
  81.5 48.5 %coupling.3 = f32[12,24,288]{2,1,0:T(8,128)} custom-call(s32[12]{0:T(128)} %get-tuple-element.10.partner_ref, f32[12]{0:T(128)} %get-tuple-element.11.weight_ref, f32[12]{0:T(128)} %copy-done.3, bf16[12,288,256]{2,1,0:T(8,128)(2,1)} %get-tuple-element.12.grid_ref, bf16[12,288,288]{2,1,0:T(8,128)(2,1)} %get-tuple-element.13.grid_t_ref, ...), custom_call_target="tpu_custom_call" | custom-call | flops 13759414272 | bytes 7962624 | tf_op jit(solution)/shard_map/coupling/pallas_call | solution.py:574
  130.0 18.9 %all_to_all.15 = f32[4,3,24,288]{3,2,1,0:T(8,128)S(1)} all-to-all(f32[4,3,24,288]{3,2,1,0:T(8,128)} %bitcast.19), channel_id=1, replica_groups=mesh['grp'=2,'qp'=4,'mode'=2,'fc'=2] {'qp'}, dimensions={0} | all-to-all | bytes 663552 | tf_op jit(solution)/shard_map/all_to_all | solution.py:636
  148.9 0.1 maximum_bitcast_fusion
  149.0 0.8 reshape.66
  149.8 0.1 slice.32
  149.9 0.1 pad_maximum_fusion.2
  150.0 0.6 reshape.65
  (20 shorter events, 0.2 us)
Async XLA Ops:
  7.2 38.2 %all-gather.3.cloned.1.call-start = ((), (), s32[]{:S(2)}) async-start(), calls=%async_computation.3 | async-start | bytes 2433024 | tf_op jit(solution)/shard_map/all_gather | solution.py:611
  9.7 16.1 %copy-start.2 = (bf16[288]{0:T(512)(128)(2,1)S(1)}, bf16[288]{0:T(512)(128)(2,1)}, u32[]{:S(2)}) copy-start(bf16[288]{0:T(512)(128)(2,1)} %param.8) | copy-start | bytes 1732
  21.6 18.5 %all-to-all-start.1 = ((bf16[4,7,72,256]{3,2,1,0:T(8,128)(2,1)}), bf16[4,7,72,256]{3,2,1,0:T(8,128)(2,1)S(1)}, u32[]{:S(2)}, u32[]{:S(2)}) async-start(bf16[4,7,72,256]{3,2,1,0:T(8,128)(2,1)} %get-tuple-element.17), calls=%async_computation.1 | async-start | bytes 2064384 | tf_op jit(solution)/shard_map/all_to_all | solution.py:618
  40.1 10.3 %copy-start.1 = (bf16[4,7,72,256]{3,2,1,0:T(8,128)(2,1)}, bf16[4,7,72,256]{3,2,1,0:T(8,128)(2,1)S(1)}, u32[]{:S(2)}) copy-start(bf16[4,7,72,256]{3,2,1,0:T(8,128)(2,1)S(1)} %all-to-all-done.1.moved_ref) | copy-start | bytes 3096580
  40.1 40.1 %all-to-all-start = ((bf16[4,14,72,256]{3,2,1,0:T(8,128)(2,1)}), bf16[4,14,72,256]{3,2,1,0:T(8,128)(2,1)S(1)}, u32[]{:S(2)}, u32[]{:S(2)}) async-start(bf16[4,14,72,256]{3,2,1,0:T(8,128)(2,1)} %get-tuple-element.16), calls=%async_computation | async-start | bytes 4128768 | tf_op jit(solution)/shard_map/all_to_all | solution.py:618
  43.7 6.7 %copy-start.4 = (f32[6]{0:T(128)}, f32[6]{0:T(128)S(1)}, u32[]{:S(2)}) copy-start(f32[6]{0:T(128)S(1)} %slice_bitcast_fusion.home_ref) | copy-start | bytes 76
  44.0 36.2 %copy-start.3 = (f32[12]{0:T(128)}, f32[12]{0:T(128)S(1)}, u32[]{:S(2)}) copy-start(f32[12]{0:T(128)S(1)} %slice_bitcast_fusion.1.home_ref) | copy-start | bytes 148
  80.2 1.3 copy-start
Sparse Core Ops, SparseCore 0:
  10.2 32.3 all-gather.2

commit v8 on v5

--- a/solution.py
+++ b/solution.py
@@ -40,29 +40,31 @@
     return count + ceil_div(count, MAIN // (modes - MAIN))
 
 
-def project_kernel(groups, n_qp, group, chunks, here_ref, home_ref, force_ref, *refs):
-    outs = refs[: len(chunks)]
-    rows_ref, main_ref, rest_ref = refs[len(chunks) :]
+STREAMS = 3
+
+
+def project_kernel(groups, group, share, first, count, here_ref, home_ref, *refs):
+    force_refs, (out_ref, rows_ref, main_ref, rest_ref) = refs[:STREAMS], refs[STREAMS:]
     modes = home_ref.shape[0]
-    lines = rows_ref.shape[0]
-    share = lines // groups
+    lines = groups * count
     rest = modes - MAIN
     per_slot = MAIN // rest
-    depth = outs[0].shape[2]
+    depth = out_ref.shape[2]
     step = pl.program_id(0)
-    here = force_ref.shape[1] // modes
+    here = force_refs[0].shape[1] // modes
     pitch = lines + 1
 
     @pl.when(step == 0)
     def _():
         line = lax.broadcasted_iota(jnp.int32, (lines, modes), 0)
         column = lax.broadcasted_iota(jnp.int32, (lines, modes), 1)
-        own = here_ref[0] * share + line % share
-        wanted = (line // share) * group + own
+        own = here_ref[0] * share + first + line % count
+        wanted = (line // count) * group + own
         select = jnp.logical_and(column == wanted, own < group).astype(BF16)
         rows_ref[...] = dot_nt(select, home_ref[...]).astype(BF16)
 
-    result = dot_nn(rows_ref[...], force_ref[...])
+    force = jnp.concatenate([ref[...] for ref in force_refs], axis=0)
+    result = dot_nn(rows_ref[...], force)
     for c in range(here):
         row = (step * here + c) * pitch
         piece = result[:, c * modes : (c + 1) * modes]
@@ -75,52 +77,60 @@
     @pl.when(step == pl.num_programs(0) - 1)
     def _():
         lane = lax.broadcasted_iota(jnp.int32, (depth, TILE), 1)
-        for (first, count), out_ref in zip(chunks, outs):
-            for t in range(groups):
-                base = t * share + first
-                for r in range(count):
-                    for h in range(2):
-                        out_ref[t, r, :, h * TILE : (h + 1) * TILE] = main_ref[
-                            h, pl.ds(base + r, depth, stride=pitch), :
-                        ].astype(BF16)
-                for g in range(ceil_div(count, per_slot)):
-                    for h in range(2):
-                        packed = jnp.zeros((depth, TILE), F32)
-                        for b in range(per_slot // 2):
-                            r = g * per_slot + h * (per_slot // 2) + b
-                            if r < count:
-                                piece = rest_ref[pl.ds(base + r, depth, stride=pitch), :]
-                                if b > 0:
-                                    piece = pltpu.roll(piece, b * rest, 1)
-                                packed = jnp.where(lane // rest == b, piece, packed)
-                        out_ref[t, count + g, :, h * TILE : (h + 1) * TILE] = packed.astype(BF16)
-
-
-def project(here, home_vectors, force_table, groups, n_qp, group, share, chunks):
+        for t in range(groups):
+            base = t * count
+            for r in range(count):
+                for h in range(2):
+                    out_ref[t, r, :, h * TILE : (h + 1) * TILE] = main_ref[
+                        h, pl.ds(base + r, depth, stride=pitch), :
+                    ].astype(BF16)
+            for g in range(ceil_div(count, per_slot)):
+                for h in range(2):
+                    packed = jnp.zeros((depth, TILE), F32)
+                    for b in range(per_slot // 2):
+                        r = g * per_slot + h * (per_slot // 2) + b
+                        if r < count:
+                            piece = rest_ref[pl.ds(base + r, depth, stride=pitch), :]
+                            if b > 0:
+                                piece = pltpu.roll(piece, b * rest, 1)
+                            packed = jnp.where(lane // rest == b, piece, packed)
+                    out_ref[t, count + g, :, h * TILE : (h + 1) * TILE] = packed.astype(BF16)
+
+
+def project(here, home_vectors, force_table, groups, group, share, first, count):
     modes = home_vectors.shape[0]
-    lines = groups * share
+    lines = groups * count
     depth = force_table.shape[1] // modes
     per_step = 8 if depth % 8 == 0 else 4
-    steps = depth // per_step
-    shapes = [(groups, slots_of(count, modes), depth, MAIN) for _, count in chunks]
+    rows = modes // STREAMS
+    shape = (groups, slots_of(count, modes), depth, MAIN)
+
+    def stream(k):
+        return pl.BlockSpec((rows, per_step * modes), lambda i: (k, i))
+
     return pl.pallas_call(
-        functools.partial(project_kernel, groups, n_qp, group, chunks),
-        grid=(steps,),
+        functools.partial(project_kernel, groups, group, share, first, count),
+        grid=(depth // per_step,),
         in_specs=[
             pl.BlockSpec(memory_space=pltpu.SMEM),
             pl.BlockSpec((modes, modes), lambda i: (0, 0)),
-            pl.BlockSpec((modes, per_step * modes), lambda i: (0, i)),
-        ],
-        out_specs=[pl.BlockSpec(shape, lambda i: (0, 0, 0, 0)) for shape in shapes],
-        out_shape=[jax.ShapeDtypeStruct(shape, BF16) for shape in shapes],
+        ]
+        + [stream(k) for k in range(STREAMS)],
+        out_specs=pl.BlockSpec(shape, lambda i: (0, 0, 0, 0)),
+        out_shape=jax.ShapeDtypeStruct(shape, BF16),
         scratch_shapes=[
             pltpu.VMEM((lines, modes), BF16),
             pltpu.VMEM((2, (depth + 1) * (lines + 1), TILE), F32),
             pltpu.VMEM(((depth + 1) * (lines + 1), TILE), F32),
         ],
         compiler_params=pltpu.CompilerParams(vmem_limit_bytes=VMEM_BYTES),
+        cost_estimate=pl.CostEstimate(
+            flops=2 * lines * modes * modes * depth,
+            bytes_accessed=2 * modes * modes * depth,
+            transcendentals=0,
+        ),
         name="project",
-    )(here, home_vectors, force_table)
+    )(here, home_vectors, *[force_table] * STREAMS)
 
 
 def identity(size):
@@ -130,10 +140,11 @@
     ).astype(BF16)
 
 
-def pack_kernel(part_ref, partner_ref, weight_ref, grid_ref, freq_ref, out_ref):
+def pack_kernel(part_ref, partner_ref, weight_ref, grid_ref, freq_ref, upper_ref, lower_ref):
     own_pairs, modes, _ = grid_ref.shape
     rest = modes - MAIN
     lines = rest // 2
+    cut = upper_ref.shape[1]
     part = part_ref[0]
     line = lax.broadcasted_iota(jnp.int32, (lines, modes), 0)
     column = lax.broadcasted_iota(jnp.int32, (lines, modes), 1)
@@ -152,7 +163,8 @@
 
             @pl.when(part == p)
             def _():
-                out_ref[s, :modes, :] = grid_ref[s, :, p * TILE : (p + 1) * TILE]
+                upper_ref[s] = grid_ref[s, :cut, p * TILE : (p + 1) * TILE]
+                lower_ref[s, : modes - cut, :] = grid_ref[s, cut:, p * TILE : (p + 1) * TILE]
 
         turned = dot_nt(select, grid_ref[s])
         turned = (
@@ -161,40 +173,42 @@
             jnp.concatenate([turned[:, MAIN:], jnp.zeros((lines, TILE - rest), F32)], axis=1),
         )
         for h in range(3):
-            start = modes + h * lines
-            out_ref[s, start : start + lines, :] = turned[h].astype(BF16)
+            start = modes - cut + h * lines
+            lower_ref[s, start : start + lines, :] = turned[h].astype(BF16)
         pair = partner_ref[s].astype(F32)
         weight = weight_ref[s].astype(F32)
         side = jnp.where(lane16 == 0, pair, jnp.where(lane16 == 1, weight, 0.0))
         side = jnp.where(line16 == 3, side, 0.0)
         for h in range(3):
             side = jnp.where(line16 == h, freq_tiles[h][s : s + 1], side)
-        start = modes + 3 * lines
-        out_ref[s, start : start + 16, :] = side.astype(BF16)
+        start = modes - cut + 3 * lines
+        lower_ref[s, start : start + 16, :] = side.astype(BF16)
 
 
 def pack_own(part, partner, weights, grid_vectors, partner_frequencies):
     own_pairs, modes, _ = grid_vectors.shape
     smem = pl.BlockSpec(memory_space=pltpu.SMEM)
     vmem = pl.BlockSpec(memory_space=pltpu.VMEM)
-    rows = modes + 3 * (modes - MAIN) // 2 + 16
+    rows = (modes + 3 * (modes - MAIN) // 2 + 16) // 2
+    shape = jax.ShapeDtypeStruct((own_pairs, rows, TILE), BF16)
     return pl.pallas_call(
         pack_kernel,
         in_specs=[smem, smem, smem, vmem, vmem],
-        out_specs=vmem,
-        out_shape=jax.ShapeDtypeStruct((own_pairs, rows, TILE), BF16),
+        out_specs=[vmem] * 2,
+        out_shape=[shape] * 2,
         compiler_params=pltpu.CompilerParams(vmem_limit_bytes=VMEM_BYTES),
         name="pack_own",
     )(part, partner, weights, grid_vectors, partner_frequencies)
 
 
 def arrange_kernel(
-    pack_ref, partner_ref, weight_ref, grid_ref, grid_t_ref, freq_row_ref, freq_col_ref
+    upper_ref, lower_ref, partner_ref, weight_ref, grid_ref, grid_t_ref, freq_row_ref, freq_col_ref
 ):
-    owners, parts, each, rows, _ = pack_ref.shape
+    owners, parts, each, cut, _ = upper_ref.shape
     modes = grid_ref.shape[1]
     rest = modes - MAIN
     lines = rest // parts
+    left = modes - cut
     eye = identity(MAIN)
     source = lax.broadcasted_iota(jnp.int32, (TILE, TILE), 0)
     place = lax.broadcasted_iota(jnp.int32, (TILE, TILE), 1)
@@ -209,15 +223,17 @@
         for s in range(each):
             x = q * each + s
             for part in range(parts):
-                grid_ref[x, :, part * TILE : (part + 1) * TILE] = pack_ref[q, part, s, :modes, :]
+                lanes = slice(part * TILE, (part + 1) * TILE)
+                grid_ref[x, :cut, lanes] = upper_ref[q, part, s]
+                grid_ref[x, cut:, lanes] = lower_ref[q, part, s, :left, :]
                 for h in range(3):
-                    start, width = modes + h * lines, min(TILE, modes - h * TILE)
-                    piece = pack_ref[q, part, s, start : start + lines, :]
+                    start, width = left + h * lines, min(TILE, modes - h * TILE)
+                    piece = lower_ref[q, part, s, start : start + lines, :]
                     grid_t_ref[
                         x, MAIN + part * lines : MAIN + (part + 1) * lines, h * TILE : h * TILE + width
                     ] = piece[:, :width]
             grid_t_ref[x, :MAIN, :] = dot_nt(eye, grid_ref[x]).astype(BF16)
-            side = pack_ref[q, 0, s, modes + 3 * lines : modes + 3 * lines + 16, :]
+            side = lower_ref[q, 0, s, left + 3 * lines : left + 3 * lines + 16, :]
             wide = side.astype(F32)
             freq_row_ref[x, :, :TILE] = wide[0:1]
             freq_row_ref[x, :, TILE:MAIN] = wide[1:2]
@@ -236,17 +252,17 @@
                 ref[x] = found.astype(ref.dtype)
         return carry
 
-    lax.fori_loop(0, owners, one, 0)
-
-
-def arrange(pack, modes):
-    owners, parts, each, _, _ = pack.shape
+    lax.fori_loop(0, owners, one, 0, unroll=owners <= 4)
+
+
+def arrange(packs, modes):
+    owners, parts, each, _, _ = packs[0].shape
     pairs = owners * each
     smem = pl.BlockSpec(memory_space=pltpu.SMEM)
     vmem = pl.BlockSpec(memory_space=pltpu.VMEM)
     return pl.pallas_call(
         arrange_kernel,
-        in_specs=[vmem],
+        in_specs=[vmem] * 2,
         out_specs=[smem, smem, vmem, vmem, vmem, vmem],
         out_shape=[
             jax.ShapeDtypeStruct((pairs,), jnp.int32),
@@ -258,7 +274,7 @@
         ],
         compiler_params=pltpu.CompilerParams(vmem_limit_bytes=VMEM_BYTES),
         name="arrange",
-    )(pack)
+    )(*packs)
 
 
 def interleave(heavy, light):
@@ -596,23 +612,24 @@
 
     assert n_fc * TILE == MAIN
     own_part = lax.axis_index("fc").astype(jnp.int32)[None]
-    pack = pack_own(own_part, partner, weights, grid_vectors, partner_frequencies)
-    pack = lax.all_gather(pack, ("qp", "fc"), axis=0)
-    pack = pack.reshape(n_qp, n_fc, own_pairs, pack.shape[2], TILE)
-
-    sent = project(
-        here.astype(jnp.int32)[None], home_vectors, force_table, groups, n_qp, group, share, chunks
-    )
-    moved = [
-        lax.all_to_all(x, ("mode", "fc"), split_axis=0, concat_axis=0, tiled=True) for x in sent
-    ]
+    packs = pack_own(own_part, partner, weights, grid_vectors, partner_frequencies)
+    packs = [lax.all_gather(half, ("qp", "fc"), axis=0) for half in packs]
+    packs = [half.reshape(n_qp, n_fc, own_pairs, half.shape[2], TILE) for half in packs]
+
+    here_word = here.astype(jnp.int32)[None]
+    moved = []
+    for first, count in chunks:
+        sent = project(here_word, home_vectors, force_table, groups, group, share, first, count)
+        moved.append(
+            lax.all_to_all(sent, ("mode", "fc"), split_axis=0, concat_axis=0, tiled=True)
+        )
 
     own = lax.axis_index(("mode", "fc"))
     home = home_freqs.astype(F32).reshape(groups, group)
     home = jnp.pad(home, ((0, 0), (0, share * n_qp - group)), constant_values=1.0)
     home = lax.dynamic_slice(home, (own, here * share), (1, share)).reshape(share)
 
-    shared = arrange(pack, modes)
+    shared = arrange(packs, modes)
     parts, widths = [], []
     for (first, count), block in zip(chunks, moved):
         found = coupling(

time: 154 us -> 165 us (1.071)
  Pallas kernels: 93.8 us -> 102 us
  waiting for transfers between devices: 23.8 us -> 27.7 us
  starting transfers between devices: 18.6 us -> 16.4 us
    all_gather x1 -> x2, waiting for transfers between devices: 0.01 us -> 14.3 us  [local(): packs = [lax.all_gather(half, ('qp', 'fc'), axis=0) for half in packs]]
    all_to_all x2, waiting for transfers between devices: 14.1 us -> 2.98 us  [local(): lax.all_to_all(sent, ('mode', 'fc'), split_axis=0, concat_axis=0, tiled=T...]
    pallas_call x2 -> x3, Pallas kernels: 17.8 us -> 26.4 us  [the longest x2 21.4 us: project(): pl.pallas_call(functools.partial(project_kernel, groups, group, share, fi...]
    all_to_all x2, starting transfers between devices: 10.7 us -> 8.39 us  [local(): lax.all_to_all(found.reshape(n_qp, own_pairs, found.shape[1], modes), 'qp...]
  transfers between devices with their start and end apart: 5 -> 6, of which waited for: 2 -> 3; matrix products, arithmetic and copies ran while one was open for 1% -> 1% of each run, Pallas kernels for 59% -> 61%
where the time goes in v8:
time: 165 us; the launch traced here: 164 us
  Pallas kernels  102 us (62%)
  waiting for transfers between devices  27.7 us (17%)
  starting transfers between devices  16.4 us (10%)
  between operations  14.1 us (9%)
  local copies, waits for them, and re-layouts  1.96 us (1%)
    pallas_call x2, Pallas kernels, coupling(): pl.pallas_call(functools.partial(coupling_kernel, share, block), in_specs...  73.6 us
    pallas_call x2, Pallas kernels, project(): pl.pallas_call(functools.partial(project_kernel, groups, group, share, fi...  21.4 us
    all_gather x2, waiting for transfers between devices, local(): packs = [lax.all_gather(half, ('qp', 'fc'), axis=0) for half in packs]  14.3 us
    all_to_all x2, waiting for transfers between devices, local(): lax.all_to_all(found.reshape(n_qp, own_pairs, found.shape[1], modes), 'qp...  9.74 us
    all_to_all x2, starting transfers between devices, local(): lax.all_to_all(found.reshape(n_qp, own_pairs, found.shape[1], modes), 'qp...  8.39 us
    all_to_all x2, starting transfers between devices, local(): lax.all_to_all(sent, ('mode', 'fc'), split_axis=0, concat_axis=0, tiled=T...  7.97 us
    pallas_call x1, Pallas kernels, arrange(): pl.pallas_call(arrange_kernel, in_specs=[vmem] * 2, out_specs=[smem, smem...  5.01 us
  transfers between devices with their start and end apart: 6, of which 3 were waited for; matrix products, arithmetic and copies ran while one was open for 1% of the time, Pallas kernels for 61%

profile of v8, /device:TPU:0, one launch (start us, length us, event | category | flops | bytes accessed | tf_op | source)
XLA Modules:
  0.0 164.0 jit_solution(557749939919227496)
XLA Ops:
  7.2 2.4 %pack_own.1 = (bf16[3,176,128]{2,1,0:T(8,128)(2,1)}, bf16[3,176,128]{2,1,0:T(8,128)(2,1)}) custom-call(s32[1]{0:T(128)} %bitcast.part_ref, s32[3]{0:T(128)} %partner_ref.1, s32[3]{0:T(128)} %weight_ref.1, bf16[3,288,288]{2,1,0:T(8,128)(2,1)} %grid_ref.1, bf16[3,288]{1,0:T(4,128)(2,1)} %freq_ref.1), custom_call_target="tpu_custom_call" | custom-call | tf_op jit(solution)/shard_map/pack_own/pallas_call | solution.py:194
  9.7 0.7 all-gather.7.cloned.1.call-update
  10.4 10.3 %project.2 = bf16[4,7,72,256]{3,2,1,0:T(8,128)(2,1)} custom-call(s32[1]{0:T(128)} %bitcast.8.here_ref, bf16[288,288]{1,0:T(8,128)(2,1)} %home_ref.3, bf16[288,20736]{1,0:T(8,128)(2,1)} %refs_2_.3, bf16[288,20736]{1,0:T(8,128)(2,1)} %refs_2_.3, bf16[288,20736]{1,0:T(8,128)(2,1)} %refs_2_.3), custom_call_target="tpu_custom_call" | custom-call | flops 286654464 | bytes 11943936 | tf_op jit(solution)/shard_map/project/pallas_call | solution.py:111
  20.7 4.4 %all-to-all-start = ((bf16[4,7,72,256]{3,2,1,0:T(8,128)(2,1)}), bf16[4,7,72,256]{3,2,1,0:T(8,128)(2,1)S(1)}, u32[]{:S(2)}, u32[]{:S(2)}) async-start(bf16[4,7,72,256]{3,2,1,0:T(8,128)(2,1)} %project.2), calls=%async_computation | async-start | bytes 2064384 | tf_op jit(solution)/shard_map/all_to_all | solution.py:624
  25.1 0.1 reshape.76
  25.1 0.1 dynamic_slice.3
  25.2 11.1 %project.3 = bf16[4,14,72,256]{3,2,1,0:T(8,128)(2,1)} custom-call(s32[1]{0:T(128)} %bitcast.8.here_ref, bf16[288,288]{1,0:T(8,128)(2,1)} %home_ref.3, bf16[288,20736]{1,0:T(8,128)(2,1)} %refs_2_.3, bf16[288,20736]{1,0:T(8,128)(2,1)} %refs_2_.3, bf16[288,20736]{1,0:T(8,128)(2,1)} %refs_2_.3), custom_call_target="tpu_custom_call" | custom-call | flops 573308928 | bytes 11943936 | tf_op jit(solution)/shard_map/project/pallas_call | solution.py:111
  36.4 3.0 %all-to-all-done.moved_ref = bf16[4,7,72,256]{3,2,1,0:T(8,128)(2,1)S(1)} async-done(((bf16[4,7,72,256]{3,2,1,0:T(8,128)(2,1)}), bf16[4,7,72,256]{3,2,1,0:T(8,128)(2,1)S(1)}, u32[]{:S(2)}, u32[]{:S(2)}) %all-to-all-start) | async-done | bytes 1032224 | tf_op jit(solution)/shard_map/all_to_all | solution.py:624
  39.3 3.6 %all-to-all-start.2 = ((bf16[4,14,72,256]{3,2,1,0:T(8,128)(2,1)}), bf16[4,14,72,256]{3,2,1,0:T(8,128)(2,1)S(1)}, u32[]{:S(2)}, u32[]{:S(2)}) async-start(bf16[4,14,72,256]{3,2,1,0:T(8,128)(2,1)} %project.3), calls=%async_computation.2 | async-start | bytes 4128768 | tf_op jit(solution)/shard_map/all_to_all | solution.py:624
  43.0 0.1 slice_bitcast_fusion.home_ref
  43.1 0.1 stack.29
  43.3 0.1 reshape.70
  43.3 0.6 pad_maximum_fusion.1.home_row_ref
  44.0 0.6 pad_maximum_fusion.home_row_ref
  44.6 14.3 %all-gather.7.cloned.1.call-done = bf16[24,176,128]{2,1,0:T(8,128)(2,1)} async-done(((bf16[3,176,128]{2,1,0:T(8,128)(2,1)}), bf16[24,176,128]{2,1,0:T(8,128)(2,1)}) %all-gather.7.cloned.1.call-update) | async-done | bytes 1081360 | tf_op jit(solution)/shard_map/all_gather | solution.py:616
  58.9 5.0 %arrange.1 = (s32[12]{0:T(128)}, f32[12]{0:T(128)}, bf16[12,288,256]{2,1,0:T(8,128)(2,1)}, bf16[12,288,288]{2,1,0:T(8,128)(2,1)}, f32[12,1,384]{2,1,0:T(1,128)}, /*index=5*/f32[288,128]{1,0:T(8,128)}) custom-call(bf16[4,2,3,176,128]{4,3,2,1,0:T(8,128)(2,1)} %bitcast.23, bf16[4,2,3,176,128]{4,3,2,1,0:T(8,128)(2,1)} %bitcast.24), custom_call_target="tpu_custom_call" | custom-call | tf_op jit(solution)/shard_map/arrange/pallas_call | solution.py:263
  63.9 28.2 %coupling.2 = f32[12,8,288]{2,1,0:T(8,128)} custom-call(s32[12]{0:T(128)} %get-tuple-element.12.partner_ref, f32[12]{0:T(128)} %get-tuple-element.13.weight_ref, f32[6]{0:T(128)} %copy-done.4, bf16[12,288,256]{2,1,0:T(8,128)(2,1)} %get-tuple-element.14.grid_ref, bf16[12,288,288]{2,1,0:T(8,128)(2,1)} %get-tuple-element.15.grid_t_ref, ...), custom_call_target="tpu_custom_call" | custom-call | flops 6879707136 | bytes 3981312 | tf_op jit(solution)/shard_map/coupling/pallas_call | solution.py:579
  92.1 3.5 %all-to-all-start.1 = ((f32[4,3,8,288]{3,2,1,0:T(8,128)}), f32[4,3,8,288]{3,2,1,0:T(8,128)S(1)}, u32[]{:S(2)}, u32[]{:S(2)}) async-start(f32[4,3,8,288]{3,2,1,0:T(8,128)} %bitcast.27), calls=%async_computation.1 | async-start | bytes 294912 | tf_op jit(solution)/shard_map/all_to_all | solution.py:638
  95.7 45.4 %coupling.3 = f32[12,16,288]{2,1,0:T(8,128)} custom-call(s32[12]{0:T(128)} %get-tuple-element.12.partner_ref, f32[12]{0:T(128)} %get-tuple-element.13.weight_ref, f32[12]{0:T(128)} %copy-done.3, bf16[12,288,256]{2,1,0:T(8,128)(2,1)} %get-tuple-element.14.grid_ref, bf16[12,288,288]{2,1,0:T(8,128)(2,1)} %get-tuple-element.15.grid_t_ref, ...), custom_call_target="tpu_custom_call" | custom-call | flops 13759414272 | bytes 7962624 | tf_op jit(solution)/shard_map/coupling/pallas_call | solution.py:579
  141.0 4.9 %all-to-all-start.3 = ((f32[4,3,16,288]{3,2,1,0:T(8,128)}), f32[4,3,16,288]{3,2,1,0:T(8,128)S(1)}, u32[]{:S(2)}, u32[]{:S(2)}) async-start(f32[4,3,16,288]{3,2,1,0:T(8,128)} %bitcast.26), calls=%async_computation.3 | async-start | bytes 589824 | tf_op jit(solution)/shard_map/all_to_all | solution.py:638
  145.9 9.7 %all-to-all-done.3 = f32[4,3,16,288]{3,2,1,0:T(8,128)S(1)} async-done(((f32[4,3,16,288]{3,2,1,0:T(8,128)}), f32[4,3,16,288]{3,2,1,0:T(8,128)S(1)}, u32[]{:S(2)}, u32[]{:S(2)}) %all-to-all-start.3) | async-done | bytes 221216 | tf_op jit(solution)/shard_map/all_to_all | solution.py:638
  155.6 0.1 pad_maximum_fusion.2
  155.7 0.6 reshape.73
  156.4 0.8 reshape.74
  (25 shorter events, 0.4 us)
Async XLA Ops:
  7.2 37.4 %all-gather.5.cloned.1.call-start = ((), (), s32[]{:S(2)}) async-start(), calls=%async_computation.4 | async-start | bytes 1216512 | tf_op jit(solution)/shard_map/all_gather | solution.py:616
  9.6 49.2 %all-gather.7.cloned.1.call-start = ((), (), s32[]{:S(2)}) async-start(), calls=%async_computation.5 | async-start | bytes 1216512 | tf_op jit(solution)/shard_map/all_gather | solution.py:616
  20.7 4.4 %copy-start.2 = (bf16[288]{0:T(512)(128)(2,1)S(1)}, bf16[288]{0:T(512)(128)(2,1)}, u32[]{:S(2)}) copy-start(bf16[288]{0:T(512)(128)(2,1)} %param.8) | copy-start | bytes 1732
  20.7 18.7 %all-to-all-start = ((bf16[4,7,72,256]{3,2,1,0:T(8,128)(2,1)}), bf16[4,7,72,256]{3,2,1,0:T(8,128)(2,1)S(1)}, u32[]{:S(2)}, u32[]{:S(2)}) async-start(bf16[4,7,72,256]{3,2,1,0:T(8,128)(2,1)} %project.2), calls=%async_computation | async-start | bytes 2064384 | tf_op jit(solution)/shard_map/all_to_all | solution.py:624
  39.3 3.7 %copy-start.1 = (bf16[4,7,72,256]{3,2,1,0:T(8,128)(2,1)}, bf16[4,7,72,256]{3,2,1,0:T(8,128)(2,1)S(1)}, u32[]{:S(2)}) copy-start(bf16[4,7,72,256]{3,2,1,0:T(8,128)(2,1)S(1)} %all-to-all-done.moved_ref) | copy-start | bytes 3096580
  39.3 52.8 %all-to-all-start.2 = ((bf16[4,14,72,256]{3,2,1,0:T(8,128)(2,1)}), bf16[4,14,72,256]{3,2,1,0:T(8,128)(2,1)S(1)}, u32[]{:S(2)}, u32[]{:S(2)}) async-start(bf16[4,14,72,256]{3,2,1,0:T(8,128)(2,1)} %project.3), calls=%async_computation.2 | async-start | bytes 4128768 | tf_op jit(solution)/shard_map/all_to_all | solution.py:624
  43.0 49.1 %copy-start.3 = (f32[12]{0:T(128)}, f32[12]{0:T(128)S(1)}, u32[]{:S(2)}) copy-start(f32[12]{0:T(128)S(1)} %slice_bitcast_fusion.home_ref) | copy-start | bytes 148
  43.2 20.7 %copy-start.4 = (f32[6]{0:T(128)}, f32[6]{0:T(128)S(1)}, u32[]{:S(2)}) copy-start(f32[6]{0:T(128)S(1)} %slice_bitcast_fusion.1.home_ref) | copy-start | bytes 76
  92.1 3.5 %copy-start = (bf16[4,14,72,256]{3,2,1,0:T(8,128)(2,1)}, bf16[4,14,72,256]{3,2,1,0:T(8,128)(2,1)S(1)}, u32[]{:S(2)}) copy-start(bf16[4,14,72,256]{3,2,1,0:T(8,128)(2,1)S(1)} %all-to-all-done.2.moved_ref) | copy-start | bytes 6193156
  92.1 48.9 %all-to-all-start.1 = ((f32[4,3,8,288]{3,2,1,0:T(8,128)}), f32[4,3,8,288]{3,2,1,0:T(8,128)S(1)}, u32[]{:S(2)}, u32[]{:S(2)}) async-start(f32[4,3,8,288]{3,2,1,0:T(8,128)} %bitcast.27), calls=%async_computation.1 | async-start | bytes 294912 | tf_op jit(solution)/shard_map/all_to_all | solution.py:638
  141.0 14.6 %all-to-all-start.3 = ((f32[4,3,16,288]{3,2,1,0:T(8,128)}), f32[4,3,16,288]{3,2,1,0:T(8,128)S(1)}, u32[]{:S(2)}, u32[]{:S(2)}) async-start(f32[4,3,16,288]{3,2,1,0:T(8,128)} %bitcast.26), calls=%async_computation.3 | async-start | bytes 589824 | tf_op jit(solution)/shard_map/all_to_all | solution.py:638
Sparse Core Ops, SparseCore 0:
  10.2 24.9 all-gather.4
  36.9 21.9 all-gather.6

commit v9 on v6

--- a/solution.py
+++ b/solution.py
@@ -40,29 +40,31 @@
     return count + ceil_div(count, MAIN // (modes - MAIN))
 
 
-def project_kernel(groups, n_qp, group, chunks, here_ref, home_ref, force_ref, *refs):
-    outs = refs[: len(chunks)]
-    rows_ref, main_ref, rest_ref = refs[len(chunks) :]
+STREAMS = 3
+
+
+def project_kernel(groups, group, share, first, count, here_ref, home_ref, *refs):
+    force_refs, (out_ref, rows_ref, main_ref, rest_ref) = refs[:STREAMS], refs[STREAMS:]
     modes = home_ref.shape[0]
-    lines = rows_ref.shape[0]
-    share = lines // groups
+    lines = groups * count
     rest = modes - MAIN
     per_slot = MAIN // rest
-    depth = outs[0].shape[2]
+    depth = out_ref.shape[2]
     step = pl.program_id(0)
-    here = force_ref.shape[1] // modes
+    here = force_refs[0].shape[1] // modes
     pitch = lines + 1
 
     @pl.when(step == 0)
     def _():
         line = lax.broadcasted_iota(jnp.int32, (lines, modes), 0)
         column = lax.broadcasted_iota(jnp.int32, (lines, modes), 1)
-        own = here_ref[0] * share + line % share
-        wanted = (line // share) * group + own
+        own = here_ref[0] * share + first + line % count
+        wanted = (line // count) * group + own
         select = jnp.logical_and(column == wanted, own < group).astype(BF16)
         rows_ref[...] = dot_nt(select, home_ref[...]).astype(BF16)
 
-    result = dot_nn(rows_ref[...], force_ref[...])
+    force = jnp.concatenate([ref[...] for ref in force_refs], axis=0)
+    result = dot_nn(rows_ref[...], force)
     for c in range(here):
         row = (step * here + c) * pitch
         piece = result[:, c * modes : (c + 1) * modes]
@@ -75,52 +77,60 @@
     @pl.when(step == pl.num_programs(0) - 1)
     def _():
         lane = lax.broadcasted_iota(jnp.int32, (depth, TILE), 1)
-        for (first, count), out_ref in zip(chunks, outs):
-            for t in range(groups):
-                base = t * share + first
-                for r in range(count):
-                    for h in range(2):
-                        out_ref[t, r, :, h * TILE : (h + 1) * TILE] = main_ref[
-                            h, pl.ds(base + r, depth, stride=pitch), :
-                        ].astype(BF16)
-                for g in range(ceil_div(count, per_slot)):
-                    for h in range(2):
-                        packed = jnp.zeros((depth, TILE), F32)
-                        for b in range(per_slot // 2):
-                            r = g * per_slot + h * (per_slot // 2) + b
-                            if r < count:
-                                piece = rest_ref[pl.ds(base + r, depth, stride=pitch), :]
-                                if b > 0:
-                                    piece = pltpu.roll(piece, b * rest, 1)
-                                packed = jnp.where(lane // rest == b, piece, packed)
-                        out_ref[t, count + g, :, h * TILE : (h + 1) * TILE] = packed.astype(BF16)
-
-
-def project(here, home_vectors, force_table, groups, n_qp, group, share, chunks):
+        for t in range(groups):
+            base = t * count
+            for r in range(count):
+                for h in range(2):
+                    out_ref[t, r, :, h * TILE : (h + 1) * TILE] = main_ref[
+                        h, pl.ds(base + r, depth, stride=pitch), :
+                    ].astype(BF16)
+            for g in range(ceil_div(count, per_slot)):
+                for h in range(2):
+                    packed = jnp.zeros((depth, TILE), F32)
+                    for b in range(per_slot // 2):
+                        r = g * per_slot + h * (per_slot // 2) + b
+                        if r < count:
+                            piece = rest_ref[pl.ds(base + r, depth, stride=pitch), :]
+                            if b > 0:
+                                piece = pltpu.roll(piece, b * rest, 1)
+                            packed = jnp.where(lane // rest == b, piece, packed)
+                    out_ref[t, count + g, :, h * TILE : (h + 1) * TILE] = packed.astype(BF16)
+
+
+def project(here, home_vectors, force_table, groups, group, share, first, count):
     modes = home_vectors.shape[0]
-    lines = groups * share
+    lines = groups * count
     depth = force_table.shape[1] // modes
     per_step = 8 if depth % 8 == 0 else 4
-    steps = depth // per_step
-    shapes = [(groups, slots_of(count, modes), depth, MAIN) for _, count in chunks]
+    rows = modes // STREAMS
+    shape = (groups, slots_of(count, modes), depth, MAIN)
+
+    def stream(k):
+        return pl.BlockSpec((rows, per_step * modes), lambda i: (k, i))
+
     return pl.pallas_call(
-        functools.partial(project_kernel, groups, n_qp, group, chunks),
-        grid=(steps,),
+        functools.partial(project_kernel, groups, group, share, first, count),
+        grid=(depth // per_step,),
         in_specs=[
             pl.BlockSpec(memory_space=pltpu.SMEM),
             pl.BlockSpec((modes, modes), lambda i: (0, 0)),
-            pl.BlockSpec((modes, per_step * modes), lambda i: (0, i)),
-        ],
-        out_specs=[pl.BlockSpec(shape, lambda i: (0, 0, 0, 0)) for shape in shapes],
-        out_shape=[jax.ShapeDtypeStruct(shape, BF16) for shape in shapes],
+        ]
+        + [stream(k) for k in range(STREAMS)],
+        out_specs=pl.BlockSpec(shape, lambda i: (0, 0, 0, 0)),
+        out_shape=jax.ShapeDtypeStruct(shape, BF16),
         scratch_shapes=[
             pltpu.VMEM((lines, modes), BF16),
             pltpu.VMEM((2, (depth + 1) * (lines + 1), TILE), F32),
             pltpu.VMEM(((depth + 1) * (lines + 1), TILE), F32),
         ],
         compiler_params=pltpu.CompilerParams(vmem_limit_bytes=VMEM_BYTES),
+        cost_estimate=pl.CostEstimate(
+            flops=2 * lines * modes * modes * depth,
+            bytes_accessed=2 * modes * modes * depth,
+            transcendentals=0,
+        ),
         name="project",
-    )(here, home_vectors, force_table)
+    )(here, home_vectors, *[force_table] * STREAMS)
 
 
 def identity(size):
@@ -238,7 +248,7 @@
                 ref[x] = found.astype(ref.dtype)
         return carry
 
-    lax.fori_loop(0, owners, one, 0)
+    lax.fori_loop(0, owners, one, 0, unroll=owners <= 4)
 
 
 def arrange(pack, modes):
@@ -336,7 +346,10 @@
 
     row_id = lax.broadcasted_iota(jnp.int32, pick_ref.shape, 0)
     col_id = lax.broadcasted_iota(jnp.int32, pick_ref.shape, 1)
-    pick_ref[...] = (row_id // rest == col_id).astype(BF16)
+    branch = jnp.where(
+        row_id < share * TILE, row_id // TILE, (row_id - share * TILE) // rest
+    )
+    pick_ref[...] = (branch == col_id).astype(BF16)
     for ref in (out_ref, *inners, *sums, *rest_sums, *firsts):
         ref[...] = jnp.zeros_like(ref)
 
@@ -400,9 +413,9 @@
                     f, u = line_shapes(v, t, state["w"][b], state["c1"][b], state["c2"][b])
                     state["total"][b] = state["total"][b] + (f[:8] + f[8:])
                     r = step * block + b
-                    sum_ref[n : n + 16, r : r + 1] = jnp.sum(
-                        u[:, :TILE] + u[:, TILE:], axis=1, keepdims=True
-                    )
+                    sum_ref[n : n + 16, r * TILE : (r + 1) * TILE] = (
+                        u[:, :TILE] + u[:, TILE:]
+                    ).astype(BF16)
                 if n + 16 == modes:
                     for b in range(block):
                         r = step * block + b
@@ -488,7 +501,8 @@
 
     def collect(sum_ref, rest_sum_ref, state):
         def task():
-            second = sum_ref[...] + dot_nn(rest_sum_ref[...], pick_ref[...])
+            second = dot_nn(sum_ref[...], pick_ref[: share * TILE, :])
+            second += dot_nn(rest_sum_ref[...], pick_ref[share * TILE :, :])
             state["second"] = second.T[:share, :]
 
         return task
@@ -581,7 +595,7 @@
             pltpu.VMEM((share * modes, MAIN), BF16),
             pltpu.VMEM((pairs * rest, modes), BF16),
             pltpu.VMEM((pairs, rest_lanes, modes), BF16),
-            pltpu.VMEM((rest_lanes, TILE), BF16),
+            pltpu.VMEM((share * TILE + rest_lanes, TILE), BF16),
             pltpu.VMEM((modes, rest_lanes), F32),
             pltpu.VMEM((share // block * TILE, modes), BF16),
         ]
@@ -591,7 +605,7 @@
         + [pltpu.VMEM((modes, share // block * TILE), BF16)] * 2
         + [pltpu.VMEM((modes, block * MAIN), F32)] * 2
         + [pltpu.VMEM((4, modes, MAIN + TILE), F32)] * 2
-        + [pltpu.VMEM((modes, TILE), F32)] * 2
+        + [pltpu.VMEM((modes, share * TILE), BF16)] * 2
         + [pltpu.VMEM((modes, rest_lanes), BF16)] * 2
         + [pltpu.VMEM((padded, modes), F32)] * 2
     )
@@ -635,12 +649,13 @@
     pack = lax.all_gather(pack, ("qp", "fc"), axis=0)
     pack = pack.reshape(n_qp, n_fc, own_pairs, pack.shape[2], TILE)
 
-    sent = project(
-        here.astype(jnp.int32)[None], home_vectors, force_table, groups, n_qp, group, share, chunks
-    )
-    moved = [
-        lax.all_to_all(x, ("mode", "fc"), split_axis=0, concat_axis=0, tiled=True) for x in sent
-    ]
+    here_word = here.astype(jnp.int32)[None]
+    moved = []
+    for first, count in chunks:
+        sent = project(here_word, home_vectors, force_table, groups, group, share, first, count)
+        moved.append(
+            lax.all_to_all(sent, ("mode", "fc"), split_axis=0, concat_axis=0, tiled=True)
+        )
 
     own = lax.axis_index(("mode", "fc"))
     home = home_freqs.astype(F32).reshape(groups, group)

time: 154 us -> 156 us (1.013)
  Pallas kernels: 93.5 us -> 106 us
  waiting for transfers between devices: 23.8 us -> 12.7 us
    all_to_all x2, waiting for transfers between devices: 14.1 us -> 3 us  [local(): lax.all_to_all(sent, ('mode', 'fc'), split_axis=0, concat_axis=0, tiled=T...]
    pallas_call x1 -> x2, Pallas kernels: 11.9 us -> 21.4 us  [project(): pl.pallas_call(functools.partial(project_kernel, groups, group, share, fi...]
    pallas_call x2, Pallas kernels: 73.3 us -> 77 us  [coupling(): pl.pallas_call(functools.partial(coupling_kernel, share, block), in_specs...]
  transfers between devices with their start and end apart: 5 -> 5, of which waited for: 2 -> 2; matrix products, arithmetic and copies ran while one was open for 1% -> 1% of each run, Pallas kernels for 59% -> 67%
where the time goes in v9:
time: 156 us; the launch traced here: 155 us
  Pallas kernels  106 us (68%)
  starting transfers between devices  18.6 us (12%)
  between operations  14.1 us (9%)
  waiting for transfers between devices  12.7 us (8%)
  local copies, waits for them, and re-layouts  1.96 us (1%)
    pallas_call x2, Pallas kernels, coupling(): pl.pallas_call(functools.partial(coupling_kernel, share, block), in_specs...  77 us
    pallas_call x2, Pallas kernels, project(): pl.pallas_call(functools.partial(project_kernel, groups, group, share, fi...  21.4 us
    all_to_all x2, starting transfers between devices, local(): lax.all_to_all(found.reshape(n_qp, own_pairs, found.shape[1], modes), 'qp...  10.7 us
    all_to_all x2, waiting for transfers between devices, local(): lax.all_to_all(found.reshape(n_qp, own_pairs, found.shape[1], modes), 'qp...  9.69 us
    all_to_all x2, starting transfers between devices, local(): lax.all_to_all(sent, ('mode', 'fc'), split_axis=0, concat_axis=0, tiled=T...  7.83 us
    pallas_call x1, Pallas kernels, arrange(): pl.pallas_call(arrange_kernel, in_specs=[vmem], out_specs=[smem, smem, vm...  5.15 us
  transfers between devices with their start and end apart: 5, of which 2 were waited for; matrix products, arithmetic and copies ran while one was open for 1% of the time, Pallas kernels for 67%

profile of v9, /device:TPU:0, one launch (start us, length us, event | category | flops | bytes accessed | tf_op | source)
XLA Modules:
  0.0 154.7 jit_solution(6087631384066543834)
XLA Ops:
  7.2 2.5 %pack_own.1 = bf16[3,352,128]{2,1,0:T(8,128)(2,1)} custom-call(s32[1]{0:T(128)} %bitcast.part_ref, s32[3]{0:T(128)} %partner_ref.1, s32[3]{0:T(128)} %weight_ref.1, bf16[3,288,288]{2,1,0:T(8,128)(2,1)} %grid_ref.1, bf16[3,288]{1,0:T(4,128)(2,1)} %freq_ref.1), custom_call_target="tpu_custom_call" | custom-call | tf_op jit(solution)/shard_map/pack_own/pallas_call | solution.py:191
  9.7 10.2 %project.2 = bf16[4,7,72,256]{3,2,1,0:T(8,128)(2,1)} custom-call(s32[1]{0:T(128)} %bitcast.7.here_ref, bf16[288,288]{1,0:T(8,128)(2,1)} %home_ref.3, bf16[288,20736]{1,0:T(8,128)(2,1)} %refs_2_.3, bf16[288,20736]{1,0:T(8,128)(2,1)} %refs_2_.3, bf16[288,20736]{1,0:T(8,128)(2,1)} %refs_2_.3), custom_call_target="tpu_custom_call" | custom-call | flops 286654464 | bytes 11943936 | tf_op jit(solution)/shard_map/project/pallas_call | solution.py:111
  20.0 4.2 %all-to-all-start = ((bf16[4,7,72,256]{3,2,1,0:T(8,128)(2,1)}), bf16[4,7,72,256]{3,2,1,0:T(8,128)(2,1)S(1)}, u32[]{:S(2)}, u32[]{:S(2)}) async-start(bf16[4,7,72,256]{3,2,1,0:T(8,128)(2,1)} %project.2), calls=%async_computation | async-start | bytes 2064384 | tf_op jit(solution)/shard_map/all_to_all | solution.py:657
  24.2 0.1 reshape.72
  24.3 0.1 dynamic_slice.3
  24.4 11.1 %project.3 = bf16[4,14,72,256]{3,2,1,0:T(8,128)(2,1)} custom-call(s32[1]{0:T(128)} %bitcast.7.here_ref, bf16[288,288]{1,0:T(8,128)(2,1)} %home_ref.3, bf16[288,20736]{1,0:T(8,128)(2,1)} %refs_2_.3, bf16[288,20736]{1,0:T(8,128)(2,1)} %refs_2_.3, bf16[288,20736]{1,0:T(8,128)(2,1)} %refs_2_.3), custom_call_target="tpu_custom_call" | custom-call | flops 573308928 | bytes 11943936 | tf_op jit(solution)/shard_map/project/pallas_call | solution.py:111
  35.5 3.0 %all-to-all-done.moved_ref = bf16[4,7,72,256]{3,2,1,0:T(8,128)(2,1)S(1)} async-done(((bf16[4,7,72,256]{3,2,1,0:T(8,128)(2,1)}), bf16[4,7,72,256]{3,2,1,0:T(8,128)(2,1)S(1)}, u32[]{:S(2)}, u32[]{:S(2)}) %all-to-all-start) | async-done | bytes 1032224 | tf_op jit(solution)/shard_map/all_to_all | solution.py:657
  38.5 3.6 %all-to-all-start.2 = ((bf16[4,14,72,256]{3,2,1,0:T(8,128)(2,1)}), bf16[4,14,72,256]{3,2,1,0:T(8,128)(2,1)S(1)}, u32[]{:S(2)}, u32[]{:S(2)}) async-start(bf16[4,14,72,256]{3,2,1,0:T(8,128)(2,1)} %project.3), calls=%async_computation.2 | async-start | bytes 4128768 | tf_op jit(solution)/shard_map/all_to_all | solution.py:657
  42.1 0.1 slice_bitcast_fusion.home_ref
  42.2 0.1 broadcast_in_dim.15
  42.2 0.1 stack.29
  42.3 0.1 broadcast_in_dim.13
  42.4 0.1 reshape.66
  42.5 0.6 pad_maximum_fusion.1.home_row_ref
  43.1 0.6 pad_maximum_fusion.home_row_ref
  43.7 5.1 %arrange.1 = (s32[12]{0:T(128)}, f32[12]{0:T(128)}, bf16[12,288,256]{2,1,0:T(8,128)(2,1)}, bf16[12,288,384]{2,1,0:T(8,128)(2,1)}, f32[12,1,384]{2,1,0:T(1,128)}, /*index=5*/f32[288,128]{1,0:T(8,128)}) custom-call(bf16[4,2,3,352,128]{4,3,2,1,0:T(8,128)(2,1)} %bitcast.21), custom_call_target="tpu_custom_call" | custom-call | tf_op jit(solution)/shard_map/arrange/pallas_call | solution.py:259
  48.9 28.0 %coupling.2 = f32[12,8,288]{2,1,0:T(8,128)} custom-call(s32[12]{0:T(128)} %get-tuple-element.8.partner_ref, f32[12]{0:T(128)} %get-tuple-element.9.weight_ref, f32[6]{0:T(128)} %copy-done.4, bf16[12,288,256]{2,1,0:T(8,128)(2,1)} %get-tuple-element.10.grid_ref, bf16[12,288,384]{2,1,0:T(8,128)(2,1)} %get-tuple-element.11.grid_t_ref, ...), custom_call_target="tpu_custom_call" | custom-call | flops 6879707136 | bytes 3981312 | tf_op jit(solution)/shard_map/coupling/pallas_call | solution.py:612
  76.9 5.6 %all-to-all-start.1 = ((f32[4,3,8,288]{3,2,1,0:T(8,128)}), f32[4,3,8,288]{3,2,1,0:T(8,128)S(1)}, u32[]{:S(2)}, u32[]{:S(2)}) async-start(f32[4,3,8,288]{3,2,1,0:T(8,128)} %bitcast.25), calls=%async_computation.1 | async-start | bytes 294912 | tf_op jit(solution)/shard_map/all_to_all | solution.py:671
  82.5 49.0 %coupling.3 = f32[12,16,288]{2,1,0:T(8,128)} custom-call(s32[12]{0:T(128)} %get-tuple-element.8.partner_ref, f32[12]{0:T(128)} %get-tuple-element.9.weight_ref, f32[12]{0:T(128)} %copy-done.3, bf16[12,288,256]{2,1,0:T(8,128)(2,1)} %get-tuple-element.10.grid_ref, bf16[12,288,384]{2,1,0:T(8,128)(2,1)} %get-tuple-element.11.grid_t_ref, ...), custom_call_target="tpu_custom_call" | custom-call | flops 13759414272 | bytes 7962624 | tf_op jit(solution)/shard_map/coupling/pallas_call | solution.py:612
  131.5 5.1 %all-to-all-start.3 = ((f32[4,3,16,288]{3,2,1,0:T(8,128)}), f32[4,3,16,288]{3,2,1,0:T(8,128)S(1)}, u32[]{:S(2)}, u32[]{:S(2)}) async-start(f32[4,3,16,288]{3,2,1,0:T(8,128)} %bitcast.24), calls=%async_computation.3 | async-start | bytes 589824 | tf_op jit(solution)/shard_map/all_to_all | solution.py:671
  136.6 9.7 %all-to-all-done.3 = f32[4,3,16,288]{3,2,1,0:T(8,128)S(1)} async-done(((f32[4,3,16,288]{3,2,1,0:T(8,128)}), f32[4,3,16,288]{3,2,1,0:T(8,128)S(1)}, u32[]{:S(2)}, u32[]{:S(2)}) %all-to-all-start.3) | async-done | bytes 221216 | tf_op jit(solution)/shard_map/all_to_all | solution.py:671
  146.3 0.1 pad_maximum_fusion.2
  146.4 0.6 reshape.69
  147.1 0.8 reshape.70
  (22 shorter events, 0.2 us)
Async XLA Ops:
  7.2 36.5 %all-gather.3.cloned.1.call-start = ((), (), s32[]{:S(2)}) async-start(), calls=%async_computation.4 | async-start | bytes 2433024 | tf_op jit(solution)/shard_map/all_gather | solution.py:649
  9.7 14.5 %copy-start.2 = (bf16[288]{0:T(512)(128)(2,1)S(1)}, bf16[288]{0:T(512)(128)(2,1)}, u32[]{:S(2)}) copy-start(bf16[288]{0:T(512)(128)(2,1)} %param.8) | copy-start | bytes 1732
  20.0 18.5 %all-to-all-start = ((bf16[4,7,72,256]{3,2,1,0:T(8,128)(2,1)}), bf16[4,7,72,256]{3,2,1,0:T(8,128)(2,1)S(1)}, u32[]{:S(2)}, u32[]{:S(2)}) async-start(bf16[4,7,72,256]{3,2,1,0:T(8,128)(2,1)} %project.2), calls=%async_computation | async-start | bytes 2064384 | tf_op jit(solution)/shard_map/all_to_all | solution.py:657
  38.5 10.4 %copy-start.1 = (bf16[4,7,72,256]{3,2,1,0:T(8,128)(2,1)}, bf16[4,7,72,256]{3,2,1,0:T(8,128)(2,1)S(1)}, u32[]{:S(2)}) copy-start(bf16[4,7,72,256]{3,2,1,0:T(8,128)(2,1)S(1)} %all-to-all-done.moved_ref) | copy-start | bytes 3096580
  38.5 38.4 %all-to-all-start.2 = ((bf16[4,14,72,256]{3,2,1,0:T(8,128)(2,1)}), bf16[4,14,72,256]{3,2,1,0:T(8,128)(2,1)S(1)}, u32[]{:S(2)}, u32[]{:S(2)}) async-start(bf16[4,14,72,256]{3,2,1,0:T(8,128)(2,1)} %project.3), calls=%async_computation.2 | async-start | bytes 4128768 | tf_op jit(solution)/shard_map/all_to_all | solution.py:657
  42.2 34.7 %copy-start.3 = (f32[12]{0:T(128)}, f32[12]{0:T(128)S(1)}, u32[]{:S(2)}) copy-start(f32[12]{0:T(128)S(1)} %slice_bitcast_fusion.home_ref) | copy-start | bytes 148
  42.3 6.6 %copy-start.4 = (f32[6]{0:T(128)}, f32[6]{0:T(128)S(1)}, u32[]{:S(2)}) copy-start(f32[6]{0:T(128)S(1)} %slice_bitcast_fusion.1.home_ref) | copy-start | bytes 76
  76.9 5.6 %copy-start = (bf16[4,14,72,256]{3,2,1,0:T(8,128)(2,1)}, bf16[4,14,72,256]{3,2,1,0:T(8,128)(2,1)S(1)}, u32[]{:S(2)}) copy-start(bf16[4,14,72,256]{3,2,1,0:T(8,128)(2,1)S(1)} %all-to-all-done.2.moved_ref) | copy-start | bytes 6193156
  76.9 54.6 %all-to-all-start.1 = ((f32[4,3,8,288]{3,2,1,0:T(8,128)}), f32[4,3,8,288]{3,2,1,0:T(8,128)S(1)}, u32[]{:S(2)}, u32[]{:S(2)}) async-start(f32[4,3,8,288]{3,2,1,0:T(8,128)} %bitcast.25), calls=%async_computation.1 | async-start | bytes 294912 | tf_op jit(solution)/shard_map/all_to_all | solution.py:671
  131.5 14.8 %all-to-all-start.3 = ((f32[4,3,16,288]{3,2,1,0:T(8,128)}), f32[4,3,16,288]{3,2,1,0:T(8,128)S(1)}, u32[]{:S(2)}, u32[]{:S(2)}) async-start(f32[4,3,16,288]{3,2,1,0:T(8,128)} %bitcast.24), calls=%async_computation.3 | async-start | bytes 589824 | tf_op jit(solution)/shard_map/all_to_all | solution.py:671
Sparse Core Ops, SparseCore 0:
  10.2 32.3 all-gather.2

commit v10 on v8

--- a/solution.py
+++ b/solution.py
@@ -140,11 +140,10 @@
     ).astype(BF16)
 
 
-def pack_kernel(part_ref, partner_ref, weight_ref, grid_ref, freq_ref, upper_ref, lower_ref):
+def pack_kernel(part_ref, partner_ref, weight_ref, grid_ref, freq_ref, out_ref):
     own_pairs, modes, _ = grid_ref.shape
     rest = modes - MAIN
     lines = rest // 2
-    cut = upper_ref.shape[1]
     part = part_ref[0]
     line = lax.broadcasted_iota(jnp.int32, (lines, modes), 0)
     column = lax.broadcasted_iota(jnp.int32, (lines, modes), 1)
@@ -163,8 +162,7 @@
 
             @pl.when(part == p)
             def _():
-                upper_ref[s] = grid_ref[s, :cut, p * TILE : (p + 1) * TILE]
-                lower_ref[s, : modes - cut, :] = grid_ref[s, cut:, p * TILE : (p + 1) * TILE]
+                out_ref[s, :modes, :] = grid_ref[s, :, p * TILE : (p + 1) * TILE]
 
         turned = dot_nt(select, grid_ref[s])
         turned = (
@@ -173,42 +171,40 @@
             jnp.concatenate([turned[:, MAIN:], jnp.zeros((lines, TILE - rest), F32)], axis=1),
         )
         for h in range(3):
-            start = modes - cut + h * lines
-            lower_ref[s, start : start + lines, :] = turned[h].astype(BF16)
+            start = modes + h * lines
+            out_ref[s, start : start + lines, :] = turned[h].astype(BF16)
         pair = partner_ref[s].astype(F32)
         weight = weight_ref[s].astype(F32)
         side = jnp.where(lane16 == 0, pair, jnp.where(lane16 == 1, weight, 0.0))
         side = jnp.where(line16 == 3, side, 0.0)
         for h in range(3):
             side = jnp.where(line16 == h, freq_tiles[h][s : s + 1], side)
-        start = modes - cut + 3 * lines
-        lower_ref[s, start : start + 16, :] = side.astype(BF16)
+        start = modes + 3 * lines
+        out_ref[s, start : start + 16, :] = side.astype(BF16)
 
 
 def pack_own(part, partner, weights, grid_vectors, partner_frequencies):
     own_pairs, modes, _ = grid_vectors.shape
     smem = pl.BlockSpec(memory_space=pltpu.SMEM)
     vmem = pl.BlockSpec(memory_space=pltpu.VMEM)
-    rows = (modes + 3 * (modes - MAIN) // 2 + 16) // 2
-    shape = jax.ShapeDtypeStruct((own_pairs, rows, TILE), BF16)
+    rows = modes + 3 * (modes - MAIN) // 2 + 16
     return pl.pallas_call(
         pack_kernel,
         in_specs=[smem, smem, smem, vmem, vmem],
-        out_specs=[vmem] * 2,
-        out_shape=[shape] * 2,
+        out_specs=vmem,
+        out_shape=jax.ShapeDtypeStruct((own_pairs, rows, TILE), BF16),
         compiler_params=pltpu.CompilerParams(vmem_limit_bytes=VMEM_BYTES),
         name="pack_own",
     )(part, partner, weights, grid_vectors, partner_frequencies)
 
 
 def arrange_kernel(
-    upper_ref, lower_ref, partner_ref, weight_ref, grid_ref, grid_t_ref, freq_row_ref, freq_col_ref
+    pack_ref, partner_ref, weight_ref, grid_ref, grid_t_ref, freq_row_ref, freq_col_ref
 ):
-    owners, parts, each, cut, _ = upper_ref.shape
+    owners, parts, each, rows, _ = pack_ref.shape
     modes = grid_ref.shape[1]
     rest = modes - MAIN
     lines = rest // parts
-    left = modes - cut
     eye = identity(MAIN)
     source = lax.broadcasted_iota(jnp.int32, (TILE, TILE), 0)
     place = lax.broadcasted_iota(jnp.int32, (TILE, TILE), 1)
@@ -223,17 +219,15 @@
         for s in range(each):
             x = q * each + s
             for part in range(parts):
-                lanes = slice(part * TILE, (part + 1) * TILE)
-                grid_ref[x, :cut, lanes] = upper_ref[q, part, s]
-                grid_ref[x, cut:, lanes] = lower_ref[q, part, s, :left, :]
+                grid_ref[x, :, part * TILE : (part + 1) * TILE] = pack_ref[q, part, s, :modes, :]
                 for h in range(3):
-                    start, width = left + h * lines, min(TILE, modes - h * TILE)
-                    piece = lower_ref[q, part, s, start : start + lines, :]
+                    start, width = modes + h * lines, min(TILE, modes - h * TILE)
+                    piece = pack_ref[q, part, s, start : start + lines, :]
                     grid_t_ref[
                         x, MAIN + part * lines : MAIN + (part + 1) * lines, h * TILE : h * TILE + width
                     ] = piece[:, :width]
             grid_t_ref[x, :MAIN, :] = dot_nt(eye, grid_ref[x]).astype(BF16)
-            side = lower_ref[q, 0, s, left + 3 * lines : left + 3 * lines + 16, :]
+            side = pack_ref[q, 0, s, modes + 3 * lines : modes + 3 * lines + 16, :]
             wide = side.astype(F32)
             freq_row_ref[x, :, :TILE] = wide[0:1]
             freq_row_ref[x, :, TILE:MAIN] = wide[1:2]
@@ -255,14 +249,14 @@
     lax.fori_loop(0, owners, one, 0, unroll=owners <= 4)
 
 
-def arrange(packs, modes):
-    owners, parts, each, _, _ = packs[0].shape
+def arrange(pack, modes):
+    owners, parts, each, _, _ = pack.shape
     pairs = owners * each
     smem = pl.BlockSpec(memory_space=pltpu.SMEM)
     vmem = pl.BlockSpec(memory_space=pltpu.VMEM)
     return pl.pallas_call(
         arrange_kernel,
-        in_specs=[vmem] * 2,
+        in_specs=[vmem],
         out_specs=[smem, smem, vmem, vmem, vmem, vmem],
         out_shape=[
             jax.ShapeDtypeStruct((pairs,), jnp.int32),
@@ -274,7 +268,7 @@
         ],
         compiler_params=pltpu.CompilerParams(vmem_limit_bytes=VMEM_BYTES),
         name="arrange",
-    )(*packs)
+    )(pack)
 
 
 def interleave(heavy, light):
@@ -300,7 +294,6 @@
     grid_t_ref,
     freq_row_ref,
     freq_col_ref,
-    home_row_ref,
     moved_ref,
     out_ref,
     turned_ref,
@@ -308,6 +301,7 @@
     inner_rest_ref,
     pick_ref,
     rest_value_ref,
+    home_row_ref,
     *work,
 ):
     gathers, inners, values, tabs, sums, rest_sums, firsts = (
@@ -324,6 +318,14 @@
 
     for x in range(pairs):
         grid_rest_ref[x * rest : (x + 1) * rest, :] = grid_t_ref[x, MAIN:, :]
+    spot = lax.broadcasted_iota(jnp.int32, (1, rest_lanes), 1) // rest
+    row = jnp.ones((1, rest_lanes), F32)
+    for r in range(share):
+        row = jnp.where(spot == r, home_ref[r], row)
+    home_row_ref[0:1, :] = row
+    home_row_ref[1:2, :] = row * row - s2
+    home_row_ref[2:3, :] = (4.0 * s2) * (row * row)
+    home_row_ref[3:4, :] = 1.0 / row
     eye = identity(modes)
     if share * rest < rest_lanes:
         inner_rest_ref[...] = jnp.zeros_like(inner_rest_ref)
@@ -551,10 +553,6 @@
     share = home.shape[0]
     rest = modes - MAIN
     rest_lanes = ceil_div(share * rest, TILE) * TILE
-    row = jnp.repeat(home, rest)
-    row = jnp.pad(row, (0, rest_lanes - share * rest), constant_values=1.0)
-    s2 = smearing * smearing
-    home_row = jnp.stack([row, row * row - s2, (4.0 * s2) * (row * row), 1.0 / row])
     padded = (share // 8 + 1) * 8
     smem = pl.BlockSpec(memory_space=pltpu.SMEM)
     vmem = pl.BlockSpec(memory_space=pltpu.VMEM)
@@ -567,6 +565,7 @@
             pltpu.VMEM((pairs, rest_lanes, modes), BF16),
             pltpu.VMEM((rest_lanes, TILE), BF16),
             pltpu.VMEM((modes, rest_lanes), F32),
+            pltpu.VMEM((8, rest_lanes), F32),
         ]
         + [pltpu.VMEM((modes, modes), F32)] * 2
         + [pltpu.VMEM((modes, block * MAIN), BF16)] * 2
@@ -578,7 +577,7 @@
     )
     return pl.pallas_call(
         functools.partial(coupling_kernel, share, block),
-        in_specs=[smem, smem, smem, vmem, vmem, vmem, vmem, vmem, vmem],
+        in_specs=[smem, smem, smem, vmem, vmem, vmem, vmem, vmem],
         out_specs=vmem,
         out_shape=jax.ShapeDtypeStruct((pairs, padded, modes), F32),
         scratch_shapes=scratch,
@@ -589,7 +588,7 @@
             transcendentals=2 * share * pairs * modes**2,
         ),
         name="coupling",
-    )(partner, weights, home, grid, grid_t, freq_rows, freq_cols, home_row, moved)
+    )(partner, weights, home, grid, grid_t, freq_rows, freq_cols, moved)
 
 
 def local(
@@ -612,9 +611,9 @@
 
     assert n_fc * TILE == MAIN
     own_part = lax.axis_index("fc").astype(jnp.int32)[None]
-    packs = pack_own(own_part, partner, weights, grid_vectors, partner_frequencies)
-    packs = [lax.all_gather(half, ("qp", "fc"), axis=0) for half in packs]
-    packs = [half.reshape(n_qp, n_fc, own_pairs, half.shape[2], TILE) for half in packs]
+    pack = pack_own(own_part, partner, weights, grid_vectors, partner_frequencies)
+    pack = lax.all_gather(pack, ("qp", "fc"), axis=0)
+    pack = pack.reshape(n_qp, n_fc, own_pairs, pack.shape[2], TILE)
 
     here_word = here.astype(jnp.int32)[None]
     moved = []
@@ -629,7 +628,7 @@
     home = jnp.pad(home, ((0, 0), (0, share * n_qp - group)), constant_values=1.0)
     home = lax.dynamic_slice(home, (own, here * share), (1, share)).reshape(share)
 
-    shared = arrange(packs, modes)
+    shared = arrange(pack, modes)
     parts, widths = [], []
     for (first, count), block in zip(chunks, moved):
         found = coupling(

time: 165 us -> 153 us (0.927)
  waiting for transfers between devices: 27.7 us -> 12.9 us
  starting transfers between devices: 16.4 us -> 18.6 us
    all_gather x2 -> x1, waiting for transfers between devices: 14.3 us -> 0.01 us  [local(): pack = lax.all_gather(pack, ('qp', 'fc'), axis=0)]
    all_to_all x2, starting transfers between devices: 8.39 us -> 10.7 us  [local(): lax.all_to_all(found.reshape(n_qp, own_pairs, found.shape[1], modes), 'qp...]
  transfers between devices with their start and end apart: 6 -> 5, of which waited for: 3 -> 2; matrix products, arithmetic and copies ran while one was open for 1% -> 1% of each run, Pallas kernels for 61% -> 66%
where the time goes in v10:
time: 153 us; the launch traced here: 152 us
  Pallas kernels  103 us (67%)
  starting transfers between devices  18.6 us (12%)
  between operations  14.1 us (9%)
  waiting for transfers between devices  12.9 us (8%)
  local copies, waits for them, and re-layouts  2.78 us (2%)
    pallas_call x2, Pallas kernels, coupling(): pl.pallas_call(functools.partial(coupling_kernel, share, block), in_specs...  74.4 us
    pallas_call x2, Pallas kernels, project(): pl.pallas_call(functools.partial(project_kernel, groups, group, share, fi...  21.4 us
    all_to_all x2, starting transfers between devices, local(): lax.all_to_all(found.reshape(n_qp, own_pairs, found.shape[1], modes), 'qp...  10.7 us
    all_to_all x2, waiting for transfers between devices, local(): lax.all_to_all(found.reshape(n_qp, own_pairs, found.shape[1], modes), 'qp...  9.7 us
    all_to_all x2, starting transfers between devices, local(): lax.all_to_all(sent, ('mode', 'fc'), split_axis=0, concat_axis=0, tiled=T...  7.83 us
    pallas_call x1, Pallas kernels, arrange(): pl.pallas_call(arrange_kernel, in_specs=[vmem], out_specs=[smem, smem, vm...  5.09 us
    all_to_all x2, waiting for transfers between devices, local(): lax.all_to_all(sent, ('mode', 'fc'), split_axis=0, concat_axis=0, tiled=T...  3.2 us
  transfers between devices with their start and end apart: 5, of which 2 were waited for; matrix products, arithmetic and copies ran while one was open for 1% of the time, Pallas kernels for 66%

profile of v10, /device:TPU:0, one launch (start us, length us, event | category | flops | bytes accessed | tf_op | source)
XLA Modules:
  0.0 151.8 jit_solution(13009800913416937438)
XLA Ops:
  7.2 0.0 all-gather.3.cloned.1.call-start
  7.2 2.5 %pack_own.1 = bf16[3,352,128]{2,1,0:T(8,128)(2,1)} custom-call(s32[1]{0:T(128)} %bitcast.part_ref, s32[3]{0:T(128)} %partner_ref.1, s32[3]{0:T(128)} %weight_ref.1, bf16[3,288,288]{2,1,0:T(8,128)(2,1)} %grid_ref.1, bf16[3,288]{1,0:T(4,128)(2,1)} %freq_ref.1), custom_call_target="tpu_custom_call" | custom-call | tf_op jit(solution)/shard_map/pack_own/pallas_call | solution.py:191
  9.7 0.0 all-gather.3.cloned.1.call-update
  9.7 10.3 %project.2 = bf16[4,7,72,256]{3,2,1,0:T(8,128)(2,1)} custom-call(s32[1]{0:T(128)} %bitcast.3.here_ref, bf16[288,288]{1,0:T(8,128)(2,1)} %home_ref.3, bf16[288,20736]{1,0:T(8,128)(2,1)} %refs_2_.3, bf16[288,20736]{1,0:T(8,128)(2,1)} %refs_2_.3, bf16[288,20736]{1,0:T(8,128)(2,1)} %refs_2_.3), custom_call_target="tpu_custom_call" | custom-call | flops 286654464 | bytes 11943936 | tf_op jit(solution)/shard_map/project/pallas_call | solution.py:111
  20.0 4.2 %all-to-all-start = ((bf16[4,7,72,256]{3,2,1,0:T(8,128)(2,1)}), bf16[4,7,72,256]{3,2,1,0:T(8,128)(2,1)S(1)}, u32[]{:S(2)}, u32[]{:S(2)}) async-start(bf16[4,7,72,256]{3,2,1,0:T(8,128)(2,1)} %project.2), calls=%async_computation | async-start | bytes 2064384 | tf_op jit(solution)/shard_map/all_to_all | solution.py:623
  24.2 11.1 %project.3 = bf16[4,14,72,256]{3,2,1,0:T(8,128)(2,1)} custom-call(s32[1]{0:T(128)} %bitcast.3.here_ref, bf16[288,288]{1,0:T(8,128)(2,1)} %home_ref.3, bf16[288,20736]{1,0:T(8,128)(2,1)} %refs_2_.3, bf16[288,20736]{1,0:T(8,128)(2,1)} %refs_2_.3, bf16[288,20736]{1,0:T(8,128)(2,1)} %refs_2_.3), custom_call_target="tpu_custom_call" | custom-call | flops 573308928 | bytes 11943936 | tf_op jit(solution)/shard_map/project/pallas_call | solution.py:111
  35.3 3.2 %all-to-all-done.moved_ref = bf16[4,7,72,256]{3,2,1,0:T(8,128)(2,1)S(1)} async-done(((bf16[4,7,72,256]{3,2,1,0:T(8,128)(2,1)}), bf16[4,7,72,256]{3,2,1,0:T(8,128)(2,1)S(1)}, u32[]{:S(2)}, u32[]{:S(2)}) %all-to-all-start) | async-done | bytes 1032224 | tf_op jit(solution)/shard_map/all_to_all | solution.py:623
  38.5 3.6 %all-to-all-start.2 = ((bf16[4,14,72,256]{3,2,1,0:T(8,128)(2,1)}), bf16[4,14,72,256]{3,2,1,0:T(8,128)(2,1)S(1)}, u32[]{:S(2)}, u32[]{:S(2)}) async-start(bf16[4,14,72,256]{3,2,1,0:T(8,128)(2,1)} %project.3), calls=%async_computation.2 | async-start | bytes 4128768 | tf_op jit(solution)/shard_map/all_to_all | solution.py:623
  42.1 0.1 reshape.36
  42.2 0.1 dynamic_slice.3
  42.3 0.7 slice_bitcast_fusion.home_ref
  42.9 0.5 slice_bitcast_fusion.1.home_ref
  43.5 5.1 %arrange.1 = (s32[12]{0:T(128)}, f32[12]{0:T(128)}, bf16[12,288,256]{2,1,0:T(8,128)(2,1)}, bf16[12,288,288]{2,1,0:T(8,128)(2,1)}, f32[12,1,384]{2,1,0:T(1,128)}, /*index=5*/f32[288,128]{1,0:T(8,128)}) custom-call(bf16[4,2,3,352,128]{4,3,2,1,0:T(8,128)(2,1)} %bitcast.17), custom_call_target="tpu_custom_call" | custom-call | tf_op jit(solution)/shard_map/arrange/pallas_call | solution.py:257
  48.6 27.9 %coupling.2 = f32[12,8,288]{2,1,0:T(8,128)} custom-call(s32[12]{0:T(128)} %get-tuple-element.8.partner_ref, f32[12]{0:T(128)} %get-tuple-element.9.weight_ref, f32[6]{0:T(128)} %slice_bitcast_fusion.1.home_ref, bf16[12,288,256]{2,1,0:T(8,128)(2,1)} %get-tuple-element.10.grid_ref, bf16[12,288,288]{2,1,0:T(8,128)(2,1)} %get-tuple-element.11.grid_t_ref, ...), custom_call_target="tpu_custom_call" | custom-call | flops 6879707136 | bytes 3981312 | tf_op jit(solution)/shard_map/coupling/pallas_call | solution.py:578
  76.5 0.0 all-to-all-done.2.moved_ref
  76.5 5.6 %all-to-all-start.1 = ((f32[4,3,8,288]{3,2,1,0:T(8,128)}), f32[4,3,8,288]{3,2,1,0:T(8,128)S(1)}, u32[]{:S(2)}, u32[]{:S(2)}) async-start(f32[4,3,8,288]{3,2,1,0:T(8,128)} %bitcast.21), calls=%async_computation.1 | async-start | bytes 294912 | tf_op jit(solution)/shard_map/all_to_all | solution.py:637
  82.1 46.5 %coupling.3 = f32[12,16,288]{2,1,0:T(8,128)} custom-call(s32[12]{0:T(128)} %get-tuple-element.8.partner_ref, f32[12]{0:T(128)} %get-tuple-element.9.weight_ref, f32[12]{0:T(128)} %slice_bitcast_fusion.home_ref, bf16[12,288,256]{2,1,0:T(8,128)(2,1)} %get-tuple-element.10.grid_ref, bf16[12,288,288]{2,1,0:T(8,128)(2,1)} %get-tuple-element.11.grid_t_ref, ...), custom_call_target="tpu_custom_call" | custom-call | flops 13759414272 | bytes 7962624 | tf_op jit(solution)/shard_map/coupling/pallas_call | solution.py:578
  128.7 0.0 all-to-all-done.1
  128.7 5.1 %all-to-all-start.3 = ((f32[4,3,16,288]{3,2,1,0:T(8,128)}), f32[4,3,16,288]{3,2,1,0:T(8,128)S(1)}, u32[]{:S(2)}, u32[]{:S(2)}) async-start(f32[4,3,16,288]{3,2,1,0:T(8,128)} %bitcast.20), calls=%async_computation.3 | async-start | bytes 589824 | tf_op jit(solution)/shard_map/all_to_all | solution.py:637
  133.7 9.7 %all-to-all-done.3 = f32[4,3,16,288]{3,2,1,0:T(8,128)S(1)} async-done(((f32[4,3,16,288]{3,2,1,0:T(8,128)}), f32[4,3,16,288]{3,2,1,0:T(8,128)S(1)}, u32[]{:S(2)}, u32[]{:S(2)}) %all-to-all-start.3) | async-done | bytes 221216 | tf_op jit(solution)/shard_map/all_to_all | solution.py:637
  143.4 0.1 pad_maximum_fusion
  143.5 0.6 reshape.33
  144.1 0.1 maximum_bitcast_fusion
  144.2 0.8 reshape.34
  (10 shorter events, 0.1 us)
Async XLA Ops:
  7.2 36.3 %all-gather.3.cloned.1.call-start = ((), (), s32[]{:S(2)}) async-start(), calls=%async_computation.4 | async-start | bytes 2433024 | tf_op jit(solution)/shard_map/all_gather | solution.py:615
  20.0 18.5 %all-to-all-start = ((bf16[4,7,72,256]{3,2,1,0:T(8,128)(2,1)}), bf16[4,7,72,256]{3,2,1,0:T(8,128)(2,1)S(1)}, u32[]{:S(2)}, u32[]{:S(2)}) async-start(bf16[4,7,72,256]{3,2,1,0:T(8,128)(2,1)} %project.2), calls=%async_computation | async-start | bytes 2064384 | tf_op jit(solution)/shard_map/all_to_all | solution.py:623
  35.3 6.8 %copy-start.2 = (bf16[288]{0:T(512)(128)(2,1)S(1)}, bf16[288]{0:T(512)(128)(2,1)}, u32[]{:S(2)}) copy-start(bf16[288]{0:T(512)(128)(2,1)} %param.8) | copy-start | bytes 1732
  38.5 10.1 %copy-start.1 = (bf16[4,7,72,256]{3,2,1,0:T(8,128)(2,1)}, bf16[4,7,72,256]{3,2,1,0:T(8,128)(2,1)S(1)}, u32[]{:S(2)}) copy-start(bf16[4,7,72,256]{3,2,1,0:T(8,128)(2,1)S(1)} %all-to-all-done.moved_ref) | copy-start | bytes 3096580
  38.5 38.0 %all-to-all-start.2 = ((bf16[4,14,72,256]{3,2,1,0:T(8,128)(2,1)}), bf16[4,14,72,256]{3,2,1,0:T(8,128)(2,1)S(1)}, u32[]{:S(2)}, u32[]{:S(2)}) async-start(bf16[4,14,72,256]{3,2,1,0:T(8,128)(2,1)} %project.3), calls=%async_computation.2 | async-start | bytes 4128768 | tf_op jit(solution)/shard_map/all_to_all | solution.py:623
  76.5 5.6 %copy-start = (bf16[4,14,72,256]{3,2,1,0:T(8,128)(2,1)}, bf16[4,14,72,256]{3,2,1,0:T(8,128)(2,1)S(1)}, u32[]{:S(2)}) copy-start(bf16[4,14,72,256]{3,2,1,0:T(8,128)(2,1)S(1)} %all-to-all-done.2.moved_ref) | copy-start | bytes 6193156
  76.5 52.1 %all-to-all-start.1 = ((f32[4,3,8,288]{3,2,1,0:T(8,128)}), f32[4,3,8,288]{3,2,1,0:T(8,128)S(1)}, u32[]{:S(2)}, u32[]{:S(2)}) async-start(f32[4,3,8,288]{3,2,1,0:T(8,128)} %bitcast.21), calls=%async_computation.1 | async-start | bytes 294912 | tf_op jit(solution)/shard_map/all_to_all | solution.py:637
  128.7 14.8 %all-to-all-start.3 = ((f32[4,3,16,288]{3,2,1,0:T(8,128)}), f32[4,3,16,288]{3,2,1,0:T(8,128)S(1)}, u32[]{:S(2)}, u32[]{:S(2)}) async-start(f32[4,3,16,288]{3,2,1,0:T(8,128)} %bitcast.20), calls=%async_computation.3 | async-start | bytes 589824 | tf_op jit(solution)/shard_map/all_to_all | solution.py:637
Sparse Core Ops, SparseCore 0:
  10.2 32.3 all-gather.2

commit v11 on v10

--- a/solution.py
+++ b/solution.py
@@ -285,13 +285,14 @@
 
 
 def coupling_kernel(
+    first,
     share,
     block,
     partner_ref,
     weight_ref,
     home_ref,
-    grid_ref,
-    grid_t_ref,
+    grid_source,
+    grid_t_source,
     freq_row_ref,
     freq_col_ref,
     moved_ref,
@@ -302,6 +303,9 @@
     pick_ref,
     rest_value_ref,
     home_row_ref,
+    grid_ref,
+    grid_t_ref,
+    copy_sem,
     *work,
 ):
     gathers, inners, values, tabs, sums, rest_sums, firsts = (
@@ -316,12 +320,14 @@
     s2 = smearing * smearing
     steps = share // block
 
-    for x in range(pairs):
-        grid_rest_ref[x * rest : (x + 1) * rest, :] = grid_t_ref[x, MAIN:, :]
+    fetch_turned = pltpu.make_async_copy(grid_t_source, grid_t_ref, copy_sem.at[0])
+    fetch_grid = pltpu.make_async_copy(grid_source, grid_ref, copy_sem.at[1])
+    fetch_turned.start()
+    fetch_grid.start()
     spot = lax.broadcasted_iota(jnp.int32, (1, rest_lanes), 1) // rest
     row = jnp.ones((1, rest_lanes), F32)
     for r in range(share):
-        row = jnp.where(spot == r, home_ref[r], row)
+        row = jnp.where(spot == r, home_ref[first + r], row)
     home_row_ref[0:1, :] = row
     home_row_ref[1:2, :] = row * row - s2
     home_row_ref[2:3, :] = (4.0 * s2) * (row * row)
@@ -341,9 +347,16 @@
             gather_ref[s * depth : (s + 1) * depth, MAIN:] = tail[:, :rest]
         whole = gather_ref[...].astype(BF16)
         turned_ref[r * modes : (r + 1) * modes, :] = dot_nt(eye, whole).astype(BF16)
-        found = dot_nn(grid_rest_ref[...], whole).astype(BF16)
+
+    fetch_turned.wait()
+    for x in range(pairs):
+        grid_rest_ref[x * rest : (x + 1) * rest, :] = grid_t_ref[x, MAIN:, :]
+    for r in range(share):
+        found = dot_nt(grid_rest_ref[...], turned_ref[r * modes : (r + 1) * modes, :]).astype(BF16)
         for x in range(pairs):
             inner_rest_ref[x, r * rest : (r + 1) * rest, :] = found[x * rest : (x + 1) * rest, :]
+
+    fetch_grid.wait()
 
     row_id = lax.broadcasted_iota(jnp.int32, pick_ref.shape, 0)
     col_id = lax.broadcasted_iota(jnp.int32, pick_ref.shape, 1)
@@ -379,7 +392,7 @@
         state = {}
 
         def begin():
-            state["w"] = [home_ref[step * block + b] for b in range(block)]
+            state["w"] = [home_ref[first + step * block + b] for b in range(block)]
             state["c1"] = [w * w - s2 for w in state["w"]]
             state["c2"] = [(4.0 * s2) * (w * w) for w in state["w"]]
             state["total"] = [jnp.zeros((8, MAIN), F32) for _ in range(block)]
@@ -548,9 +561,8 @@
     )
 
 
-def coupling(partner, weights, home, grid, grid_t, freq_rows, freq_cols, moved):
+def coupling(first, share, partner, weights, home, grid, grid_t, freq_rows, freq_cols, moved):
     pairs, modes = grid.shape[0], grid.shape[1]
-    share = home.shape[0]
     rest = modes - MAIN
     rest_lanes = ceil_div(share * rest, TILE) * TILE
     padded = (share // 8 + 1) * 8
@@ -566,6 +578,9 @@
             pltpu.VMEM((rest_lanes, TILE), BF16),
             pltpu.VMEM((modes, rest_lanes), F32),
             pltpu.VMEM((8, rest_lanes), F32),
+            pltpu.VMEM(grid.shape, BF16),
+            pltpu.VMEM(grid_t.shape, BF16),
+            pltpu.SemaphoreType.DMA((2,)),
         ]
         + [pltpu.VMEM((modes, modes), F32)] * 2
         + [pltpu.VMEM((modes, block * MAIN), BF16)] * 2
@@ -576,8 +591,8 @@
         + [pltpu.VMEM((padded, modes), F32)] * 2
     )
     return pl.pallas_call(
-        functools.partial(coupling_kernel, share, block),
-        in_specs=[smem, smem, smem, vmem, vmem, vmem, vmem, vmem],
+        functools.partial(coupling_kernel, first, share, block),
+        in_specs=[smem] * 3 + [pl.BlockSpec(memory_space=pl.ANY)] * 2 + [vmem] * 3,
         out_specs=vmem,
         out_shape=jax.ShapeDtypeStruct((pairs, padded, modes), F32),
         scratch_shapes=scratch,
@@ -632,7 +647,7 @@
     parts, widths = [], []
     for (first, count), block in zip(chunks, moved):
         found = coupling(
-            shared[0], shared[1], home[first : first + count], *shared[2:], block
+            first, count, shared[0], shared[1], home, *shared[2:], block
         )
         back = lax.all_to_all(
             found.reshape(n_qp, own_pairs, found.shape[1], modes),

time: 153 us -> 152 us (level)
  transfers between devices with their start and end apart: 5 -> 5, of which waited for: 2 -> 2; matrix products, arithmetic and copies ran while one was open for 1% -> 0% of each run, Pallas kernels for 66% -> 67%
where the time goes in v11:
time: 152 us; the launch traced here: 151 us
  Pallas kernels  103 us (68%)
  starting transfers between devices  18.6 us (12%)
  between operations  14.1 us (9%)
  waiting for transfers between devices  12.9 us (8%)
  local copies, waits for them, and re-layouts  2.15 us (1%)
    pallas_call x2, Pallas kernels, coupling(): pl.pallas_call(functools.partial(coupling_kernel, first, share, block), i...  74.2 us
    pallas_call x2, Pallas kernels, project(): pl.pallas_call(functools.partial(project_kernel, groups, group, share, fi...  21.3 us
    all_to_all x2, starting transfers between devices, local(): lax.all_to_all(found.reshape(n_qp, own_pairs, found.shape[1], modes), 'qp...  10.7 us
    all_to_all x2, waiting for transfers between devices, local(): lax.all_to_all(found.reshape(n_qp, own_pairs, found.shape[1], modes), 'qp...  9.68 us
    all_to_all x2, starting transfers between devices, local(): lax.all_to_all(sent, ('mode', 'fc'), split_axis=0, concat_axis=0, tiled=T...  7.83 us
    pallas_call x1, Pallas kernels, arrange(): pl.pallas_call(arrange_kernel, in_specs=[vmem], out_specs=[smem, smem, vm...  5.07 us
    all_to_all x2, waiting for transfers between devices, local(): lax.all_to_all(sent, ('mode', 'fc'), split_axis=0, concat_axis=0, tiled=T...  3.2 us
  transfers between devices with their start and end apart: 5, of which 2 were waited for; matrix products, arithmetic and copies ran while one was open for 0% of the time, Pallas kernels for 67%

profile of v11, /device:TPU:0, one launch (start us, length us, event | category | flops | bytes accessed | tf_op | source)
XLA Modules:
  0.0 151.0 jit_solution(8404916427140233022)
XLA Ops:
  7.2 0.0 all-gather.3.cloned.1.call-start
  7.2 2.5 %pack_own.1 = bf16[3,352,128]{2,1,0:T(8,128)(2,1)} custom-call(s32[1]{0:T(128)} %bitcast.part_ref, s32[3]{0:T(128)} %partner_ref.1, s32[3]{0:T(128)} %weight_ref.1, bf16[3,288,288]{2,1,0:T(8,128)(2,1)} %grid_ref.1, bf16[3,288]{1,0:T(4,128)(2,1)} %freq_ref.1), custom_call_target="tpu_custom_call" | custom-call | tf_op jit(solution)/shard_map/pack_own/pallas_call | solution.py:191
  9.7 0.0 all-gather.3.cloned.1.call-update
  9.7 10.3 %project.2 = bf16[4,7,72,256]{3,2,1,0:T(8,128)(2,1)} custom-call(s32[1]{0:T(128)} %bitcast.3.here_ref, bf16[288,288]{1,0:T(8,128)(2,1)} %home_ref.3, bf16[288,20736]{1,0:T(8,128)(2,1)} %refs_2_.3, bf16[288,20736]{1,0:T(8,128)(2,1)} %refs_2_.3, bf16[288,20736]{1,0:T(8,128)(2,1)} %refs_2_.3), custom_call_target="tpu_custom_call" | custom-call | flops 286654464 | bytes 11943936 | tf_op jit(solution)/shard_map/project/pallas_call | solution.py:111
  20.0 4.2 %all-to-all-start = ((bf16[4,7,72,256]{3,2,1,0:T(8,128)(2,1)}), bf16[4,7,72,256]{3,2,1,0:T(8,128)(2,1)S(1)}, u32[]{:S(2)}, u32[]{:S(2)}) async-start(bf16[4,7,72,256]{3,2,1,0:T(8,128)(2,1)} %project.2), calls=%async_computation | async-start | bytes 2064384 | tf_op jit(solution)/shard_map/all_to_all | solution.py:638
  24.2 11.1 %project.3 = bf16[4,14,72,256]{3,2,1,0:T(8,128)(2,1)} custom-call(s32[1]{0:T(128)} %bitcast.3.here_ref, bf16[288,288]{1,0:T(8,128)(2,1)} %home_ref.3, bf16[288,20736]{1,0:T(8,128)(2,1)} %refs_2_.3, bf16[288,20736]{1,0:T(8,128)(2,1)} %refs_2_.3, bf16[288,20736]{1,0:T(8,128)(2,1)} %refs_2_.3), custom_call_target="tpu_custom_call" | custom-call | flops 573308928 | bytes 11943936 | tf_op jit(solution)/shard_map/project/pallas_call | solution.py:111
  35.3 3.2 %all-to-all-done.moved_ref = bf16[4,7,72,256]{3,2,1,0:T(8,128)(2,1)S(1)} async-done(((bf16[4,7,72,256]{3,2,1,0:T(8,128)(2,1)}), bf16[4,7,72,256]{3,2,1,0:T(8,128)(2,1)S(1)}, u32[]{:S(2)}, u32[]{:S(2)}) %all-to-all-start) | async-done | bytes 1032224 | tf_op jit(solution)/shard_map/all_to_all | solution.py:638
  38.5 3.6 %all-to-all-start.2 = ((bf16[4,14,72,256]{3,2,1,0:T(8,128)(2,1)}), bf16[4,14,72,256]{3,2,1,0:T(8,128)(2,1)S(1)}, u32[]{:S(2)}, u32[]{:S(2)}) async-start(bf16[4,14,72,256]{3,2,1,0:T(8,128)(2,1)} %project.3), calls=%async_computation.2 | async-start | bytes 4128768 | tf_op jit(solution)/shard_map/all_to_all | solution.py:638
  42.1 0.0 copy-done.2
  42.1 0.1 reshape.37
  42.2 0.7 dynamic-slice_bitcast_fusion.home_ref
  42.8 5.1 %arrange.1 = (s32[12]{0:T(128)}, f32[12]{0:T(128)}, bf16[12,288,256]{2,1,0:T(8,128)(2,1)}, bf16[12,288,288]{2,1,0:T(8,128)(2,1)}, f32[12,1,384]{2,1,0:T(1,128)}, /*index=5*/f32[288,128]{1,0:T(8,128)}) custom-call(bf16[4,2,3,352,128]{4,3,2,1,0:T(8,128)(2,1)} %bitcast.15), custom_call_target="tpu_custom_call" | custom-call | tf_op jit(solution)/shard_map/arrange/pallas_call | solution.py:257
  47.9 0.0 copy-done.1
  47.9 28.2 %coupling.2 = f32[12,8,288]{2,1,0:T(8,128)} custom-call(s32[12]{0:T(128)} %get-tuple-element.8.partner_ref, f32[12]{0:T(128)} %get-tuple-element.9.weight_ref, f32[18]{0:T(128)} %dynamic-slice_bitcast_fusion.home_ref, bf16[12,288,256]{2,1,0:T(8,128)(2,1)} %get-tuple-element.10.grid_source, bf16[12,288,288]{2,1,0:T(8,128)(2,1)} %get-tuple-element.11.grid_t_source, ...), custom_call_target="tpu_custom_call" | custom-call | flops 6879707136 | bytes 3981312 | tf_op jit(solution)/shard_map/coupling/pallas_call | solution.py:593
  76.2 0.0 all-to-all-done.2.moved_ref
  76.2 5.6 %all-to-all-start.1 = ((f32[4,3,8,288]{3,2,1,0:T(8,128)}), f32[4,3,8,288]{3,2,1,0:T(8,128)S(1)}, u32[]{:S(2)}, u32[]{:S(2)}) async-start(f32[4,3,8,288]{3,2,1,0:T(8,128)} %bitcast.19), calls=%async_computation.1 | async-start | bytes 294912 | tf_op jit(solution)/shard_map/all_to_all | solution.py:652
  81.8 46.0 %coupling.3 = f32[12,16,288]{2,1,0:T(8,128)} custom-call(s32[12]{0:T(128)} %get-tuple-element.8.partner_ref, f32[12]{0:T(128)} %get-tuple-element.9.weight_ref, f32[18]{0:T(128)} %dynamic-slice_bitcast_fusion.home_ref, bf16[12,288,256]{2,1,0:T(8,128)(2,1)} %get-tuple-element.10.grid_source, bf16[12,288,288]{2,1,0:T(8,128)(2,1)} %get-tuple-element.11.grid_t_source, ...), custom_call_target="tpu_custom_call" | custom-call | flops 13759414272 | bytes 7962624 | tf_op jit(solution)/shard_map/coupling/pallas_call | solution.py:593
  127.8 0.0 all-to-all-done.1
  127.8 5.1 %all-to-all-start.3 = ((f32[4,3,16,288]{3,2,1,0:T(8,128)}), f32[4,3,16,288]{3,2,1,0:T(8,128)S(1)}, u32[]{:S(2)}, u32[]{:S(2)}) async-start(f32[4,3,16,288]{3,2,1,0:T(8,128)} %bitcast.18), calls=%async_computation.3 | async-start | bytes 589824 | tf_op jit(solution)/shard_map/all_to_all | solution.py:652
  133.0 9.7 %all-to-all-done.3 = f32[4,3,16,288]{3,2,1,0:T(8,128)S(1)} async-done(((f32[4,3,16,288]{3,2,1,0:T(8,128)}), f32[4,3,16,288]{3,2,1,0:T(8,128)S(1)}, u32[]{:S(2)}, u32[]{:S(2)}) %all-to-all-start.3) | async-done | bytes 221216 | tf_op jit(solution)/shard_map/all_to_all | solution.py:652
  142.6 0.1 pad_maximum_fusion
  142.7 0.6 reshape.34
  143.3 0.1 maximum_bitcast_fusion
  143.4 0.8 reshape.35
  (8 shorter events, 0.0 us)
Async XLA Ops:
  7.2 35.7 %all-gather.3.cloned.1.call-start = ((), (), s32[]{:S(2)}) async-start(), calls=%async_computation.4 | async-start | bytes 2433024 | tf_op jit(solution)/shard_map/all_gather | solution.py:630
  20.0 18.5 %all-to-all-start = ((bf16[4,7,72,256]{3,2,1,0:T(8,128)(2,1)}), bf16[4,7,72,256]{3,2,1,0:T(8,128)(2,1)S(1)}, u32[]{:S(2)}, u32[]{:S(2)}) async-start(bf16[4,7,72,256]{3,2,1,0:T(8,128)(2,1)} %project.2), calls=%async_computation | async-start | bytes 2064384 | tf_op jit(solution)/shard_map/all_to_all | solution.py:638
  35.3 6.8 %copy-start.2 = (bf16[288]{0:T(512)(128)(2,1)S(1)}, bf16[288]{0:T(512)(128)(2,1)}, u32[]{:S(2)}) copy-start(bf16[288]{0:T(512)(128)(2,1)} %param.8) | copy-start | bytes 1732
  38.5 9.4 %copy-start.1 = (bf16[4,7,72,256]{3,2,1,0:T(8,128)(2,1)}, bf16[4,7,72,256]{3,2,1,0:T(8,128)(2,1)S(1)}, u32[]{:S(2)}) copy-start(bf16[4,7,72,256]{3,2,1,0:T(8,128)(2,1)S(1)} %all-to-all-done.moved_ref) | copy-start | bytes 3096580
  38.5 37.7 %all-to-all-start.2 = ((bf16[4,14,72,256]{3,2,1,0:T(8,128)(2,1)}), bf16[4,14,72,256]{3,2,1,0:T(8,128)(2,1)S(1)}, u32[]{:S(2)}, u32[]{:S(2)}) async-start(bf16[4,14,72,256]{3,2,1,0:T(8,128)(2,1)} %project.3), calls=%async_computation.2 | async-start | bytes 4128768 | tf_op jit(solution)/shard_map/all_to_all | solution.py:638
  76.2 5.6 %copy-start = (bf16[4,14,72,256]{3,2,1,0:T(8,128)(2,1)}, bf16[4,14,72,256]{3,2,1,0:T(8,128)(2,1)S(1)}, u32[]{:S(2)}) copy-start(bf16[4,14,72,256]{3,2,1,0:T(8,128)(2,1)S(1)} %all-to-all-done.2.moved_ref) | copy-start | bytes 6193156
  76.2 51.7 %all-to-all-start.1 = ((f32[4,3,8,288]{3,2,1,0:T(8,128)}), f32[4,3,8,288]{3,2,1,0:T(8,128)S(1)}, u32[]{:S(2)}, u32[]{:S(2)}) async-start(f32[4,3,8,288]{3,2,1,0:T(8,128)} %bitcast.19), calls=%async_computation.1 | async-start | bytes 294912 | tf_op jit(solution)/shard_map/all_to_all | solution.py:652
  127.8 14.8 %all-to-all-start.3 = ((f32[4,3,16,288]{3,2,1,0:T(8,128)}), f32[4,3,16,288]{3,2,1,0:T(8,128)S(1)}, u32[]{:S(2)}, u32[]{:S(2)}) async-start(f32[4,3,16,288]{3,2,1,0:T(8,128)} %bitcast.18), calls=%async_computation.3 | async-start | bytes 589824 | tf_op jit(solution)/shard_map/all_to_all | solution.py:652
Sparse Core Ops, SparseCore 0:
  10.2 32.3 all-gather.2

commit v12 on v11

--- a/solution.py
+++ b/solution.py
@@ -401,16 +401,16 @@
             def task():
                 if n == 0:
                     begin()
-                t = [tab[k, n : n + 16, :MAIN] for k in range(4)]
+                t = [tab[k, n : n + 8, :MAIN] for k in range(4)]
                 for b in range(block):
-                    v = source[n : n + 16, b * MAIN : (b + 1) * MAIN]
+                    v = source[n : n + 8, b * MAIN : (b + 1) * MAIN]
                     f, u = line_shapes(v, t, state["w"][b], state["c1"][b], state["c2"][b])
-                    state["total"][b] = state["total"][b] + (f[:8] + f[8:])
+                    state["total"][b] = state["total"][b] + f
                     r = step * block + b
-                    sum_ref[n : n + 16, r : r + 1] = jnp.sum(
+                    sum_ref[n : n + 8, r : r + 1] = jnp.sum(
                         u[:, :TILE] + u[:, TILE:], axis=1, keepdims=True
                     )
-                if n + 16 == modes:
+                if n + 8 == modes:
                     for b in range(block):
                         r = step * block + b
                         line = jnp.sum(state["total"][b], axis=0, keepdims=True)
@@ -418,7 +418,7 @@
 
             return task
 
-        return [rows(n) for n in range(0, modes, 16)]
+        return [rows(n) for n in range(0, modes, 8)]
 
     def contract_rest(x):
         def task():

time: 152 us -> 152 us (level)
  no operation moved by 1% of the time
where the time goes in v12:
time: 152 us; the launch traced here: 151 us
  Pallas kernels  103 us (68%)
  starting transfers between devices  18.6 us (12%)
  between operations  14.1 us (9%)
  waiting for transfers between devices  12.9 us (8%)
  local copies, waits for them, and re-layouts  2.15 us (1%)
    pallas_call x2, Pallas kernels, coupling(): pl.pallas_call(functools.partial(coupling_kernel, first, share, block), i...  73.9 us
    pallas_call x2, Pallas kernels, project(): pl.pallas_call(functools.partial(project_kernel, groups, group, share, fi...  21.3 us
    all_to_all x2, starting transfers between devices, local(): lax.all_to_all(found.reshape(n_qp, own_pairs, found.shape[1], modes), 'qp...  10.7 us
    all_to_all x2, waiting for transfers between devices, local(): lax.all_to_all(found.reshape(n_qp, own_pairs, found.shape[1], modes), 'qp...  9.68 us
    all_to_all x2, starting transfers between devices, local(): lax.all_to_all(sent, ('mode', 'fc'), split_axis=0, concat_axis=0, tiled=T...  7.83 us
    pallas_call x1, Pallas kernels, arrange(): pl.pallas_call(arrange_kernel, in_specs=[vmem], out_specs=[smem, smem, vm...  5.07 us
    all_to_all x2, waiting for transfers between devices, local(): lax.all_to_all(sent, ('mode', 'fc'), split_axis=0, concat_axis=0, tiled=T...  3.2 us
  transfers between devices with their start and end apart: 5, of which 2 were waited for; matrix products, arithmetic and copies ran while one was open for 0% of the time, Pallas kernels for 67%

profile of v12, /device:TPU:0, one launch (start us, length us, event | category | flops | bytes accessed | tf_op | source)
XLA Modules:
  0.0 150.7 jit_solution(11255037944503365154)
XLA Ops:
  7.2 0.0 all-gather.3.cloned.1.call-start
  7.2 2.5 %pack_own.1 = bf16[3,352,128]{2,1,0:T(8,128)(2,1)} custom-call(s32[1]{0:T(128)} %bitcast.part_ref, s32[3]{0:T(128)} %partner_ref.1, s32[3]{0:T(128)} %weight_ref.1, bf16[3,288,288]{2,1,0:T(8,128)(2,1)} %grid_ref.1, bf16[3,288]{1,0:T(4,128)(2,1)} %freq_ref.1), custom_call_target="tpu_custom_call" | custom-call | tf_op jit(solution)/shard_map/pack_own/pallas_call | solution.py:191
  9.7 0.0 all-gather.3.cloned.1.call-update
  9.7 10.3 %project.2 = bf16[4,7,72,256]{3,2,1,0:T(8,128)(2,1)} custom-call(s32[1]{0:T(128)} %bitcast.3.here_ref, bf16[288,288]{1,0:T(8,128)(2,1)} %home_ref.3, bf16[288,20736]{1,0:T(8,128)(2,1)} %refs_2_.3, bf16[288,20736]{1,0:T(8,128)(2,1)} %refs_2_.3, bf16[288,20736]{1,0:T(8,128)(2,1)} %refs_2_.3), custom_call_target="tpu_custom_call" | custom-call | flops 286654464 | bytes 11943936 | tf_op jit(solution)/shard_map/project/pallas_call | solution.py:111
  20.0 4.2 %all-to-all-start = ((bf16[4,7,72,256]{3,2,1,0:T(8,128)(2,1)}), bf16[4,7,72,256]{3,2,1,0:T(8,128)(2,1)S(1)}, u32[]{:S(2)}, u32[]{:S(2)}) async-start(bf16[4,7,72,256]{3,2,1,0:T(8,128)(2,1)} %project.2), calls=%async_computation | async-start | bytes 2064384 | tf_op jit(solution)/shard_map/all_to_all | solution.py:638
  24.2 11.1 %project.3 = bf16[4,14,72,256]{3,2,1,0:T(8,128)(2,1)} custom-call(s32[1]{0:T(128)} %bitcast.3.here_ref, bf16[288,288]{1,0:T(8,128)(2,1)} %home_ref.3, bf16[288,20736]{1,0:T(8,128)(2,1)} %refs_2_.3, bf16[288,20736]{1,0:T(8,128)(2,1)} %refs_2_.3, bf16[288,20736]{1,0:T(8,128)(2,1)} %refs_2_.3), custom_call_target="tpu_custom_call" | custom-call | flops 573308928 | bytes 11943936 | tf_op jit(solution)/shard_map/project/pallas_call | solution.py:111
  35.3 3.2 %all-to-all-done.moved_ref = bf16[4,7,72,256]{3,2,1,0:T(8,128)(2,1)S(1)} async-done(((bf16[4,7,72,256]{3,2,1,0:T(8,128)(2,1)}), bf16[4,7,72,256]{3,2,1,0:T(8,128)(2,1)S(1)}, u32[]{:S(2)}, u32[]{:S(2)}) %all-to-all-start) | async-done | bytes 1032224 | tf_op jit(solution)/shard_map/all_to_all | solution.py:638
  38.5 3.6 %all-to-all-start.2 = ((bf16[4,14,72,256]{3,2,1,0:T(8,128)(2,1)}), bf16[4,14,72,256]{3,2,1,0:T(8,128)(2,1)S(1)}, u32[]{:S(2)}, u32[]{:S(2)}) async-start(bf16[4,14,72,256]{3,2,1,0:T(8,128)(2,1)} %project.3), calls=%async_computation.2 | async-start | bytes 4128768 | tf_op jit(solution)/shard_map/all_to_all | solution.py:638
  42.1 0.0 copy-done.2
  42.1 0.1 reshape.37
  42.2 0.7 dynamic-slice_bitcast_fusion.home_ref
  42.8 5.1 %arrange.1 = (s32[12]{0:T(128)}, f32[12]{0:T(128)}, bf16[12,288,256]{2,1,0:T(8,128)(2,1)}, bf16[12,288,288]{2,1,0:T(8,128)(2,1)}, f32[12,1,384]{2,1,0:T(1,128)}, /*index=5*/f32[288,128]{1,0:T(8,128)}) custom-call(bf16[4,2,3,352,128]{4,3,2,1,0:T(8,128)(2,1)} %bitcast.15), custom_call_target="tpu_custom_call" | custom-call | tf_op jit(solution)/shard_map/arrange/pallas_call | solution.py:257
  47.9 0.0 copy-done.1
  47.9 28.1 %coupling.2 = f32[12,8,288]{2,1,0:T(8,128)} custom-call(s32[12]{0:T(128)} %get-tuple-element.8.partner_ref, f32[12]{0:T(128)} %get-tuple-element.9.weight_ref, f32[18]{0:T(128)} %dynamic-slice_bitcast_fusion.home_ref, bf16[12,288,256]{2,1,0:T(8,128)(2,1)} %get-tuple-element.10.grid_source, bf16[12,288,288]{2,1,0:T(8,128)(2,1)} %get-tuple-element.11.grid_t_source, ...), custom_call_target="tpu_custom_call" | custom-call | flops 6879707136 | bytes 3981312 | tf_op jit(solution)/shard_map/coupling/pallas_call | solution.py:593
  76.1 0.0 all-to-all-done.2.moved_ref
  76.1 5.6 %all-to-all-start.1 = ((f32[4,3,8,288]{3,2,1,0:T(8,128)}), f32[4,3,8,288]{3,2,1,0:T(8,128)S(1)}, u32[]{:S(2)}, u32[]{:S(2)}) async-start(f32[4,3,8,288]{3,2,1,0:T(8,128)} %bitcast.19), calls=%async_computation.1 | async-start | bytes 294912 | tf_op jit(solution)/shard_map/all_to_all | solution.py:652
  81.7 45.7 %coupling.3 = f32[12,16,288]{2,1,0:T(8,128)} custom-call(s32[12]{0:T(128)} %get-tuple-element.8.partner_ref, f32[12]{0:T(128)} %get-tuple-element.9.weight_ref, f32[18]{0:T(128)} %dynamic-slice_bitcast_fusion.home_ref, bf16[12,288,256]{2,1,0:T(8,128)(2,1)} %get-tuple-element.10.grid_source, bf16[12,288,288]{2,1,0:T(8,128)(2,1)} %get-tuple-element.11.grid_t_source, ...), custom_call_target="tpu_custom_call" | custom-call | flops 13759414272 | bytes 7962624 | tf_op jit(solution)/shard_map/coupling/pallas_call | solution.py:593
  127.5 0.0 all-to-all-done.1
  127.5 5.1 %all-to-all-start.3 = ((f32[4,3,16,288]{3,2,1,0:T(8,128)}), f32[4,3,16,288]{3,2,1,0:T(8,128)S(1)}, u32[]{:S(2)}, u32[]{:S(2)}) async-start(f32[4,3,16,288]{3,2,1,0:T(8,128)} %bitcast.18), calls=%async_computation.3 | async-start | bytes 589824 | tf_op jit(solution)/shard_map/all_to_all | solution.py:652
  132.6 9.7 %all-to-all-done.3 = f32[4,3,16,288]{3,2,1,0:T(8,128)S(1)} async-done(((f32[4,3,16,288]{3,2,1,0:T(8,128)}), f32[4,3,16,288]{3,2,1,0:T(8,128)S(1)}, u32[]{:S(2)}, u32[]{:S(2)}) %all-to-all-start.3) | async-done | bytes 221216 | tf_op jit(solution)/shard_map/all_to_all | solution.py:652
  142.3 0.1 pad_maximum_fusion
  142.4 0.6 reshape.34
  143.0 0.1 maximum_bitcast_fusion
  143.1 0.8 reshape.35
  (8 shorter events, 0.0 us)
Async XLA Ops:
  7.2 35.7 %all-gather.3.cloned.1.call-start = ((), (), s32[]{:S(2)}) async-start(), calls=%async_computation.4 | async-start | bytes 2433024 | tf_op jit(solution)/shard_map/all_gather | solution.py:630
  20.0 18.5 %all-to-all-start = ((bf16[4,7,72,256]{3,2,1,0:T(8,128)(2,1)}), bf16[4,7,72,256]{3,2,1,0:T(8,128)(2,1)S(1)}, u32[]{:S(2)}, u32[]{:S(2)}) async-start(bf16[4,7,72,256]{3,2,1,0:T(8,128)(2,1)} %project.2), calls=%async_computation | async-start | bytes 2064384 | tf_op jit(solution)/shard_map/all_to_all | solution.py:638
  35.3 6.8 %copy-start.2 = (bf16[288]{0:T(512)(128)(2,1)S(1)}, bf16[288]{0:T(512)(128)(2,1)}, u32[]{:S(2)}) copy-start(bf16[288]{0:T(512)(128)(2,1)} %param.8) | copy-start | bytes 1732
  38.5 9.4 %copy-start.1 = (bf16[4,7,72,256]{3,2,1,0:T(8,128)(2,1)}, bf16[4,7,72,256]{3,2,1,0:T(8,128)(2,1)S(1)}, u32[]{:S(2)}) copy-start(bf16[4,7,72,256]{3,2,1,0:T(8,128)(2,1)S(1)} %all-to-all-done.moved_ref) | copy-start | bytes 3096580
  38.5 37.6 %all-to-all-start.2 = ((bf16[4,14,72,256]{3,2,1,0:T(8,128)(2,1)}), bf16[4,14,72,256]{3,2,1,0:T(8,128)(2,1)S(1)}, u32[]{:S(2)}, u32[]{:S(2)}) async-start(bf16[4,14,72,256]{3,2,1,0:T(8,128)(2,1)} %project.3), calls=%async_computation.2 | async-start | bytes 4128768 | tf_op jit(solution)/shard_map/all_to_all | solution.py:638
  76.1 5.7 %copy-start = (bf16[4,14,72,256]{3,2,1,0:T(8,128)(2,1)}, bf16[4,14,72,256]{3,2,1,0:T(8,128)(2,1)S(1)}, u32[]{:S(2)}) copy-start(bf16[4,14,72,256]{3,2,1,0:T(8,128)(2,1)S(1)} %all-to-all-done.2.moved_ref) | copy-start | bytes 6193156
  76.1 51.4 %all-to-all-start.1 = ((f32[4,3,8,288]{3,2,1,0:T(8,128)}), f32[4,3,8,288]{3,2,1,0:T(8,128)S(1)}, u32[]{:S(2)}, u32[]{:S(2)}) async-start(f32[4,3,8,288]{3,2,1,0:T(8,128)} %bitcast.19), calls=%async_computation.1 | async-start | bytes 294912 | tf_op jit(solution)/shard_map/all_to_all | solution.py:652
  127.5 14.8 %all-to-all-start.3 = ((f32[4,3,16,288]{3,2,1,0:T(8,128)}), f32[4,3,16,288]{3,2,1,0:T(8,128)S(1)}, u32[]{:S(2)}, u32[]{:S(2)}) async-start(f32[4,3,16,288]{3,2,1,0:T(8,128)} %bitcast.18), calls=%async_computation.3 | async-start | bytes 589824 | tf_op jit(solution)/shard_map/all_to_all | solution.py:652
Sparse Core Ops, SparseCore 0:
  10.2 32.3 all-gather.2
